TPU v7x, 32 devices: a whole 2x2x4 slice. The times are simulated.
32 devices in a mesh: fsdp: 8 (over y, x, core), tensor: 4 (over z).
Axes of the slice: x: 2, y: 2, z: 4, core: 2. Of those that a mesh axis runs over, the one named last changes fastest.
Arguments:
- layer_input: bfloat16 [16384, 2048], P(('fsdp', 'tensor')), may hold values from -6 to 6
- query_weight: bfloat16 [2048, 2048], P('fsdp', 'tensor'), as said below
- key_weight: bfloat16 [2048, 2048], P('fsdp', 'tensor'), as said below
- value_weight: bfloat16 [2048, 2048], P('fsdp', 'tensor'), may hold values from -0.125 to 0.125
- out_weight: bfloat16 [2048, 2048], P('tensor', 'fsdp'), may hold values from -0.125 to 0.125
- gate_weight: bfloat16 [2048, 8192], P('fsdp', 'tensor'), may hold values from -0.125 to 0.125
- up_weight: bfloat16 [2048, 8192], P('fsdp', 'tensor'), may hold values from -0.125 to 0.125
- down_weight: bfloat16 [8192, 2048], P('tensor', 'fsdp'), may hold values from -0.0625 to 0.0625
- query_gain: float32 [2048], replicated, may hold values from 0.25 to 1.75
- key_gain: float32 [2048], replicated, may hold values from 0.25 to 1.75
- attn_gain: float32 [2048], replicated, may hold values from 0.25 to 1.75
- ffn_gain: float32 [2048], replicated, may hold values from 0.25 to 1.75
- out_cotangent: bfloat16 [16384, 2048], P(('fsdp', 'tensor')), may hold values from -6 to 6
Outputs:
- layer_output: bfloat16 [16384, 2048], P(('fsdp', 'tensor'))
- input_grad: float32 [16384, 2048], P(('fsdp', 'tensor'))
- query_weight_grad: float32 [2048, 2048], P('fsdp', 'tensor')
- key_weight_grad: float32 [2048, 2048], P('fsdp', 'tensor')
- value_weight_grad: float32 [2048, 2048], P('fsdp', 'tensor')
- out_weight_grad: float32 [2048, 2048], P('tensor', 'fsdp')
- gate_weight_grad: float32 [2048, 8192], P('fsdp', 'tensor')
- up_weight_grad: float32 [2048, 8192], P('fsdp', 'tensor')
- down_weight_grad: float32 [8192, 2048], P('tensor', 'fsdp')
- query_gain_grad: float32 [2048], replicated
- key_gain_grad: float32 [2048], replicated
- attn_gain_grad: float32 [2048], replicated
- ffn_gain_grad: float32 [2048], replicated
Inputs may be any that keep to these rules, and one draw needn't show every extreme that they name: `query_weight`: entries have magnitude under 17 / sqrt(2048). `key_weight`: entries have magnitude under 17 / sqrt(2048).
All inputs are finite; a program needn't handle non-finite values.
Results may differ from a plain program's by a relative error of at most 0.02.
Values may be sent and summed in bfloat16 or wider, within the bound.
A program may use at most 384 MiB of HBM per device.

v0:
```python
import math

import jax
import jax.numpy as jnp
from jax import lax
from jax.sharding import PartitionSpec as P

HEAD_DIM = 128
SEQ_LEN = 1024


EPSILON = 1e-06
THETA = 500000.0


def rotary_tables(count, head_dim):
    position = (jnp.arange(count) % SEQ_LEN).astype(jnp.float32)
    inverse = THETA ** (-jnp.arange(0, head_dim, 2).astype(jnp.float32) / head_dim)
    angles = position[:, None] * inverse[None, :]
    angles = jnp.concatenate([angles, angles], axis=-1)
    return (jnp.cos(angles), jnp.sin(angles))


def rotate(values, cos_table, sin_table):
    half_dim = values.shape[-1] // 2
    turned = jnp.concatenate([-values[..., half_dim:], values[..., :half_dim]], axis=-1)
    return values * cos_table[:, None, :] + turned * sin_table[:, None, :]


def rotate_back(grads, cos_table, sin_table):
    half_dim = grads.shape[-1] // 2
    scaled = grads * sin_table[:, None, :]
    turned = jnp.concatenate([scaled[..., half_dim:], -scaled[..., :half_dim]], axis=-1)
    return grads * cos_table[:, None, :] + turned


def block_scores(query_blk, key_seq, row_start, scale):
    scores = (
        jnp.einsum("qhd,khd->hqk", query_blk, key_seq, preferred_element_type=jnp.float32) * scale
    )
    rows_here = row_start + jnp.arange(query_blk.shape[0])
    causal = rows_here[:, None] >= jnp.arange(key_seq.shape[0])[None, :]
    return jnp.where(causal[None], scores, -1e30)


def attend_forward(query_all, key_all, value_all, seq_len, block_rows, scale):
    pieces = []
    lse_parts = []
    for seq_start in range(0, query_all.shape[0], seq_len):
        key_seq = key_all[seq_start : seq_start + seq_len]
        value_seq = value_all[seq_start : seq_start + seq_len]
        for row_start in range(0, seq_len, block_rows):
            query_blk = query_all[seq_start + row_start : seq_start + row_start + block_rows]
            scores = block_scores(query_blk, key_seq, row_start, scale)
            top_score = jnp.max(scores, axis=-1, keepdims=True)
            exps = jnp.exp(scores - top_score)
            totals = jnp.sum(exps, axis=-1, keepdims=True)
            weights = (exps / totals).astype(jnp.bfloat16)
            pieces.append(
                jnp.einsum("hqk,khd->qhd", weights, value_seq, preferred_element_type=jnp.float32)
            )
            lse_parts.append((top_score + jnp.log(totals))[..., 0])
    return (jnp.concatenate(pieces, axis=0), jnp.concatenate(lse_parts, axis=1))


def attend_backward(query_all, key_all, value_all, grad_all, lse_all, seq_len, block_rows, scale):
    query_pieces = []
    key_pieces = []
    value_pieces = []
    for seq_start in range(0, query_all.shape[0], seq_len):
        key_seq = key_all[seq_start : seq_start + seq_len]
        value_seq = value_all[seq_start : seq_start + seq_len]
        key_acc = jnp.zeros(key_seq.shape, jnp.float32)
        value_acc = jnp.zeros(value_seq.shape, jnp.float32)
        for row_start in range(0, seq_len, block_rows):
            first = seq_start + row_start
            query_blk = query_all[first : first + block_rows]
            grad_blk = grad_all[first : first + block_rows]
            lse_blk = lse_all[:, first : first + block_rows]
            scores = block_scores(query_blk, key_seq, row_start, scale)
            probs = jnp.exp(scores - lse_blk[:, :, None])
            weights = probs.astype(jnp.bfloat16)
            grad_probs = jnp.einsum(
                "qhd,khd->hqk", grad_blk, value_seq, preferred_element_type=jnp.float32
            )
            row_delta = jnp.sum(probs * grad_probs, axis=-1, keepdims=True)
            grad_scores = (probs * (grad_probs - row_delta) * scale).astype(jnp.bfloat16)
            query_pieces.append(
                jnp.einsum("hqk,khd->qhd", grad_scores, key_seq, preferred_element_type=jnp.float32)
            )
            key_acc = key_acc + jnp.einsum(
                "hqk,qhd->khd", grad_scores, query_blk, preferred_element_type=jnp.float32
            )
            value_acc = value_acc + jnp.einsum(
                "hqk,qhd->khd", weights, grad_blk, preferred_element_type=jnp.float32
            )
        key_pieces.append(key_acc)
        value_pieces.append(value_acc)
    return (
        jnp.concatenate(query_pieces, axis=0),
        jnp.concatenate(key_pieces, axis=0),
        jnp.concatenate(value_pieces, axis=0),
    )


def norm_back(grad_hat, values_hat, inverse, width):
    inner = jnp.sum(grad_hat * values_hat, axis=1, keepdims=True) / width
    return inverse * (grad_hat - values_hat * inner)


def shards(
    layer_input,
    query_weight,
    key_weight,
    value_weight,
    out_weight,
    gate_weight,
    up_weight,
    down_weight,
    query_gain,
    key_gain,
    attn_gain,
    ffn_gain,
    out_cotangent,
):
    tensor_rank = lax.axis_index("tensor")
    width = layer_input.shape[1]
    local_width = query_weight.shape[1]
    head_dim = HEAD_DIM
    local_heads = local_width // head_dim
    scale = 1.0 / math.sqrt(head_dim)
    seq_len = SEQ_LEN
    block_rows = min(512, seq_len)

    def full_weights():
        return (
            lax.all_gather(query_weight, "fsdp", axis=0, tiled=True),
            lax.all_gather(key_weight, "fsdp", axis=0, tiled=True),
            lax.all_gather(value_weight, "fsdp", axis=0, tiled=True),
            lax.all_gather(out_weight, "fsdp", axis=1, tiled=True),
            lax.all_gather(gate_weight, "fsdp", axis=0, tiled=True),
            lax.all_gather(up_weight, "fsdp", axis=0, tiled=True),
            lax.all_gather(down_weight, "fsdp", axis=1, tiled=True),
        )

    weights_fwd = full_weights()
    full_query, full_key, full_value, full_out, full_gate, full_up, full_down = weights_fwd
    rows = lax.all_gather(layer_input, "tensor", axis=0, tiled=True)
    count = rows.shape[0]
    query_pre = jnp.dot(rows, full_query, preferred_element_type=jnp.float32)
    key_pre = jnp.dot(rows, full_key, preferred_element_type=jnp.float32)
    value_low = jnp.dot(rows, full_value, preferred_element_type=jnp.float32).astype(jnp.bfloat16)
    query_sq, key_sq = lax.psum(
        (jnp.sum(query_pre * query_pre, axis=1), jnp.sum(key_pre * key_pre, axis=1)), "tensor"
    )
    query_inv = lax.rsqrt(query_sq / width + EPSILON)[:, None]
    key_inv = lax.rsqrt(key_sq / width + EPSILON)[:, None]
    query_hat = query_pre * query_inv
    key_hat = key_pre * key_inv
    query_gain_here = lax.dynamic_slice_in_dim(query_gain, tensor_rank * local_width, local_width)
    key_gain_here = lax.dynamic_slice_in_dim(key_gain, tensor_rank * local_width, local_width)
    cos_table, sin_table = rotary_tables(count, head_dim)
    head_shape = (count, local_heads, head_dim)
    query_rot = rotate(
        (query_hat * query_gain_here).reshape(head_shape), cos_table, sin_table
    ).astype(jnp.bfloat16)
    key_rot = rotate((key_hat * key_gain_here).reshape(head_shape), cos_table, sin_table).astype(
        jnp.bfloat16
    )
    value_heads = value_low.reshape(head_shape)
    attended, lse_all = attend_forward(query_rot, key_rot, value_heads, seq_len, block_rows, scale)
    attended_low = attended.reshape(count, local_width).astype(jnp.bfloat16)
    branch = lax.psum_scatter(
        jnp.dot(attended_low, full_out, preferred_element_type=jnp.float32),
        "tensor",
        scatter_dimension=0,
        tiled=True,
    )
    branch_inv = lax.rsqrt(jnp.mean(branch * branch, axis=1, keepdims=True) + EPSILON)
    branch_hat = branch * branch_inv
    middle = layer_input.astype(jnp.float32) + branch_hat * attn_gain
    mixed = lax.all_gather(middle.astype(jnp.bfloat16), "tensor", axis=0, tiled=True)
    gate = jnp.dot(mixed, full_gate, preferred_element_type=jnp.float32)
    upper = jnp.dot(mixed, full_up, preferred_element_type=jnp.float32)
    hidden = (jax.nn.silu(gate) * upper).astype(jnp.bfloat16)
    second = lax.psum_scatter(
        jnp.dot(hidden, full_down, preferred_element_type=jnp.float32),
        "tensor",
        scatter_dimension=0,
        tiled=True,
    )
    second_inv = lax.rsqrt(jnp.mean(second * second, axis=1, keepdims=True) + EPSILON)
    second_hat = second * second_inv
    output = middle + second_hat * ffn_gain
    weights_bwd = full_weights()
    back_query, back_key, back_value, back_out, back_gate, back_up, back_down = weights_bwd
    grad_out = out_cotangent.astype(jnp.float32)
    ffn_gain_part = jnp.sum(grad_out * second_hat, axis=0)
    grad_second = norm_back(grad_out * ffn_gain, second_hat, second_inv, width)
    grad_rows = lax.all_gather(grad_second.astype(jnp.bfloat16), "tensor", axis=0, tiled=True)
    grad_hidden = jnp.dot(grad_rows, back_down.T, preferred_element_type=jnp.float32)
    down_grad = jnp.dot(hidden.T, grad_rows, preferred_element_type=jnp.float32)
    sigmoid_gate = jax.nn.sigmoid(gate)
    grad_upper = (grad_hidden * gate * sigmoid_gate).astype(jnp.bfloat16)
    grad_gate = (grad_hidden * upper * sigmoid_gate * (1.0 + gate * (1.0 - sigmoid_gate))).astype(
        jnp.bfloat16
    )
    gate_grad = jnp.dot(mixed.T, grad_gate, preferred_element_type=jnp.float32)
    up_grad = jnp.dot(mixed.T, grad_upper, preferred_element_type=jnp.float32)
    mixed_part = jnp.dot(grad_gate, back_gate.T, preferred_element_type=jnp.float32) + jnp.dot(
        grad_upper, back_up.T, preferred_element_type=jnp.float32
    )
    grad_mixed = lax.psum_scatter(mixed_part, "tensor", scatter_dimension=0, tiled=True)
    gate_grad, up_grad, down_grad = (
        lax.psum_scatter(
            gate_grad.astype(jnp.bfloat16), "fsdp", scatter_dimension=0, tiled=True
        ).astype(jnp.float32),
        lax.psum_scatter(
            up_grad.astype(jnp.bfloat16), "fsdp", scatter_dimension=0, tiled=True
        ).astype(jnp.float32),
        lax.psum_scatter(
            down_grad.astype(jnp.bfloat16), "fsdp", scatter_dimension=1, tiled=True
        ).astype(jnp.float32),
    )
    grad_middle = grad_out + grad_mixed
    attn_gain_part = jnp.sum(grad_middle * branch_hat, axis=0)
    grad_branch = norm_back(grad_middle * attn_gain, branch_hat, branch_inv, width)
    grad_branch_rows = lax.all_gather(
        grad_branch.astype(jnp.bfloat16), "tensor", axis=0, tiled=True
    )
    grad_attended = jnp.dot(
        grad_branch_rows, back_out.T, preferred_element_type=jnp.float32
    ).astype(jnp.bfloat16)
    out_grad = jnp.dot(attended_low.T, grad_branch_rows, preferred_element_type=jnp.float32)
    grad_query_rot, grad_key_rot, grad_value = attend_backward(
        query_rot,
        key_rot,
        value_heads,
        grad_attended.reshape(head_shape),
        lse_all,
        seq_len,
        block_rows,
        scale,
    )
    grad_query_gained = rotate_back(grad_query_rot, cos_table, sin_table).reshape(
        count, local_width
    )
    grad_key_gained = rotate_back(grad_key_rot, cos_table, sin_table).reshape(count, local_width)
    query_gain_part = jnp.sum(grad_query_gained * query_hat, axis=0)
    key_gain_part = jnp.sum(grad_key_gained * key_hat, axis=0)
    grad_query_hat = grad_query_gained * query_gain_here
    grad_key_hat = grad_key_gained * key_gain_here
    query_inner, key_inner = lax.psum(
        (jnp.sum(grad_query_hat * query_hat, axis=1), jnp.sum(grad_key_hat * key_hat, axis=1)),
        "tensor",
    )
    grad_query = (query_inv * (grad_query_hat - query_hat * (query_inner / width)[:, None])).astype(
        jnp.bfloat16
    )
    grad_key = (key_inv * (grad_key_hat - key_hat * (key_inner / width)[:, None])).astype(
        jnp.bfloat16
    )
    grad_value_low = grad_value.reshape(count, local_width).astype(jnp.bfloat16)
    input_part = jnp.dot(grad_query, back_query.T, preferred_element_type=jnp.float32)
    input_part = input_part + jnp.dot(grad_key, back_key.T, preferred_element_type=jnp.float32)
    input_part = input_part + jnp.dot(
        grad_value_low, back_value.T, preferred_element_type=jnp.float32
    )
    grad_input_attn = lax.psum_scatter(
        input_part.astype(jnp.bfloat16), "tensor", scatter_dimension=0, tiled=True
    ).astype(jnp.float32)
    input_grad = grad_middle + grad_input_attn
    query_grad = jnp.dot(rows.T, grad_query, preferred_element_type=jnp.float32)
    key_grad = jnp.dot(rows.T, grad_key, preferred_element_type=jnp.float32)
    value_grad = jnp.dot(rows.T, grad_value_low, preferred_element_type=jnp.float32)
    query_grad, key_grad, value_grad, out_grad = (
        lax.psum_scatter(
            query_grad.astype(jnp.bfloat16), "fsdp", scatter_dimension=0, tiled=True
        ).astype(jnp.float32),
        lax.psum_scatter(
            key_grad.astype(jnp.bfloat16), "fsdp", scatter_dimension=0, tiled=True
        ).astype(jnp.float32),
        lax.psum_scatter(
            value_grad.astype(jnp.bfloat16), "fsdp", scatter_dimension=0, tiled=True
        ).astype(jnp.float32),
        lax.psum_scatter(
            out_grad.astype(jnp.bfloat16), "fsdp", scatter_dimension=1, tiled=True
        ).astype(jnp.float32),
    )
    query_full = lax.dynamic_update_slice_in_dim(
        jnp.zeros((width,), jnp.float32), query_gain_part, tensor_rank * local_width, 0
    )
    key_full = lax.dynamic_update_slice_in_dim(
        jnp.zeros((width,), jnp.float32), key_gain_part, tensor_rank * local_width, 0
    )
    query_gain_grad, key_gain_grad, attn_gain_grad, ffn_gain_grad = lax.psum(
        (query_full, key_full, attn_gain_part, ffn_gain_part), ("fsdp", "tensor")
    )
    return (
        output.astype(jnp.bfloat16),
        input_grad,
        query_grad,
        key_grad,
        value_grad,
        out_grad,
        gate_grad,
        up_grad,
        down_grad,
        query_gain_grad,
        key_gain_grad,
        attn_gain_grad,
        ffn_gain_grad,
    )


def solution(mesh):
    placed = (
        P(("fsdp", "tensor"), None),
        P("fsdp", "tensor"),
        P("fsdp", "tensor"),
        P("fsdp", "tensor"),
        P("tensor", "fsdp"),
        P("fsdp", "tensor"),
        P("fsdp", "tensor"),
        P("tensor", "fsdp"),
        P(),
        P(),
        P(),
        P(),
        P(("fsdp", "tensor"), None),
    )
    return jax.shard_map(
        shards,
        mesh=mesh,
        in_specs=placed,
        out_specs=(
            P(("fsdp", "tensor"), None),
            P(("fsdp", "tensor"), None),
            P("fsdp", "tensor"),
            P("fsdp", "tensor"),
            P("fsdp", "tensor"),
            P("tensor", "fsdp"),
            P("fsdp", "tensor"),
            P("fsdp", "tensor"),
            P("tensor", "fsdp"),
            P(),
            P(),
            P(),
            P(),
        ),
        check_vma=False,
    )
```

profile of v0, /device:TPU:0, one launch (start us, length us, event | category | flops | bytes accessed | tf_op | source)
XLA Modules:
  0.0 2558.1 jit_solution(12239897725501848239)
XLA Ops:
  18.6 21.9 all-gather.14.cloned.1.call-done
  40.5 151.2 %all-gather.12.cloned.1.call-done = bf16[2048,2048]{1,0:T(8,128)(2,1)} async-done(((bf16[512,2048]{1,0:T(8,128)(2,1)}), bf16[2048,2048]{1,0:T(8,128)(2,1)}) %all-gather.12.cloned.1.call-update) | async-done | bytes 8388624 | tf_op jit(solution)/shard_map/all_gather | solution.py:148
  230.4 19.1 all-gather.18.cloned.1.call-done
  260.3 18.7 all-reduce.2
  364.5 276.9 %reduce-scatter.12.cloned.1.call-done = f32[512,2048]{1,0:T(8,128)} async-done(((f32[2048,2048]{1,0:T(8,128)}), f32[512,2048]{1,0:T(8,128)}) %reduce-scatter.12.cloned.1.call-update) | async-done | bytes 4194320 | tf_op jit(solution)/shard_map/reduce_scatter | solution.py:173
  650.1 48.5 %all-gather.24.cloned.1.call-done = bf16[2048,2048]{1,0:T(8,128)(2,1)} async-done(((bf16[256,2048]{1,0:T(8,128)(2,1)}), bf16[2048,2048]{1,0:T(8,128)(2,1)}) %all-gather.24.cloned.1.call-update) | async-done | bytes 8388624 | tf_op jit(solution)/shard_map/all_gather | solution.py:141
  698.6 151.9 %all-gather.22.cloned.1.call-done = bf16[2048,2048]{1,0:T(8,128)(2,1)} async-done(((bf16[512,2048]{1,0:T(8,128)(2,1)}), bf16[2048,2048]{1,0:T(8,128)(2,1)}) %all-gather.22.cloned.1.call-update) | async-done | bytes 8388624 | tf_op jit(solution)/shard_map/all_gather | solution.py:182
  850.5 24.4 fusion.283
  874.9 30.3 %all-gather.26.cloned.1.call-done = bf16[2048,2048]{1,0:T(8,128)(2,1)} async-done(((bf16[256,2048]{1,0:T(8,128)(2,1)}), bf16[2048,2048]{1,0:T(8,128)(2,1)}) %all-gather.26.cloned.1.call-update) | async-done | bytes 8388624 | tf_op jit(solution)/shard_map/all_gather | solution.py:142
  905.2 28.0 %multiply_convert_fusion.2 = (bf16[2048,2048]{1,0:T(8,128)(2,1)}, f32[2048,2048]{1,0:T(8,128)}) fusion(f32[2048,2048]{1,0:T(8,128)} %fusion.283, bf16[2048,2048]{1,0:T(8,128)(2,1)} %all-gather.22.cloned.1.call-done, bf16[2048,2048]{1,0:T(8,128)(2,1)} %all-gather.26.cloned.1.call-done), kind=kOutput, calls=%fused_computation.7 | convolution fusion | flops 17205035008 | bytes 58720256 | tf_op jit(solution)/shard_map/dot_general | solution.py:184
  933.2 29.9 %all-gather.28.cloned.1.call-done = bf16[2048,2048]{1,0:T(8,128)(2,1)} async-done(((bf16[2048,256]{1,0:T(8,128)(2,1)}), bf16[2048,2048]{1,0:T(8,128)(2,1)}) %all-gather.28.cloned.1.call-update) | async-done | bytes 8388624 | tf_op jit(solution)/shard_map/all_gather | solution.py:143
  963.1 24.3 fusion.284
  987.9 279.9 %reduce-scatter.14.cloned.1.call-done = f32[512,2048]{1,0:T(8,128)} async-done(((f32[2048,2048]{1,0:T(8,128)}), f32[512,2048]{1,0:T(8,128)}) %reduce-scatter.14.cloned.1.call-update) | async-done | bytes 4194320 | tf_op jit(solution)/shard_map/reduce_scatter | solution.py:186
  1276.9 150.5 %all-gather.30.cloned.1.call-done = bf16[2048,2048]{1,0:T(8,128)(2,1)} async-done(((bf16[512,2048]{1,0:T(8,128)(2,1)}), bf16[2048,2048]{1,0:T(8,128)(2,1)}) %all-gather.30.cloned.1.call-update) | async-done | bytes 8388624 | tf_op jit(solution)/shard_map/all_gather | solution.py:200
  1427.4 34.1 %multiply_convert_fusion = (bf16[2048,2048]{1,0:T(8,128)(2,1)}, bf16[2048,2048]{1,0:T(8,128)(2,1)}) fusion(f32[2048,2048]{1,0:T(8,128)} %fusion.283, f32[2048,2048]{1,0:T(8,128)} %get-tuple-element.86, bf16[2048,2048]{1,0:T(8,128)(2,1)} %all-gather.30.cloned.1.call-done, bf16[2048,2048]{1,0:T(8,128)(2,1)} %all-gather.28.cloned.1.call-done), kind=kOutput, calls=%fused_computation.5 | convolution fusion | flops 17234395136 | bytes 67108864 | tf_op jit(solution)/shard_map/dot_general | solution.py:201
  1461.5 24.4 fusion.285
  1485.9 26.5 %convolution_add_fusion = f32[2048,2048]{1,0:T(8,128)} fusion(f32[2048,2048]{1,0:T(8,128)} %fusion.285, bf16[2048,2048]{1,0:T(8,128)(2,1)} %get-tuple-element.48, bf16[2048,2048]{1,0:T(8,128)(2,1)} %all-gather.26.cloned.1.call-done), kind=kOutput, calls=%fused_computation.9 | convolution fusion | flops 17184063488 | bytes 50331648 | tf_op jit(solution)/shard_map/dot_general | solution.py:210
  1512.5 278.6 %reduce-scatter.16.cloned.1.call-done = f32[512,2048]{1,0:T(8,128)} async-done(((f32[2048,2048]{1,0:T(8,128)}), f32[512,2048]{1,0:T(8,128)}) %reduce-scatter.16.cloned.1.call-update) | async-done | bytes 4194320 | tf_op jit(solution)/shard_map/reduce_scatter | solution.py:213
  1803.0 23.8 convolution_convert_fusion
  1826.9 24.0 convolution_convert_fusion.1
  1850.9 23.8 convolution_convert_fusion.2
  1877.4 76.0 %all-gather.32.cloned.1.call-done = bf16[2048,2048]{1,0:T(8,128)(2,1)} async-done(((bf16[512,2048]{1,0:T(8,128)(2,1)}), bf16[2048,2048]{1,0:T(8,128)(2,1)}) %all-gather.32.cloned.1.call-update) | async-done | bytes 8388624 | tf_op jit(solution)/shard_map/all_gather | solution.py:228
  1969.7 22.8 fusion.183
  1998.4 22.5 fusion.180
  2022.4 26.5 %fusion.28 = f32[4,128,1024]{1,2,0:T(8,128)} fusion(f32[4,512,1024]{2,1,0:T(8,128)} %fusion.286, f32[4,512,1024]{2,1,0:T(8,128)} %copy-done.77, f32[4,512]{1,0:T(4,128)S(1)} %log_add_fusion.3, pred[512,1024]{1,0:T(8,128)(4,1)} %copy-done.26, bf16[2048,4,128]{2,0,1:T(8,128)(2,1)} %get-tuple-element.66), kind=kOutput, calls=%fused_computation.57 | convolution fusion | flops 559942656 | bytes 37240832 | tf_op jit(solution)/shard_map/hqk,qhd->khd/dot_general | solution.py:91
  2048.9 25.4 add_bitcast_fusion.1
  2081.7 23.5 fusion.177
  2114.0 22.4 fusion.174
  2137.7 26.9 %fusion.42 = f32[4,128,1024]{1,2,0:T(8,128)} fusion(f32[4,512,1024]{2,1,0:T(8,128)} %fusion.288, f32[4,512,1024]{2,1,0:T(8,128)} %copy-done.18, f32[4,512]{1,0:T(4,128)S(1)} %log_add_fusion.1, pred[512,1024]{1,0:T(8,128)(4,1)} %copy-done.26, bf16[2048,4,128]{2,0,1:T(8,128)(2,1)} %get-tuple-element.66), kind=kOutput, calls=%fused_computation.63 | convolution fusion | flops 559942656 | bytes 37240832 | tf_op jit(solution)/shard_map/hqk,qhd->khd/dot_general | solution.py:91
  2164.6 26.6 %add_bitcast_fusion = f32[1024,4,128]{2,0,1:T(8,128)} fusion(f32[4,128,1024]{1,2,0:T(8,128)} %fusion.42, f32[4,512,1024]{2,1,0:T(8,128)} %fusion.289, f32[4,512,1024]{2,1,0:T(8,128)} %copy-done.19, f32[4,512]{1,0:T(4,128)S(1)} %log_add_fusion, pred[512,1024]{1,0:T(8,128)(4,1)} %iota_compare_fusion, bf16[2048,4,128]{2,0,1:T(8,128)(2,1)} %get-tuple-element.66), kind=kOutput, calls=%fused_computation.176 | convolution fusion | flops 560466944 | bytes 39337984 | tf_op jit(solution)/shard_map/hqk,qhd->khd/dot_general | solution.py:91
  2375.4 40.2 %all-reduce = (f32[2048]{0:T(1024)}, f32[2048]{0:T(1024)}, f32[2048]{0:T(1024)}, f32[2048]{0:T(1024)}) all-reduce(f32[2048]{0:T(1024)S(1)} %dynamic_update_slice.6, f32[2048]{0:T(1024)S(1)} %dynamic_update_slice.7, f32[2048]{0:T(1024)S(1)} %copy-done.51, f32[2048]{0:T(1024)S(1)} %copy-done.50), channel_id=1, replica_groups=mesh['fsdp'=8,'tensor'=4] {'fsdp','tensor'}, use_global_device_ids=true, to_apply=%region_36.37 | all-reduce | flops 8192 | bytes 65536 | tf_op jit(solution)/shard_map/psum | solution.py:296
  2423.0 122.1 %reduce-scatter.18.cloned.1.call-done = bf16[512,2048]{1,0:T(8,128)(2,1)} async-done(((bf16[2048,2048]{1,0:T(8,128)(2,1)}), bf16[512,2048]{1,0:T(8,128)(2,1)}) %reduce-scatter.18.cloned.1.call-update) | async-done | bytes 2097168 | tf_op jit(solution)/shard_map/reduce_scatter | solution.py:269
  (319 shorter events, 416.8 us)
Async XLA Ops:
  7.2 33.4 %all-gather.14.cloned.1.call-start = ((), (), s32[]{:S(2)}) async-start(), calls=%async_computation.12 | async-start | bytes 2359296 | tf_op jit(solution)/shard_map/all_gather | solution.py:139
  7.9 183.9 %all-gather.12.cloned.1.call-start = ((), (), s32[]{:S(2)}) async-start(), calls=%async_computation.11 | async-start | bytes 10485760 | tf_op jit(solution)/shard_map/all_gather | solution.py:148
  8.7 211.2 %all-gather.16.cloned.1.call-start = ((), (), s32[]{:S(2)}) async-start(), calls=%async_computation.13 | async-start | bytes 2359296 | tf_op jit(solution)/shard_map/all_gather | solution.py:137
  9.4 240.1 %all-gather.18.cloned.1.call-start = ((), (), s32[]{:S(2)}) async-start(), calls=%async_computation.14 | async-start | bytes 2359296 | tf_op jit(solution)/shard_map/all_gather | solution.py:138
  10.0 343.2 %all-gather.20.cloned.1.call-start = ((), (), s32[]{:S(2)}) async-start(), calls=%async_computation.15 | async-start | bytes 2359296 | tf_op jit(solution)/shard_map/all_gather | solution.py:140
  10.6 630.8 %reduce-scatter.12.cloned.1.call-start = ((), (), s32[]{:S(2)}) async-start(), calls=%async_computation.16 | async-start | bytes 20971520 | tf_op jit(solution)/shard_map/reduce_scatter | solution.py:173
  10.8 333.6 %copy-start.26 = (pred[512,1024]{1,0:T(8,128)(4,1)}, pred[512,1024]{1,0:T(8,128)(4,1)S(1)}, u32[]{:S(2)}) copy-start(pred[512,1024]{1,0:T(8,128)(4,1)S(1)} %iota_compare_fusion.1) | copy-start | bytes 1572868
  18.6 288.7 %copy-start.10 = (f32[2048,128]{1,0:T(8,128)}, f32[2048,128]{1,0:T(8,128)S(1)}, u32[]{:S(2)}) copy-start(f32[2048,128]{1,0:T(8,128)S(1)} %get-tuple-element.74) | copy-start | bytes 3145732
  363.7 280.8 %copy-start.8 = (bf16[512,2048]{1,0:T(8,128)(2,1)S(1)}, bf16[512,2048]{1,0:T(8,128)(2,1)}, u32[]{:S(2)}) copy-start(bf16[512,2048]{1,0:T(8,128)(2,1)} %param.13) | copy-start | bytes 6291460
  363.7 280.8 %copy-start.48 = (f32[2048]{0:T(1024)S(1)}, f32[2048]{0:T(1024)}, u32[]{:S(2)}) copy-start(f32[2048]{0:T(1024)} %param.23) | copy-start | bytes 24580
  363.7 334.9 %all-gather.24.cloned.1.call-start = ((), (), s32[]{:S(2)}) async-start(), calls=%async_computation.18 | async-start | bytes 9437184 | tf_op jit(solution)/shard_map/all_gather | solution.py:141
  364.4 486.0 %all-gather.22.cloned.1.call-start = ((), (), s32[]{:S(2)}) async-start(), calls=%async_computation.17 | async-start | bytes 10485760 | tf_op jit(solution)/shard_map/all_gather | solution.py:182
  648.7 256.4 %all-gather.26.cloned.1.call-start = ((), (), s32[]{:S(2)}) async-start(), calls=%async_computation.19 | async-start | bytes 9437184 | tf_op jit(solution)/shard_map/all_gather | solution.py:142
  649.5 313.6 %all-gather.28.cloned.1.call-start = ((), (), s32[]{:S(2)}) async-start(), calls=%async_computation.20 | async-start | bytes 9437184 | tf_op jit(solution)/shard_map/all_gather | solution.py:143
  650.1 617.7 %reduce-scatter.14.cloned.1.call-start = ((), (), s32[]{:S(2)}) async-start(), calls=%async_computation.21 | async-start | bytes 20971520 | tf_op jit(solution)/shard_map/reduce_scatter | solution.py:186
  987.3 283.2 %copy-start.5 = (bf16[512,2048]{1,0:T(8,128)(2,1)S(1)}, bf16[512,2048]{1,0:T(8,128)(2,1)}, u32[]{:S(2)}) copy-start(bf16[512,2048]{1,0:T(8,128)(2,1)} %param.25) | copy-start | bytes 6291460
  987.3 283.2 %copy-start.46 = (f32[2048]{0:T(1024)S(1)}, f32[2048]{0:T(1024)}, u32[]{:S(2)}) copy-start(f32[2048]{0:T(1024)} %param.24) | copy-start | bytes 24580
  987.3 440.0 %all-gather.30.cloned.1.call-start = ((), (), s32[]{:S(2)}) async-start(), calls=%async_computation.22 | async-start | bytes 10485760 | tf_op jit(solution)/shard_map/all_gather | solution.py:200
  1276.8 514.2 %reduce-scatter.16.cloned.1.call-start = ((), (), s32[]{:S(2)}) async-start(), calls=%async_computation.23 | async-start | bytes 20971520 | tf_op jit(solution)/shard_map/reduce_scatter | solution.py:213
  1512.3 278.7 %copy-start.49 = (f32[2048]{0:T(1024)S(1)}, f32[2048]{0:T(1024)}, u32[]{:S(2)}) copy-start(f32[2048]{0:T(1024)} %param.23) | copy-start | bytes 24580
  1512.3 278.7 %copy-start.67 = (f32[512]{0:T(512)S(1)}, f32[512]{0:T(512)}, u32[]{:S(2)}) copy-start(f32[512]{0:T(512)} %copy-done.66) | copy-start | bytes 6148
  1512.4 284.2 %copy-start.47 = (f32[2048]{0:T(1024)S(1)}, f32[2048]{0:T(1024)}, u32[]{:S(2)}) copy-start(f32[2048]{0:T(1024)} %param.24) | copy-start | bytes 24580
  1512.4 284.2 %copy-start.65 = (f32[512]{0:T(512)S(1)}, f32[512]{0:T(512)}, u32[]{:S(2)}) copy-start(f32[512]{0:T(512)} %copy-done.64) | copy-start | bytes 6148
  1512.4 441.1 %all-gather.32.cloned.1.call-start = ((), (), s32[]{:S(2)}) async-start(), calls=%async_computation.24 | async-start | bytes 10485760 | tf_op jit(solution)/shard_map/all_gather | solution.py:228
  1803.0 563.4 %reduce-scatter.32.cloned.1.call-start = ((), (), s32[]{:S(2)}) async-start(), calls=%async_computation.32 | async-start | bytes 9437184 | tf_op jit(solution)/shard_map/reduce_scatter | solution.py:221
  1826.8 542.5 %reduce-scatter.30.cloned.1.call-start = ((), (), s32[]{:S(2)}) async-start(), calls=%async_computation.31 | async-start | bytes 9437184 | tf_op jit(solution)/shard_map/reduce_scatter | solution.py:218
  1850.9 521.2 %reduce-scatter.28.cloned.1.call-start = ((), (), s32[]{:S(2)}) async-start(), calls=%async_computation.30 | async-start | bytes 9437184 | tf_op jit(solution)/shard_map/reduce_scatter | solution.py:215
  1874.8 540.7 %reduce-scatter.26.cloned.1.call-start = ((), (), s32[]{:S(2)}) async-start(), calls=%async_computation.29 | async-start | bytes 2359296 | tf_op jit(solution)/shard_map/reduce_scatter | solution.py:286
  2222.1 195.2 %reduce-scatter.24.cloned.1.call-start = ((), (), s32[]{:S(2)}) async-start(), calls=%async_computation.28 | async-start | bytes 2359296 | tf_op jit(solution)/shard_map/reduce_scatter | solution.py:283
  2253.6 165.6 %reduce-scatter.22.cloned.1.call-start = ((), (), s32[]{:S(2)}) async-start(), calls=%async_computation.27 | async-start | bytes 2359296 | tf_op jit(solution)/shard_map/reduce_scatter | solution.py:280
  2312.2 109.0 %reduce-scatter.20.cloned.1.call-start = ((), (), s32[]{:S(2)}) async-start(), calls=%async_computation.26 | async-start | bytes 2359296 | tf_op jit(solution)/shard_map/reduce_scatter | solution.py:277
  2327.7 217.5 %reduce-scatter.18.cloned.1.call-start = ((), (), s32[]{:S(2)}) async-start(), calls=%async_computation.25 | async-start | bytes 10485760 | tf_op jit(solution)/shard_map/reduce_scatter | solution.py:269
  (73 other events, 1647.3 us)
Sparse Core Ops, SparseCore 0:
  9.9 30.5 all-gather.13
  42.1 149.6 all-gather.11
  193.7 26.1 all-gather.15
  221.6 27.8 all-gather.17
  251.2 28.1 all-gather.19
  363.8 277.5 reduce-scatter.11
  643.4 55.1 all-gather.23
  700.8 149.6 all-gather.21
  852.5 52.6 all-gather.25
  907.1 55.9 all-gather.27
  987.5 280.2 reduce-scatter.13
  1277.0 150.3 all-gather.29
  1512.5 278.5 reduce-scatter.15
  1803.1 150.3 all-gather.31
  1957.2 69.5 reduce-scatter.31
  2030.1 71.2 reduce-scatter.29
  2105.2 71.4 reduce-scatter.27
  2222.3 39.7 reduce-scatter.25
  2265.7 41.2 reduce-scatter.23
  2312.3 40.1 reduce-scatter.21
  2356.7 41.5 reduce-scatter.19
  2400.6 144.4 reduce-scatter.17
where the time goes:
time: 2570 us; the launch traced here: 2560 us
  waiting for transfers between devices  1660 us (65%)
  matrix products  631 us (25%)
  other arithmetic  123 us (5%)
  blocking collectives  74.9 us (3%)
  local copies, waits for them, and re-layouts  51.5 us (2%)
    reduce_scatter x1, waiting for transfers between devices, shards(): lax.psum_scatter(jnp.dot(hidden, full_down, preferred_element_type=jnp.fl...  280 us
    reduce_scatter x1, waiting for transfers between devices, shards(): lax.psum_scatter(mixed_part, 'tensor', scatter_dimension=0, tiled=True)  279 us
    reduce_scatter x1, waiting for transfers between devices, shards(): lax.psum_scatter(jnp.dot(attended_low, full_out, preferred_element_type=j...  277 us
    all_gather x1, waiting for transfers between devices, shards(): lax.all_gather(middle.astype(jnp.bfloat16), 'tensor', axis=0, tiled=True)  152 us
    all_gather x1, waiting for transfers between devices, shards(): rows = lax.all_gather(layer_input, 'tensor', axis=0, tiled=True)  151 us
    all_gather x1, waiting for transfers between devices, shards(): lax.all_gather(grad_second.astype(jnp.bfloat16), 'tensor', axis=0, tiled=...  150 us
    reduce_scatter x1, waiting for transfers between devices, shards(): lax.psum_scatter(input_part.astype(jnp.bfloat16), 'tensor', scatter_dimen...  122 us
    dot_general x4, matrix products, attend_backward(): jnp.einsum('hqk,qhd->khd', grad_scores, query_blk, preferred_element_type...  105 us
  transfers between devices with their start and end apart: 22, of which 14 were waited for; matrix products, arithmetic and copies ran while one was open for 26% of the time, Pallas kernels for 0%

commit v1 on v0

v1 whole, which is shorter than its diff:
```python
import functools
import math

import jax
import jax.numpy as jnp
from jax import lax
from jax.experimental import pallas as pl
from jax.experimental.pallas import tpu as pltpu
from jax.sharding import PartitionSpec as P

HEAD_DIM = 128
SEQ_LEN = 1024
EPSILON = 1e-06
THETA = 500000.0
BLOCK = 256
LOW = jnp.bfloat16
F32 = jnp.float32


def nn(a, b):
    return lax.dot_general(a, b, (((1,), (0,)), ((), ())), preferred_element_type=F32)


def nt(a, b):
    return lax.dot_general(a, b, (((1,), (1,)), ((), ())), preferred_element_type=F32)


def tn(a, b):
    return lax.dot_general(a, b, (((0,), (0,)), ((), ())), preferred_element_type=F32)


def block_start(place, block, rows, parts):
    part = block * BLOCK // rows
    return pl.multiple_of(
        lax.rem(place + parts - part, parts) * rows + block * BLOCK % rows, BLOCK
    )


def masked(scores):
    row = lax.broadcasted_iota(jnp.int32, scores.shape, 0)
    col = lax.broadcasted_iota(jnp.int32, scores.shape, 1)
    return jnp.where(row + (scores.shape[1] - scores.shape[0]) >= col, scores, -1e30)


def attend_kernel(
    rows,
    parts,
    scale,
    place_ref,
    query_ref,
    key_ref,
    value_ref,
    query_inv_ref,
    key_inv_ref,
    query_gain_ref,
    key_gain_ref,
    cos_ref,
    sin_ref,
    out_ref,
    query_rot_ref,
    key_rot_ref,
    lse_ref,
    key_seq,
    value_seq,
):
    place = place_ref[0]
    half = HEAD_DIM // 2
    for block in range(SEQ_LEN // BLOCK):
        here = pl.ds(block_start(place, block, rows, parts), BLOCK)
        there = pl.ds(block * BLOCK, BLOCK)
        cos, sin = cos_ref[here], sin_ref[here]
        key = key_ref[here] * key_inv_ref[here] * key_gain_ref[...]
        key = (key * cos + pltpu.roll(key, half, 1) * sin).astype(LOW)
        key_rot_ref[here] = key
        key_seq[there] = key
        value_seq[there] = value_ref[here]
        query = query_ref[here] * query_inv_ref[here] * query_gain_ref[...]
        query = (query * cos + pltpu.roll(query, half, 1) * sin).astype(LOW)
        query_rot_ref[here] = query
        span = (block + 1) * BLOCK
        scores = masked(nt(query, key_seq[:span]) * scale)
        top = jnp.max(scores, axis=1, keepdims=True)
        exps = jnp.exp(scores - top)
        total = jnp.sum(exps, axis=1, keepdims=True)
        weights = (exps * (1.0 / total)).astype(LOW)
        out_ref[here] = nn(weights, value_seq[:span]).astype(LOW)
        lse_ref[here] = top + jnp.log(total)


def attend_back_kernel(
    rows,
    parts,
    scale,
    place_ref,
    query_rot_ref,
    key_rot_ref,
    value_ref,
    grad_ref,
    lse_ref,
    query_ref,
    key_ref,
    query_inv_ref,
    key_inv_ref,
    query_gain_ref,
    key_gain_ref,
    cos_ref,
    sin_ref,
    query_out_ref,
    key_out_ref,
    value_out_ref,
    query_gain_out_ref,
    key_gain_out_ref,
    query_inner_ref,
    key_inner_ref,
    key_seq,
    value_seq,
    key_acc,
    value_acc,
):
    place = place_ref[0]
    half = HEAD_DIM // 2
    count = SEQ_LEN // BLOCK

    @pl.when(pl.program_id(0) == 0)
    def _():
        query_inner_ref[...] = jnp.zeros_like(query_inner_ref)
        key_inner_ref[...] = jnp.zeros_like(key_inner_ref)

    def finish(grad, here, values_ref, inv_ref, gain_ref, out_ref, inner_ref):
        back = grad * cos_ref[here] - pltpu.roll(grad, half, 1) * sin_ref[here]
        hat = values_ref[here] * inv_ref[here]
        gained = back * gain_ref[...]
        out_ref[here] = gained
        inner_ref[here] += jnp.sum(gained * hat, axis=1, keepdims=True)
        return jnp.sum(back * hat, axis=0, keepdims=True)

    query_gain_sum = jnp.zeros((1, HEAD_DIM), F32)
    for block in range(count):
        here = pl.ds(block_start(place, block, rows, parts), BLOCK)
        there = pl.ds(block * BLOCK, BLOCK)
        key_seq[there] = key_rot_ref[here]
        value_seq[there] = value_ref[here]
        query, grad = query_rot_ref[here], grad_ref[here]
        span = (block + 1) * BLOCK
        scores = masked(nt(query, key_seq[:span]) * scale)
        probs = jnp.exp(scores - lse_ref[here])
        weights = probs.astype(LOW)
        grad_probs = nt(grad, value_seq[:span])
        delta = jnp.sum(probs * grad_probs, axis=1, keepdims=True)
        grad_scores = (probs * (grad_probs - delta) * scale).astype(LOW)
        value_part = tn(weights, grad)
        key_part = tn(grad_scores, query)
        past = block * BLOCK
        if block:
            key_acc[:past] += key_part[:past]
            value_acc[:past] += value_part[:past]
        key_acc[past:span] = key_part[past:]
        value_acc[past:span] = value_part[past:]
        query_gain_sum += finish(
            nn(grad_scores, key_seq[:span]),
            here,
            query_ref,
            query_inv_ref,
            query_gain_ref,
            query_out_ref,
            query_inner_ref,
        )
    query_gain_out_ref[...] = query_gain_sum
    key_gain_sum = jnp.zeros((1, HEAD_DIM), F32)
    for block in range(count):
        here = pl.ds(block_start(place, block, rows, parts), BLOCK)
        there = pl.ds(block * BLOCK, BLOCK)
        value_out_ref[here] = value_acc[there].astype(LOW)
        key_gain_sum += finish(
            key_acc[there],
            here,
            key_ref,
            key_inv_ref,
            key_gain_ref,
            key_out_ref,
            key_inner_ref,
        )
    key_gain_out_ref[...] = key_gain_sum


def attention_specs(width):
    head = pl.BlockSpec((SEQ_LEN, HEAD_DIM), lambda i, place: (0, i))
    whole = pl.BlockSpec((SEQ_LEN, HEAD_DIM), lambda i, place: (0, 0))
    column = pl.BlockSpec((SEQ_LEN, 1), lambda i, place: (0, 0))
    gain = pl.BlockSpec((1, HEAD_DIM), lambda i, place: (0, i))
    lse = pl.BlockSpec((None, SEQ_LEN, 1), lambda i, place: (i, 0, 0))
    return head, whole, column, gain, lse


def attend(rows, parts, place, query, key, value, invs, gains, tables):
    width = query.shape[1]
    heads = width // HEAD_DIM
    head, whole, column, gain, lse = attention_specs(width)
    low = jax.ShapeDtypeStruct((SEQ_LEN, width), LOW)
    return pl.pallas_call(
        functools.partial(attend_kernel, rows, parts, 1.0 / math.sqrt(HEAD_DIM)),
        grid_spec=pltpu.PrefetchScalarGridSpec(
            num_scalar_prefetch=1,
            grid=(heads,),
            in_specs=[head, head, head, column, column, gain, gain, whole, whole],
            out_specs=[head, head, head, lse],
            scratch_shapes=[
                pltpu.VMEM((SEQ_LEN, HEAD_DIM), LOW),
                pltpu.VMEM((SEQ_LEN, HEAD_DIM), LOW),
            ],
        ),
        out_shape=[low, low, low, jax.ShapeDtypeStruct((heads, SEQ_LEN, 1), F32)],
        compiler_params=pltpu.CompilerParams(vmem_limit_bytes=40 * 2**20),
        cost_estimate=pl.CostEstimate(
            flops=8 * heads * SEQ_LEN * SEQ_LEN * HEAD_DIM,
            bytes_accessed=16 * SEQ_LEN * width,
            transcendentals=heads * SEQ_LEN * SEQ_LEN,
        ),
        name="attend",
    )(place, query, key, value, *invs, *gains, *tables)


def attend_back(rows, parts, place, rots, value, grad, lse_all, pres, invs, gains, tables):
    width = value.shape[1]
    heads = width // HEAD_DIM
    head, whole, column, gain, lse = attention_specs(width)
    full = jax.ShapeDtypeStruct((SEQ_LEN, width), F32)
    gain_out = jax.ShapeDtypeStruct((1, width), F32)
    inner = jax.ShapeDtypeStruct((SEQ_LEN, 1), F32)
    return pl.pallas_call(
        functools.partial(attend_back_kernel, rows, parts, 1.0 / math.sqrt(HEAD_DIM)),
        grid_spec=pltpu.PrefetchScalarGridSpec(
            num_scalar_prefetch=1,
            grid=(heads,),
            in_specs=[head, head, head, head, lse, head, head]
            + [column, column, gain, gain, whole, whole],
            out_specs=[head, head, head, gain, gain, column, column],
            scratch_shapes=[
                pltpu.VMEM((SEQ_LEN, HEAD_DIM), LOW),
                pltpu.VMEM((SEQ_LEN, HEAD_DIM), LOW),
                pltpu.VMEM((SEQ_LEN, HEAD_DIM), F32),
                pltpu.VMEM((SEQ_LEN, HEAD_DIM), F32),
            ],
        ),
        out_shape=[
            full,
            full,
            jax.ShapeDtypeStruct((SEQ_LEN, width), LOW),
            gain_out,
            gain_out,
            inner,
            inner,
        ],
        compiler_params=pltpu.CompilerParams(vmem_limit_bytes=48 * 2**20),
        cost_estimate=pl.CostEstimate(
            flops=20 * heads * SEQ_LEN * SEQ_LEN * HEAD_DIM,
            bytes_accessed=32 * SEQ_LEN * width,
            transcendentals=heads * SEQ_LEN * SEQ_LEN,
        ),
        name="attend_back",
    )(place, *rots, value, grad, lse_all, *pres, *invs, *gains, *tables)


def norm_back(grad_hat, values_hat, inverse, width):
    inner = jnp.sum(grad_hat * values_hat, axis=1, keepdims=True) / width
    return inverse * (grad_hat - values_hat * inner)


def layer(fsdp, tensor, *arguments):
    layer_input, query_weight, key_weight, value_weight, out_weight = arguments[:5]
    gate_weight, up_weight, down_weight = arguments[5:8]
    query_gain, key_gain, attn_gain, ffn_gain, out_cotangent = arguments[8:]
    rows_here, width = layer_input.shape
    head_cols = query_weight.shape[1]
    parts = SEQ_LEN // rows_here
    spans = tensor // parts
    fsdp_rank = lax.axis_index("fsdp")
    rank = lax.axis_index("tensor")
    place, span = rank % parts, rank // parts
    core = fsdp_rank % 2

    def to_part(x, shift):
        pairs = [
            (s * parts + p, s * parts + (p + shift) % parts)
            for s in range(spans)
            for p in range(parts)
        ]
        return lax.ppermute(x, "tensor", pairs)

    def to_span(x, shift):
        pairs = [
            (s * parts + p, (s + shift) % spans * parts + p)
            for s in range(spans)
            for p in range(parts)
        ]
        return lax.ppermute(x, "tensor", pairs)

    def to_other_core(x):
        return lax.ppermute(x, "fsdp", [(f, f ^ 1) for f in range(fsdp)])

    def gather_weight(shard):
        wide = [shard] + [to_span(shard, s) for s in range(1, spans)]
        return lax.all_gather(jnp.concatenate(wide, axis=1), "fsdp", axis=0, tiled=True)

    def gather_rows(own):
        return jnp.concatenate([own] + [to_part(own, p) for p in range(1, parts)], axis=0)

    def scatter_rows(make):
        away = [
            to_part(make(slice(p * rows_here, (p + 1) * rows_here)).astype(LOW), -p)
            for p in range(1, parts)
        ]
        total = make(slice(0, rows_here))
        for piece in away:
            total = total + piece.astype(F32)
        return total

    def sum_parts(x):
        total = x
        for p in range(1, parts):
            total = total + jnp.roll(to_part(x, p), p * rows_here, axis=1)
        return total

    def core_halves(x):
        split = x.reshape(x.shape[0], fsdp // 2, 2, width // fsdp)
        return [
            lax.dynamic_index_in_dim(split, which, 2, keepdims=False).reshape(
                x.shape[0], width // 2
            )
            for which in (core, 1 - core)
        ]

    same_core = [list(range(c, fsdp, 2)) for c in range(2)]

    def weight_grad(halves, grads):
        mine, other = halves
        sent = to_other_core(tn(other, grads).astype(LOW))
        total = (tn(mine, grads) + sent.astype(F32)).astype(LOW)
        total = lax.psum_scatter(
            total, "fsdp", scatter_dimension=0, tiled=True, axis_index_groups=same_core
        )
        cols = total.shape[1] // spans
        result = total[:, :cols].astype(F32)
        for s in range(1, spans):
            result = result + to_span(total[:, s * cols : (s + 1) * cols], -s).astype(F32)
        return result

    def own_columns(s):
        return ((span + spans - s) % spans * parts + place) * head_cols

    def gain_here(gain):
        return jnp.concatenate(
            [lax.dynamic_slice_in_dim(gain, own_columns(s), head_cols) for s in range(spans)]
        )[None, :]

    def gain_whole(part):
        whole = jnp.zeros((width,), F32)
        for s in range(spans):
            whole = lax.dynamic_update_slice_in_dim(
                whole, part[0, s * head_cols : (s + 1) * head_cols], own_columns(s), 0
            )
        return whole

    inputs = gather_rows(layer_input)
    full_query = gather_weight(query_weight)
    full_key = gather_weight(key_weight)
    full_value = gather_weight(value_weight)
    full_out = gather_weight(out_weight.T)
    full_gate = gather_weight(gate_weight)
    full_up = gather_weight(up_weight)
    full_down = gather_weight(down_weight.T)

    local = jnp.arange(SEQ_LEN)
    position = (place + parts - local // rows_here) % parts * rows_here + local % rows_here
    inverse = THETA ** (-jnp.arange(0, HEAD_DIM, 2).astype(F32) / HEAD_DIM)
    angles = position.astype(F32)[:, None] * inverse[None, :]
    cos, sin = jnp.cos(angles), jnp.sin(angles)
    tables = (jnp.concatenate([cos, cos], axis=1), jnp.concatenate([-sin, sin], axis=1))
    gains = (gain_here(query_gain), gain_here(key_gain))
    place_arr = jnp.full((1,), place, jnp.int32)

    query_pre = nn(inputs, full_query)
    key_pre = nn(inputs, full_key)
    value_low = nn(inputs, full_value).astype(LOW)
    squares = jnp.stack(
        [jnp.sum(query_pre * query_pre, axis=1), jnp.sum(key_pre * key_pre, axis=1)]
    )
    invs = lax.rsqrt(sum_parts(squares) / width + EPSILON)
    invs = (invs[0][:, None], invs[1][:, None])
    attended, query_rot, key_rot, lse = attend(
        rows_here, parts, place_arr, query_pre, key_pre, value_low, invs, gains, tables
    )
    branch = scatter_rows(lambda part: nt(attended[part], full_out))
    branch_inv = lax.rsqrt(jnp.mean(branch * branch, axis=1, keepdims=True) + EPSILON)
    branch_hat = branch * branch_inv
    middle = layer_input.astype(F32) + branch_hat * attn_gain
    mixed = gather_rows(middle.astype(LOW))
    gate = nn(mixed, full_gate)
    upper = nn(mixed, full_up)
    hidden = (jax.nn.silu(gate) * upper).astype(LOW)
    second = scatter_rows(lambda part: nt(hidden[part], full_down))
    second_inv = lax.rsqrt(jnp.mean(second * second, axis=1, keepdims=True) + EPSILON)
    second_hat = second * second_inv
    output = (middle + second_hat * ffn_gain).astype(LOW)

    grad_out = out_cotangent.astype(F32)
    ffn_gain_part = jnp.sum(grad_out * second_hat, axis=0)
    grad_second = norm_back(grad_out * ffn_gain, second_hat, second_inv, width)
    grad_rows = gather_rows(grad_second.astype(LOW))
    grad_hidden = nn(grad_rows, full_down)
    down_grad = weight_grad(core_halves(grad_rows), hidden).T
    sigmoid = jax.nn.sigmoid(gate)
    grad_upper = (grad_hidden * gate * sigmoid).astype(LOW)
    grad_gate = (grad_hidden * upper * sigmoid * (1.0 + gate * (1.0 - sigmoid))).astype(LOW)
    mixed_halves = core_halves(mixed)
    gate_grad = weight_grad(mixed_halves, grad_gate)
    up_grad = weight_grad(mixed_halves, grad_upper)
    grad_mixed = scatter_rows(
        lambda part: nt(grad_gate[part], full_gate) + nt(grad_upper[part], full_up)
    )
    grad_middle = grad_out + grad_mixed
    attn_gain_part = jnp.sum(grad_middle * branch_hat, axis=0)
    grad_branch = norm_back(grad_middle * attn_gain, branch_hat, branch_inv, width)
    grad_branch_rows = gather_rows(grad_branch.astype(LOW))
    grad_attended = nn(grad_branch_rows, full_out).astype(LOW)
    out_grad = weight_grad(core_halves(grad_branch_rows), attended).T
    (
        query_gained,
        key_gained,
        grad_value,
        query_gain_part,
        key_gain_part,
        query_inner,
        key_inner,
    ) = attend_back(
        rows_here,
        parts,
        place_arr,
        (query_rot, key_rot),
        value_low,
        grad_attended,
        lse,
        (query_pre, key_pre),
        invs,
        gains,
        tables,
    )
    inners = sum_parts(jnp.concatenate([query_inner, key_inner], axis=1).T).T / width
    grad_query = (
        invs[0] * (query_gained - query_pre * invs[0] * inners[:, :1])
    ).astype(LOW)
    grad_key = (invs[1] * (key_gained - key_pre * invs[1] * inners[:, 1:])).astype(LOW)
    input_grad = grad_middle + scatter_rows(
        lambda part: nt(grad_query[part], full_query)
        + nt(grad_key[part], full_key)
        + nt(grad_value[part], full_value)
    )
    input_halves = core_halves(inputs)
    value_grad = weight_grad(input_halves, grad_value)
    query_grad = weight_grad(input_halves, grad_query)
    key_grad = weight_grad(input_halves, grad_key)
    gain_grads = lax.psum(
        (gain_whole(query_gain_part), gain_whole(key_gain_part), attn_gain_part, ffn_gain_part),
        ("fsdp", "tensor"),
    )
    return (
        output,
        input_grad,
        query_grad,
        key_grad,
        value_grad,
        out_grad,
        gate_grad,
        up_grad,
        down_grad,
        *gain_grads,
    )


def solution(mesh):
    columns, rows = P("fsdp", "tensor"), P("tensor", "fsdp")
    tokens = P(("fsdp", "tensor"), None)
    weights = (columns, columns, columns, rows, columns, columns, rows)
    return jax.shard_map(
        functools.partial(layer, mesh.shape["fsdp"], mesh.shape["tensor"]),
        mesh=mesh,
        in_specs=(tokens, *weights, P(), P(), P(), P(), tokens),
        out_specs=(tokens, tokens, *weights, P(), P(), P(), P()),
        check_vma=False,
    )
```

time: 2570 us -> 1410 us (0.55)
  waiting for transfers between devices: 1660 us -> 611 us
  matrix products: 631 us -> 363 us
  local copies, waits for them, and re-layouts: 51.5 us -> 165 us
  Pallas kernels: 0 us -> 70.3 us
  other arithmetic: 123 us -> 73.6 us
    reduce_scatter x11 -> x7, waiting for transfers between devices: 958 us -> 0.01 us  [weight_grad(): lax.psum_scatter(total, 'fsdp', scatter_dimension=0, tiled=True, axis_ind...]
    all_gather x11 -> x7, waiting for transfers between devices: 697 us -> 0.03 us  [gather_weight(): lax.all_gather(jnp.concatenate(wide, axis=1), 'fsdp', axis=0, tiled=True)]
    ppermute x0 -> x31, waiting for transfers between devices: none -> 611 us  [the longest x14 338 us: to_span(): return lax.ppermute(x, 'tensor', pairs)]
    dot_general x45 -> x35, matrix products: 631 us -> 363 us  [the longest x14 124 us: nt(): lax.dot_general(a, b, (((1,), (1,)), ((), ())), preferred_element_type=F32)]
    pallas_call x0 -> x2, Pallas kernels: none -> 70.3 us  [the longest x1 41.4 us: attend_back(): pl.pallas_call(functools.partial(attend_back_kernel, rows, parts, 1.0 / m...]
    unnamed x170 -> x147, local copies, waits for them, and re-layouts: 13.5 us -> 82.1 us
    dynamic_slice x2 -> x5, local copies, waits for them, and re-layouts: 1.57 us -> 36.6 us  [the longest x4 36.5 us: core_halves(): lax.dynamic_index_in_dim(split, which, 2, keepdims=False)]
    reduce_sum x7 -> x1, other arithmetic: 33.5 us -> 1.93 us  [layer(): ffn_gain_part = jnp.sum(grad_out * second_hat, axis=0)]
  transfers between devices with their start and end apart: 22 -> 45, of which waited for: 14 -> 23; matrix products, arithmetic and copies ran while one was open for 26% -> 30% of each run, Pallas kernels for 0% -> 5%
where the time goes in v1:
time: 1410 us; the launch traced here: 1390 us
  waiting for transfers between devices  611 us (43%)
  matrix products  363 us (26%)
  local copies, waits for them, and re-layouts  165 us (12%)
  other arithmetic  73.6 us (5%)
  blocking collectives  71 us (5%)
  Pallas kernels  70.3 us (5%)
  starting transfers between devices  24.1 us (2%)
  between operations  15 us (1%)
    ppermute x14, waiting for transfers between devices, to_span(): return lax.ppermute(x, 'tensor', pairs)  338 us
    ppermute x10, waiting for transfers between devices, to_part(): return lax.ppermute(x, 'tensor', pairs)  250 us
    dot_general x14, matrix products, nt(): lax.dot_general(a, b, (((1,), (1,)), ((), ())), preferred_element_type=F32)  124 us
    dot_general x7, matrix products, nn(): lax.dot_general(a, b, (((1,), (0,)), ((), ())), preferred_element_type=F32)  121 us
    dot_general x14, matrix products, tn(): lax.dot_general(a, b, (((0,), (0,)), ((), ())), preferred_element_type=F32)  117 us
    unnamed x147, local copies, waits for them, and re-layouts  82.1 us
    psum x1, blocking collectives, layer(): lax.psum((gain_whole(query_gain_part), gain_whole(key_gain_part), attn_ga...  71 us
    pallas_call x1, Pallas kernels, attend_back(): pl.pallas_call(functools.partial(attend_back_kernel, rows, parts, 1.0 / m...  41.4 us
  transfers between devices with their start and end apart: 45, of which 23 were waited for; matrix products, arithmetic and copies ran while one was open for 30% of the time, Pallas kernels for 5%

profile of v1, /device:TPU:0, one launch (start us, length us, event | category | flops | bytes accessed | tf_op | source)
XLA Modules:
  0.0 1392.6 jit_solution(1549730100618419721)
XLA Ops:
  25.4 14.2 %collective-permute-done.1 = bf16[256,512]{1,0:T(8,128)(2,1)S(1)} collective-permute-done((bf16[256,512]{1,0:T(8,128)(2,1)}, bf16[256,512]{1,0:T(8,128)(2,1)S(1)}, u32[]{:S(2)}, u32[]{:S(2)}) %collective-permute-start.1) | collective-permute-done | bytes 262176 | tf_op jit(solution)/shard_map/ppermute | solution.py:296
  41.6 13.3 collective-permute-done.3
  56.9 13.3 collective-permute-done.5
  71.2 48.2 %collective-permute-done.8 = bf16[256,2048]{1,0:T(8,128)(2,1)S(1)} collective-permute-done((bf16[256,2048]{1,0:T(8,128)(2,1)S(1)}, bf16[256,2048]{1,0:T(8,128)(2,1)S(1)}, u32[]{:S(2)}, u32[]{:S(2)}) %collective-permute-start.8) | collective-permute-done | bytes 1048608 | tf_op jit(solution)/shard_map/ppermute | solution.py:296
  121.1 47.2 %collective-permute-done.9 = bf16[256,2048]{1,0:T(8,128)(2,1)S(1)} collective-permute-done((bf16[256,2048]{1,0:T(8,128)(2,1)S(1)}, bf16[256,2048]{1,0:T(8,128)(2,1)S(1)}, u32[]{:S(2)}, u32[]{:S(2)}) %collective-permute-start.9) | collective-permute-done | bytes 1048608 | tf_op jit(solution)/shard_map/ppermute | solution.py:296
  170.0 48.2 %collective-permute-done.10 = bf16[256,2048]{0,1:T(8,128)(2,1)S(1)} collective-permute-done((bf16[256,2048]{0,1:T(8,128)(2,1)S(1)}, bf16[256,2048]{0,1:T(8,128)(2,1)S(1)}, u32[]{:S(2)}, u32[]{:S(2)}) %collective-permute-start.10) | collective-permute-done | bytes 1048608 | tf_op jit(solution)/shard_map/ppermute | solution.py:296
  224.7 45.4 %collective-permute-done = bf16[512,2048]{0,1:T(8,128)(2,1)} collective-permute-done((bf16[512,2048]{0,1:T(8,128)(2,1)}, bf16[512,2048]{0,1:T(8,128)(2,1)}, u32[]{:S(2)}, u32[]{:S(2)}) %collective-permute-start) | collective-permute-done | bytes 2097184 | tf_op jit(solution)/shard_map/ppermute | solution.py:288
  312.3 28.9 %attend.1 = (bf16[1024,1024]{1,0:T(8,128)(2,1)S(1)}, bf16[1024,1024]{1,0:T(8,128)(2,1)S(1)}, bf16[1024,1024]{1,0:T(8,128)(2,1)S(1)}, f32[8,1024,1]{2,1,0:T(8,128)}) custom-call(s32[1]{0:T(128)} %bitcast.place_ref, f32[1024,1024]{1,0:T(8,128)} %copy.88.query_ref, f32[1024,1024]{1,0:T(8,128)} %copy.89.key_ref, bf16[1024,1024]{1,0:T(8,128)(2,1)S(1)} %copy-done.8, ...), custom_call_target="tpu_custom_call" | custom-call | flops 8589934592 | bytes 16777216 | tf_op jit(solution)/shard_map/attend/pallas_call | solution.py:200
  352.3 44.4 %collective-permute-done.6 = bf16[512,2048]{1,0:T(8,128)(2,1)S(1)} collective-permute-done((bf16[512,2048]{1,0:T(8,128)(2,1)S(1)}, bf16[512,2048]{1,0:T(8,128)(2,1)S(1)}, u32[]{:S(2)}, u32[]{:S(2)}) %collective-permute-start.6) | collective-permute-done | bytes 2097184 | tf_op jit(solution)/shard_map/ppermute | solution.py:288
  402.8 44.1 %collective-permute-done.7 = bf16[512,2048]{1,0:T(8,128)(2,1)} collective-permute-done((bf16[512,2048]{1,0:T(8,128)(2,1)S(1)}, bf16[512,2048]{1,0:T(8,128)(2,1)}, u32[]{:S(2)}, u32[]{:S(2)}) %collective-permute-start.7) | collective-permute-done | bytes 2097184 | tf_op jit(solution)/shard_map/ppermute | solution.py:288
  446.9 23.6 %fusion.64 = f32[1024,4096]{1,0:T(8,128)} fusion(bf16[2048,4096]{1,0:T(8,128)(2,1)} %all-gather.16.cloned.1.call-done, bf16[512,2048]{1,0:T(8,128)(2,1)} %collective-permute-done.7, bf16[512,2048]{1,0:T(8,128)(2,1)} %copy-done.19), kind=kOutput, calls=%fused_computation.144 | convolution fusion | flops 17188257792 | bytes 37748736 | tf_op jit(solution)/shard_map/dot_general | solution.py:21
  470.5 30.4 %multiply_convert_fusion.2 = (bf16[1024,4096]{1,0:T(8,128)(2,1)}, f32[1024,4096]{1,0:T(8,128)}) fusion(f32[1024,4096]{1,0:T(8,128)} %fusion.64, bf16[2048,4096]{1,0:T(8,128)(2,1)} %all-gather.18.cloned.1.call-done, bf16[512,2048]{1,0:T(8,128)(2,1)} %collective-permute-done.7, bf16[512,2048]{1,0:T(8,128)(2,1)} %copy-done.19), kind=kOutput, calls=%fused_computation.5 | convolution fusion | flops 17213423616 | bytes 62914560 | tf_op jit(solution)/shard_map/dot_general | solution.py:21
  500.9 13.8 fusion.24
  515.9 43.5 %collective-permute-done.11 = bf16[512,2048]{1,0:T(8,128)(2,1)S(1)} collective-permute-done((bf16[512,2048]{1,0:T(8,128)(2,1)S(1)}, bf16[512,2048]{1,0:T(8,128)(2,1)S(1)}, u32[]{:S(2)}, u32[]{:S(2)}) %collective-permute-start.11) | collective-permute-done | bytes 2097184 | tf_op jit(solution)/shard_map/ppermute | solution.py:288
  575.8 42.4 %collective-permute-done.12 = bf16[512,2048]{1,0:T(8,128)(2,1)S(1)} collective-permute-done((bf16[512,2048]{1,0:T(8,128)(2,1)S(1)}, bf16[512,2048]{1,0:T(8,128)(2,1)S(1)}, u32[]{:S(2)}, u32[]{:S(2)}) %collective-permute-start.12) | collective-permute-done | bytes 2097184 | tf_op jit(solution)/shard_map/ppermute | solution.py:288
  619.5 31.0 %multiply_convert_fusion.1 = (bf16[1024,4096]{1,0:T(8,128)(2,1)}, bf16[1024,4096]{1,0:T(8,128)(2,1)}) fusion(f32[1024,4096]{1,0:T(8,128)} %fusion.64, f32[1024,4096]{1,0:T(8,128)} %get-tuple-element.148, bf16[2048,4096]{0,1:T(8,128)(2,1)} %all-gather.20.cloned.1.call-done, bf16[512,2048]{1,0:T(8,128)(2,1)} %copy-done.37, bf16[512,2048]{1,0:T(8,128)(2,1)} %copy-done.16), kind=kOutput, calls=%fused_computation.4 | convolution fusion | flops 17242783744 | bytes 71303168 | tf_op jit(solution)/shard_map/dot_general | solution.py:21
  650.5 15.3 %fusion.6 = f32[512,2048]{1,0:T(8,128)} fusion(bf16[2048,4096]{1,0:T(8,128)(2,1)} %all-gather.18.cloned.1.call-done, bf16[1024,4096]{1,0:T(8,128)(2,1)} %get-tuple-element.109), kind=kOutput, calls=%fused_computation.19 | convolution fusion | flops 8589934592 | bytes 25165824 | tf_op jit(solution)/shard_map/dot_general | solution.py:25
  665.9 14.3 %add_convert_fusion.8 = bf16[512,2048]{1,0:T(8,128)(2,1)S(1)} fusion(f32[512,2048]{1,0:T(8,128)} %fusion.6, bf16[2048,4096]{1,0:T(8,128)(2,1)} %all-gather.16.cloned.1.call-done, bf16[1024,4096]{1,0:T(8,128)(2,1)} %get-tuple-element.108), kind=kOutput, calls=%fused_computation.46 | convolution fusion | flops 8592031744 | bytes 27262976 | tf_op jit(solution)/shard_map/dot_general | solution.py:25
  680.5 15.1 %fusion.10 = f32[512,2048]{1,0:T(8,128)} fusion(bf16[2048,4096]{1,0:T(8,128)(2,1)} %all-gather.18.cloned.1.call-done, bf16[1024,4096]{1,0:T(8,128)(2,1)} %get-tuple-element.109), kind=kOutput, calls=%fused_computation.23 | convolution fusion | flops 8589934592 | bytes 25165824 | tf_op jit(solution)/shard_map/dot_general | solution.py:25
  695.7 27.4 %collective-permute-done.13 = bf16[512,2048]{1,0:T(8,128)(2,1)} collective-permute-done((bf16[512,2048]{1,0:T(8,128)(2,1)S(1)}, bf16[512,2048]{1,0:T(8,128)(2,1)}, u32[]{:S(2)}, u32[]{:S(2)}) %collective-permute-start.13) | collective-permute-done | bytes 2097184 | tf_op jit(solution)/shard_map/ppermute | solution.py:288
  723.1 19.8 %multiply_reduce_fusion = (f32[2048]{0:T(1024)}, f32[512]{0:T(512)S(1)}, f32[512,2048]{1,0:T(8,128)}) fusion(f32[512,2048]{1,0:T(8,128)} %copy-done.14, f32[512]{0:T(512)S(1)} %copy-done.54, f32[2048]{0:T(1024)S(1)} %copy-done.52, bf16[512,2048]{1,0:T(8,128)(2,1)} %collective-permute-done.13, f32[512,2048]{1,0:T(8,128)} %fusion.10, ...), kind=kOutput, calls=%fused_computation.35 | convolution fusion | flops 8601466880 | bytes 37769216 | tf_op jit(solution)/shard_map/dot_general | solution.py:25
  833.7 14.4 %convolution_convert_fusion = bf16[1024,4096]{1,0:T(8,128)(2,1)} fusion(bf16[1024,1024]{0,1:T(8,128)(2,1)S(1)} %bitcast.102, bf16[1024,4096]{1,0:T(8,128)(2,1)} %get-tuple-element.147), kind=kOutput, calls=%fused_computation.7 | convolution fusion | flops 8594128896 | bytes 18874368 | tf_op jit(solution)/shard_map/dot_general | solution.py:29
  873.6 41.4 %attend_back.1 = (f32[1024,1024]{1,0:T(8,128)}, f32[1024,1024]{1,0:T(8,128)}, bf16[1024,1024]{1,0:T(8,128)(2,1)S(1)}, f32[1,1024]{1,0:T(1,128)S(1)}, f32[1,1024]...) custom-call(s32[1]{0:T(128)} %bitcast.place_ref, bf16[1024,1024]{1,0:T(8,128)(2,1)} %copy-done.9, ...), custom_call_target="tpu_custom_call" | custom-call | flops 21474836480 | bytes 33554432 | tf_op jit(solution)/shard_map/attend_back/pallas_call | solution.py:230
  935.9 16.2 %add_convert_fusion = bf16[1024,4096]{1,0:T(8,128)(2,1)} fusion(bf16[1024,4096]{1,0:T(8,128)(2,1)} %collective-permute-done.29, bf16[1024,1024]{0,1:T(8,128)(2,1)} %bitcast.104, bf16[1024,4096]{1,0:T(8,128)(2,1)} %get-tuple-element.147), kind=kOutput, calls=%fused_computation | convolution fusion | flops 8602517504 | bytes 27262976 | tf_op jit(solution)/shard_map/dot_general | solution.py:29
  1036.2 16.1 %add_convert_fusion.1 = bf16[1024,4096]{1,0:T(8,128)(2,1)} fusion(bf16[1024,4096]{1,0:T(8,128)(2,1)} %collective-permute-done.27, bf16[1024,1024]{0,1:T(8,128)(2,1)S(1)} %bitcast.100, bf16[1024,4096]{1,0:T(8,128)(2,1)} %get-tuple-element.109), kind=kOutput, calls=%fused_computation.1 | convolution fusion | flops 8602517504 | bytes 27262976 | tf_op jit(solution)/shard_map/dot_general | solution.py:29
  1054.0 14.4 %convolution_convert_fusion.2 = bf16[1024,4096]{1,0:T(8,128)(2,1)} fusion(bf16[1024,1024]{0,1:T(8,128)(2,1)S(1)} %bitcast.99, bf16[1024,4096]{1,0:T(8,128)(2,1)} %get-tuple-element.108), kind=kOutput, calls=%fused_computation.9 | convolution fusion | flops 8594128896 | bytes 18874368 | tf_op jit(solution)/shard_map/dot_general | solution.py:29
  1081.8 14.8 %add_convert_fusion.2 = bf16[1024,4096]{1,0:T(8,128)(2,1)} fusion(bf16[1024,4096]{1,0:T(8,128)(2,1)S(1)} %collective-permute-done.25, bf16[1024,1024]{0,1:T(8,128)(2,1)S(1)} %bitcast.101, bf16[1024,4096]{1,0:T(8,128)(2,1)} %get-tuple-element.108), kind=kOutput, calls=%fused_computation.2 | convolution fusion | flops 8602517504 | bytes 27262976 | tf_op jit(solution)/shard_map/dot_general | solution.py:29
  1112.2 71.0 %all-reduce = (f32[2048]{0:T(1024)}, f32[2048]{0:T(1024)}, f32[2048]{0:T(1024)}, f32[2048]{0:T(1024)}) all-reduce(f32[2048]{0:T(1024)S(1)} %dynamic_update_slice.13, f32[2048]{0:T(1024)S(1)} %dynamic_update_slice.15, f32[2048]{0:T(1024)S(1)} %copy-done.57, ...), channel_id=1, replica_groups=mesh['fsdp'=8,'tensor'=4] {'fsdp','tensor'}, use_global_device_ids=true, to_apply=%region_13.14 | all-reduce | flops 8192 | bytes 65536 | tf_op jit(solution)/shard_map/psum | solution.py:462
  1224.5 30.2 %collective-permute-done.24 = bf16[256,512]{1,0:T(8,128)(2,1)S(1)} collective-permute-done((bf16[256,512]{1,0:T(8,128)(2,1)S(1)}, bf16[256,512]{1,0:T(8,128)(2,1)S(1)}, u32[]{:S(2)}, u32[]{:S(2)}) %collective-permute-start.24) | collective-permute-done | bytes 262176 | tf_op jit(solution)/shard_map/ppermute | solution.py:296
  1264.7 46.4 %collective-permute-done.20 = bf16[256,512]{1,0:T(8,128)(2,1)} collective-permute-done((bf16[256,512]{1,0:T(8,128)(2,1)S(1)}, bf16[256,512]{1,0:T(8,128)(2,1)}, u32[]{:S(2)}, u32[]{:S(2)}) %collective-permute-start.20) | collective-permute-done | bytes 262176 | tf_op jit(solution)/shard_map/ppermute | solution.py:296
  1324.6 37.0 %collective-permute-done.28 = bf16[256,2048]{1,0:T(8,128)(2,1)} collective-permute-done((bf16[256,2048]{1,0:T(8,128)(2,1)S(1)}, bf16[256,2048]{1,0:T(8,128)(2,1)}, u32[]{:S(2)}, u32[]{:S(2)}) %collective-permute-start.28) | collective-permute-done | bytes 1048608 | tf_op jit(solution)/shard_map/ppermute | solution.py:296
  1364.8 18.2 %collective-permute-done.26 = bf16[256,2048]{1,0:T(8,128)(2,1)} collective-permute-done((bf16[256,2048]{1,0:T(8,128)(2,1)}, bf16[256,2048]{1,0:T(8,128)(2,1)}, u32[]{:S(2)}, u32[]{:S(2)}) %collective-permute-start.26) | collective-permute-done | bytes 1048608 | tf_op jit(solution)/shard_map/ppermute | solution.py:296
  (330 shorter events, 433.7 us)
Async XLA Ops:
  7.2 263.0 %all-gather.10.cloned.1.call-start = ((), (), s32[]{:S(2)}) async-start(), calls=%async_computation.8 | async-start | bytes 4718592 | tf_op jit(solution)/shard_map/all_gather | solution.py:303
  25.3 254.5 %all-gather.8.cloned.1.call-start = ((), (), s32[]{:S(2)}) async-start(), calls=%async_computation.7 | async-start | bytes 4718592 | tf_op jit(solution)/shard_map/all_gather | solution.py:303
  41.5 248.2 %all-gather.12.cloned.1.call-start = ((), (), s32[]{:S(2)}) async-start(), calls=%async_computation.9 | async-start | bytes 4718592 | tf_op jit(solution)/shard_map/all_gather | solution.py:303
  56.8 288.3 %all-gather.14.cloned.1.call-start = ((), (), s32[]{:S(2)}) async-start(), calls=%async_computation.10 | async-start | bytes 4718592 | tf_op jit(solution)/shard_map/all_gather | solution.py:303
  71.0 375.9 %all-gather.16.cloned.1.call-start = ((), (), s32[]{:S(2)}) async-start(), calls=%async_computation.11 | async-start | bytes 18874368 | tf_op jit(solution)/shard_map/all_gather | solution.py:303
  71.1 48.3 %collective-permute-start.8 = (bf16[256,2048]{1,0:T(8,128)(2,1)S(1)}, bf16[256,2048]{1,0:T(8,128)(2,1)S(1)}, u32[]{:S(2)}, u32[]{:S(2)}) collective-permute-start(bf16[256,2048]{1,0:T(8,128)(2,1)S(1)} %copy-done.39), channel_id=1, source_target_pairs={{0,2},{1,3},{2,0},{3,1},{4,6},{5,7},{6,4},{7,5},{8,10},{9,11},{10,... | collective-permute-start | bytes 3145736 | tf_op jit(solution)/shard_map/ppermute | solution.py:296
  121.0 349.5 %all-gather.18.cloned.1.call-start = ((), (), s32[]{:S(2)}) async-start(), calls=%async_computation.12 | async-start | bytes 18874368 | tf_op jit(solution)/shard_map/all_gather | solution.py:303
  121.0 47.3 %collective-permute-start.9 = (bf16[256,2048]{1,0:T(8,128)(2,1)S(1)}, bf16[256,2048]{1,0:T(8,128)(2,1)S(1)}, u32[]{:S(2)}, u32[]{:S(2)}) collective-permute-start(bf16[256,2048]{1,0:T(8,128)(2,1)S(1)} %copy-done.40), channel_id=1, source_target_pairs={{0,2},{1,3},{2,0},{3,1},{4,6},{5,7},{6,4},{7,5},{8,10},{9,11},{10,... | collective-permute-start | bytes 3145736 | tf_op jit(solution)/shard_map/ppermute | solution.py:296
  169.8 331.0 %all-gather.20.cloned.1.call-start = ((), (), s32[]{:S(2)}) async-start(), calls=%async_computation.13 | async-start | bytes 18874368 | tf_op jit(solution)/shard_map/all_gather | solution.py:303
  169.9 48.3 %collective-permute-start.10 = (bf16[256,2048]{0,1:T(8,128)(2,1)S(1)}, bf16[256,2048]{0,1:T(8,128)(2,1)S(1)}, u32[]{:S(2)}, u32[]{:S(2)}) collective-permute-start(bf16[256,2048]{0,1:T(8,128)(2,1)S(1)} %bitcast.106), channel_id=1, source_target_pairs={{0,2},{1,3},{2,0},{3,1},{4,6},{5,7},{6,4},{7,5},{8,10},{9,11},{10,... | collective-permute-start | bytes 3145736 | tf_op jit(solution)/shard_map/ppermute | solution.py:296
  219.7 978.9 %reduce-scatter.14.cloned.1.call-start = ((), (), s32[]{:S(2)}) async-start(), calls=%async_computation.17 | async-start | bytes 2621440 | tf_op jit(solution)/shard_map/reduce_scatter | solution.py:339
  222.3 47.9 %collective-permute-start = (bf16[512,2048]{0,1:T(8,128)(2,1)}, bf16[512,2048]{0,1:T(8,128)(2,1)}, u32[]{:S(2)}, u32[]{:S(2)}) collective-permute-start(bf16[512,2048]{0,1:T(8,128)(2,1)} %copy.87), channel_id=1, source_target_pairs={{0,1},{1,0},{2,3},{3,2},{4,5},{5,4},{6,7},{7,6},{8,9},{9,8},{10,11... | collective-permute-start | bytes 6291464 | tf_op jit(solution)/shard_map/ppermute | solution.py:288
  350.2 46.5 %collective-permute-start.6 = (bf16[512,2048]{1,0:T(8,128)(2,1)S(1)}, bf16[512,2048]{1,0:T(8,128)(2,1)S(1)}, u32[]{:S(2)}, u32[]{:S(2)}) collective-permute-start(bf16[512,2048]{1,0:T(8,128)(2,1)S(1)} %convolution_convert_fusion.3), channel_id=1, source_target_pairs={{0,1},{1,0},{2,3},{3,2},{4,5},{5,4},{6,7},{7,6},{8,9},{9,8},{10,11... | collective-permute-start | bytes 6291464 | tf_op jit(solution)/shard_map/ppermute | solution.py:288
  401.2 45.7 %collective-permute-start.7 = (bf16[512,2048]{1,0:T(8,128)(2,1)S(1)}, bf16[512,2048]{1,0:T(8,128)(2,1)}, u32[]{:S(2)}, u32[]{:S(2)}) collective-permute-start(bf16[512,2048]{1,0:T(8,128)(2,1)S(1)} %fusion.27), channel_id=1, source_target_pairs={{0,1},{1,0},{2,3},{3,2},{4,5},{5,4},{6,7},{7,6},{8,9},{9,8},{10,11... | collective-permute-start | bytes 6291464 | tf_op jit(solution)/shard_map/ppermute | solution.py:288
  514.6 44.7 %collective-permute-start.11 = (bf16[512,2048]{1,0:T(8,128)(2,1)S(1)}, bf16[512,2048]{1,0:T(8,128)(2,1)S(1)}, u32[]{:S(2)}, u32[]{:S(2)}) collective-permute-start(bf16[512,2048]{1,0:T(8,128)(2,1)S(1)} %fusion.24), channel_id=1, source_target_pairs={{0,1},{1,0},{2,3},{3,2},{4,5},{5,4},{6,7},{7,6},{8,9},{9,8},{10,11... | collective-permute-start | bytes 6291464 | tf_op jit(solution)/shard_map/ppermute | solution.py:288
  574.4 43.8 %collective-permute-start.12 = (bf16[512,2048]{1,0:T(8,128)(2,1)S(1)}, bf16[512,2048]{1,0:T(8,128)(2,1)S(1)}, u32[]{:S(2)}, u32[]{:S(2)}) collective-permute-start(bf16[512,2048]{1,0:T(8,128)(2,1)S(1)} %fusion.4), channel_id=1, source_target_pairs={{0,1},{1,0},{2,3},{3,2},{4,5},{5,4},{6,7},{7,6},{8,9},{9,8},{10,11... | collective-permute-start | bytes 6291464 | tf_op jit(solution)/shard_map/ppermute | solution.py:288
  680.1 43.0 %collective-permute-start.13 = (bf16[512,2048]{1,0:T(8,128)(2,1)S(1)}, bf16[512,2048]{1,0:T(8,128)(2,1)}, u32[]{:S(2)}, u32[]{:S(2)}) collective-permute-start(bf16[512,2048]{1,0:T(8,128)(2,1)S(1)} %add_convert_fusion.8), channel_id=1, source_target_pairs={{0,1},{1,0},{2,3},{3,2},{4,5},{5,4},{6,7},{7,6},{8,9},{9,8},{10,11... | collective-permute-start | bytes 6291464 | tf_op jit(solution)/shard_map/ppermute | solution.py:288
  848.1 87.9 %collective-permute-start.29 = (bf16[1024,4096]{1,0:T(8,128)(2,1)}, bf16[1024,4096]{1,0:T(8,128)(2,1)}, u32[]{:S(2)}, u32[]{:S(2)}) collective-permute-start(bf16[1024,4096]{1,0:T(8,128)(2,1)} %convolution_convert_fusion), channel_id=1, source_target_pairs={{0,4},{4,0},{8,12},{12,8},{16,20},{20,16},{24,28},{28,24},{1,5},{5... | collective-permute-start | bytes 25165832 | tf_op jit(solution)/shard_map/ppermute | solution.py:299
  873.6 328.7 %reduce-scatter.12.cloned.1.call-start = ((), (), s32[]{:S(2)}) async-start(), calls=%async_computation.16 | async-start | bytes 2621440 | tf_op jit(solution)/shard_map/reduce_scatter | solution.py:339
  925.4 278.4 %reduce-scatter.20.cloned.1.call-start = ((), (), s32[]{:S(2)}) async-start(), calls=%async_computation.20 | async-start | bytes 10485760 | tf_op jit(solution)/shard_map/reduce_scatter | solution.py:339
  952.1 266.8 %reduce-scatter.10.cloned.1.call-start = ((), (), s32[]{:S(2)}) async-start(), calls=%async_computation.15 | async-start | bytes 2621440 | tf_op jit(solution)/shard_map/reduce_scatter | solution.py:339
  1010.9 209.7 %reduce-scatter.8.cloned.1.call-start = ((), (), s32[]{:S(2)}) async-start(), calls=%async_computation.14 | async-start | bytes 2621440 | tf_op jit(solution)/shard_map/reduce_scatter | solution.py:339
  1027.1 236.2 %reduce-scatter.18.cloned.1.call-start = ((), (), s32[]{:S(2)}) async-start(), calls=%async_computation.19 | async-start | bytes 10485760 | tf_op jit(solution)/shard_map/reduce_scatter | solution.py:339
  1052.4 266.1 %reduce-scatter.16.cloned.1.call-start = ((), (), s32[]{:S(2)}) async-start(), calls=%async_computation.18 | async-start | bytes 10485760 | tf_op jit(solution)/shard_map/reduce_scatter | solution.py:339
  1109.4 98.1 %collective-permute-start.16 = (bf16[512,2048]{1,0:T(8,128)(2,1)}, bf16[512,2048]{1,0:T(8,128)(2,1)}, u32[]{:S(2)}, u32[]{:S(2)}) collective-permute-start(bf16[512,2048]{1,0:T(8,128)(2,1)} %add_convert_fusion.7), channel_id=1, source_target_pairs={{0,1},{1,0},{2,3},{3,2},{4,5},{5,4},{6,7},{7,6},{8,9},{9,8},{10,11... | collective-permute-start | bytes 6291464 | tf_op jit(solution)/shard_map/ppermute | solution.py:288
  1199.6 55.1 %collective-permute-start.24 = (bf16[256,512]{1,0:T(8,128)(2,1)S(1)}, bf16[256,512]{1,0:T(8,128)(2,1)S(1)}, u32[]{:S(2)}, u32[]{:S(2)}) collective-permute-start(bf16[256,512]{1,0:T(8,128)(2,1)S(1)} %slice.187), channel_id=1, source_target_pairs={{0,2},{1,3},{2,0},{3,1},{4,6},{5,7},{6,4},{7,5},{8,10},{9,11},{10,... | collective-permute-start | bytes 786440 | tf_op jit(solution)/shard_map/ppermute | solution.py:296
  1203.2 57.3 %collective-permute-start.22 = (bf16[256,512]{1,0:T(8,128)(2,1)S(1)}, bf16[256,512]{1,0:T(8,128)(2,1)}, u32[]{:S(2)}, u32[]{:S(2)}) collective-permute-start(bf16[256,512]{1,0:T(8,128)(2,1)S(1)} %slice.185), channel_id=1, source_target_pairs={{0,2},{1,3},{2,0},{3,1},{4,6},{5,7},{6,4},{7,5},{8,10},{9,11},{10,... | collective-permute-start | bytes 786440 | tf_op jit(solution)/shard_map/ppermute | solution.py:296
  1205.0 115.8 %collective-permute-start.30 = (bf16[256,2048]{1,0:T(8,128)(2,1)S(1)}, bf16[256,2048]{1,0:T(8,128)(2,1)}, u32[]{:S(2)}, u32[]{:S(2)}) collective-permute-start(bf16[256,2048]{1,0:T(8,128)(2,1)S(1)} %slice.193), channel_id=1, source_target_pairs={{0,2},{1,3},{2,0},{3,1},{4,6},{5,7},{6,4},{7,5},{8,10},{9,11},{10,... | collective-permute-start | bytes 3145736 | tf_op jit(solution)/shard_map/ppermute | solution.py:296
  1219.9 91.1 %collective-permute-start.20 = (bf16[256,512]{1,0:T(8,128)(2,1)S(1)}, bf16[256,512]{1,0:T(8,128)(2,1)}, u32[]{:S(2)}, u32[]{:S(2)}) collective-permute-start(bf16[256,512]{1,0:T(8,128)(2,1)S(1)} %slice.183), channel_id=1, source_target_pairs={{0,2},{1,3},{2,0},{3,1},{4,6},{5,7},{6,4},{7,5},{8,10},{9,11},{10,... | collective-permute-start | bytes 786440 | tf_op jit(solution)/shard_map/ppermute | solution.py:296
  1222.3 94.3 %collective-permute-start.18 = (bf16[256,512]{1,0:T(8,128)(2,1)}, bf16[256,512]{1,0:T(8,128)(2,1)}, u32[]{:S(2)}, u32[]{:S(2)}) collective-permute-start(bf16[256,512]{1,0:T(8,128)(2,1)} %slice.181), channel_id=1, source_target_pairs={{0,2},{1,3},{2,0},{3,1},{4,6},{5,7},{6,4},{7,5},{8,10},{9,11},{10,... | collective-permute-start | bytes 786440 | tf_op jit(solution)/shard_map/ppermute | solution.py:296
  1264.6 97.0 %collective-permute-start.28 = (bf16[256,2048]{1,0:T(8,128)(2,1)S(1)}, bf16[256,2048]{1,0:T(8,128)(2,1)}, u32[]{:S(2)}, u32[]{:S(2)}) collective-permute-start(bf16[256,2048]{1,0:T(8,128)(2,1)S(1)} %slice.191), channel_id=1, source_target_pairs={{0,2},{1,3},{2,0},{3,1},{4,6},{5,7},{6,4},{7,5},{8,10},{9,11},{10,... | collective-permute-start | bytes 3145736 | tf_op jit(solution)/shard_map/ppermute | solution.py:296
  1320.8 62.1 %collective-permute-start.26 = (bf16[256,2048]{1,0:T(8,128)(2,1)}, bf16[256,2048]{1,0:T(8,128)(2,1)}, u32[]{:S(2)}, u32[]{:S(2)}) collective-permute-start(bf16[256,2048]{1,0:T(8,128)(2,1)} %slice.189), channel_id=1, source_target_pairs={{0,2},{1,3},{2,0},{3,1},{4,6},{5,7},{6,4},{7,5},{8,10},{9,11},{10,... | collective-permute-start | bytes 3145736 | tf_op jit(solution)/shard_map/ppermute | solution.py:296
  (82 other events, 1801.6 us)
Sparse Core Ops, SparseCore 0:
  25.4 37.8 all-gather.9
  65.8 36.7 all-gather.7
  105.1 36.7 all-gather.11
  144.1 37.4 all-gather.13
  183.3 89.8 all-gather.15
  275.5 89.8 all-gather.17
  367.3 93.1 all-gather.19
  873.7 38.2 reduce-scatter.13
  925.5 38.2 reduce-scatter.11
  966.7 86.3 reduce-scatter.19
  1056.3 35.1 reduce-scatter.9
  1094.4 35.5 reduce-scatter.7
  1133.4 87.0 reduce-scatter.17
  1223.3 86.3 reduce-scatter.15

commit v2 on v1

--- a/solution.py
+++ b/solution.py
@@ -27,6 +27,10 @@
 
 def tn(a, b):
     return lax.dot_general(a, b, (((0,), (0,)), ((), ())), preferred_element_type=F32)
+
+
+def after(x, *earlier):
+    return lax.optimization_barrier((x, *earlier))[0]
 
 
 def block_start(place, block, rows, parts):
@@ -183,26 +187,440 @@
     key_gain_out_ref[...] = key_gain_sum
 
 
-def attention_specs(width):
+MESH = pl.DeviceIdType.MESH
+MIB = 2**20
+
+
+def flip(index, bit):
+    return index + bit - 2 * bit * lax.rem(lax.div(index, bit), 2)
+
+
+def row_shares(rows, count):
+    units = rows // 16
+    sizes = [16 * (units // count + (i < units % count)) for i in range(count)]
+    starts = [sum(sizes[:i]) for i in range(count)]
+    return list(zip(starts, sizes))
+
+
+class Copies:
+    def __init__(self, send_sems, recv_sems):
+        self.send_sems, self.recv_sems = send_sems, recv_sems
+        self.used = 0
+        self.open = []
+
+    def send(self, src, dst, **device):
+        copy = pltpu.make_async_remote_copy(
+            src_ref=src,
+            dst_ref=dst,
+            send_sem=self.send_sems.at[self.used],
+            recv_sem=self.recv_sems.at[self.used],
+            device_id=device,
+            device_id_type=MESH,
+        )
+        self.used += 1
+        copy.start()
+        self.open.append(copy.wait_send)
+        return copy
+
+    def move(self, src, dst):
+        copy = pltpu.make_async_copy(src, dst, self.send_sems.at[self.used])
+        self.used += 1
+        copy.start()
+        self.open.append(copy.wait)
+
+    def finish(self):
+        for wait in self.open:
+            wait()
+
+
+def exchange_kernel(fsdp, parts, spans, plan, counts, *refs):
+    rows_count, shard_count, send_count, full_count, _ = counts
+    rows_refs, refs = refs[:rows_count], refs[rows_count:]
+    shard_refs, refs = refs[:shard_count], refs[shard_count:]
+    span_refs, refs = refs[:send_count], refs[send_count + counts[4] :]
+    rows_outs, refs = refs[:rows_count], refs[rows_count:]
+    full_refs, refs = refs[:full_count], refs[full_count:]
+    span_outs = refs[:send_count]
+    copies = Copies(*refs[-2:])
+    me, rank = lax.axis_index("fsdp"), lax.axis_index("tensor")
+    place, span = lax.rem(rank, parts), lax.div(rank, parts)
+    bits = [1 << b for b in range(1, fsdp.bit_length() - 1)]
+    part_ranks = [span * parts + lax.rem(place + p, parts) for p in range(1, parts)]
+    span_ranks = [lax.rem(span + s, spans) * parts + place for s in range(1, spans)]
+    partners = [{"fsdp": flip(me, bit)} for bit in [1, *bits]]
+    if rows_count:
+        partners += [{"tensor": r} for r in part_ranks]
+    if send_count or any(s and not here for _, s, _, here in plan):
+        partners += [{"tensor": r} for r in span_ranks]
+    barrier = pltpu.get_barrier_semaphore()
+    for partner in partners:
+        pl.semaphore_signal(barrier, inc=1, device_id=partner, device_id_type=MESH)
+    pl.semaphore_wait(barrier, len(partners))
+
+    def slot(job, mask, share=None):
+        group, s, position, _ = plan[job]
+        which = me
+        for bit in [1, *bits]:
+            if mask & bit:
+                which = flip(which, bit)
+        cols = shard_refs[job].shape[1]
+        ref = full_refs[group].at[which, :, pl.ds(position * cols, cols)]
+        return ref if share is None else ref.at[pl.ds(*share)]
+
+    depth = shard_refs[0].shape[0]
+    shares = row_shares(depth, len(bits))
+    jobs = range(len(plan))
+    remote = [s and not here for _, s, _, here in plan]
+    from_span = {
+        job: copies.send(shard_refs[job], slot(job, 0), tensor=span_ranks[plan[job][1] - 1])
+        for job in jobs
+        if remote[job]
+    }
+    over = []
+    for ref, out in zip(rows_refs, rows_outs):
+        for p, r in enumerate(part_ranks):
+            over.append(copies.send(ref, out.at[p + 1], tensor=r))
+        copies.move(ref, out.at[0])
+    for ref, out in zip(span_refs, span_outs):
+        for s, r in enumerate(span_ranks):
+            over.append(copies.send(ref, out.at[s], tensor=r))
+    for job in jobs:
+        if not remote[job]:
+            copies.move(shard_refs[job], slot(job, 0))
+
+    arriving = {}
+    held = {(job, p): [0] for job in jobs for p in range(len(shares))}
+
+    def source(job, mask, share):
+        if mask == 0 and not remote[job]:
+            return shard_refs[job].at[pl.ds(*share)]
+        return slot(job, mask, share)
+
+    def send_step(job, step):
+        for p, share in enumerate(shares):
+            bit = bits[(p + step) % len(bits)]
+            for mask in held[job, p]:
+                arriving[job, p, mask | bit] = copies.send(
+                    source(job, mask, share), slot(job, mask, share), fsdp=flip(me, bit)
+                )
+
+    def take_step(job, step):
+        for p in range(len(shares)):
+            bit = bits[(p + step) % len(bits)]
+            came = [mask | bit for mask in held[job, p]]
+            for mask in came:
+                arriving[job, p, mask].wait_recv()
+            held[job, p] += came
+
+    for step in range(len(bits) + 1):
+        for job in jobs:
+            if step == 0 and remote[job]:
+                from_span[job].wait_recv()
+            if step:
+                take_step(job, step - 1)
+            if step < len(bits):
+                send_step(job, step)
+            else:
+                for mask in range(0, fsdp, 2):
+                    whole = (0, depth)
+                    over.append(
+                        copies.send(
+                            source(job, mask, whole), slot(job, mask), fsdp=flip(me, 1)
+                        )
+                    )
+    for copy in over:
+        copy.wait_recv()
+    copies.finish()
+
+
+def exchange(number, fsdp, parts, spans, shards, plan, rows=(), sends=(), earlier=()):
+    bits = fsdp.bit_length() - 2
+    depth = shards[0].shape[0]
+    per_job = 2 + bits * (2**bits - 1) + 2**bits
+    count = parts * len(rows) + len(plan) * per_job + len(sends) * spans
+    hbm = pl.BlockSpec(memory_space=pl.ANY)
+    full_count = 1 + max(group for group, *_ in plan)
+    widths = [0] * full_count
+    for shard, (group, *_) in zip(shards, plan):
+        widths[group] += shard.shape[1]
+    outs = [jax.ShapeDtypeStruct((parts, *r.shape), LOW) for r in rows]
+    outs += [jax.ShapeDtypeStruct((fsdp, depth, width), LOW) for width in widths]
+    outs += [jax.ShapeDtypeStruct((spans - 1, *x.shape), LOW) for x in sends]
+    counts = (len(rows), len(shards), len(sends), full_count, len(earlier))
+    inputs = (*rows, *shards, *sends, *earlier)
+    results = pl.pallas_call(
+        functools.partial(exchange_kernel, fsdp, parts, spans, plan, counts),
+        out_shape=outs,
+        in_specs=[hbm] * len(inputs),
+        out_specs=[hbm] * len(outs),
+        scratch_shapes=[
+            pltpu.SemaphoreType.DMA((count,)),
+            pltpu.SemaphoreType.DMA((count,)),
+        ],
+        compiler_params=pltpu.CompilerParams(collective_id=number, has_side_effects=True),
+        name="exchange",
+    )(*inputs)
+    gathered = [r.reshape(-1, r.shape[2]) for r in results[: len(rows)]]
+    full = [r.reshape(fsdp * depth, -1) for r in results[len(rows) : len(rows) + full_count]]
+    return gathered, full, results[len(rows) + full_count :]
+
+
+def sum_kernel(pairs, has_addend, *refs):
+    out_ref = refs[-1]
+    total = refs[-2][...].astype(F32) if has_addend else None
+    for i in range(pairs):
+        term = nt(refs[2 * i][...], refs[2 * i + 1][...])
+        total = term if total is None else total + term
+    out_ref[...] = total.astype(out_ref.dtype)
+
+
+def product_sum(rows, block, pairs, kind, addend=None):
+    width = pairs[0][1].shape[0]
+    tile = min(512, width)
+    specs, operands, flops = [], [], 0
+    for a, b, run in pairs:
+        depth = a.shape[1]
+        specs.append(pl.BlockSpec((rows, depth), lambda j: (block, 0)))
+        specs.append(pl.BlockSpec((tile, depth), lambda j, run=run: (j, run)))
+        operands += [a, b]
+        flops += 2 * rows * depth * width
+    out = pl.BlockSpec((rows, tile), lambda j: (0, j))
+    if addend is not None:
+        specs.append(out)
+        operands.append(addend)
+    return pl.pallas_call(
+        functools.partial(sum_kernel, len(pairs), addend is not None),
+        grid=(width // tile,),
+        in_specs=specs,
+        out_specs=out,
+        out_shape=jax.ShapeDtypeStruct((rows, width), kind),
+        compiler_params=pltpu.CompilerParams(vmem_limit_bytes=56 * MIB),
+        cost_estimate=pl.CostEstimate(
+            flops=flops, bytes_accessed=flops // rows + 4 * rows * width, transcendentals=0
+        ),
+        name="product_sum",
+    )(*operands)
+
+
+def up_kernel(mixed_ref, gate_weight_ref, up_weight_ref, gate_ref, upper_ref, hidden_ref):
+    gate = nn(mixed_ref[...], gate_weight_ref[...])
+    upper = nn(mixed_ref[...], up_weight_ref[...])
+    gate_ref[...] = gate
+    upper_ref[...] = upper
+    hidden_ref[...] = (gate * jax.nn.sigmoid(gate) * upper).astype(LOW)
+
+
+def feed_up(mixed, gate_up):
+    rows, depth = mixed.shape
+    cols = gate_up.shape[1] // 2
+    tile = min(256, cols)
+    tiles = cols // tile
+    out = pl.BlockSpec((rows, tile), lambda j: (0, j))
+    return pl.pallas_call(
+        up_kernel,
+        grid=(tiles,),
+        in_specs=[
+            pl.BlockSpec((rows, depth), lambda j: (0, 0)),
+            pl.BlockSpec((depth, tile), lambda j: (0, j)),
+            pl.BlockSpec((depth, tile), lambda j: (0, j + tiles)),
+        ],
+        out_specs=[out, out, out],
+        out_shape=[
+            jax.ShapeDtypeStruct((rows, cols), F32),
+            jax.ShapeDtypeStruct((rows, cols), F32),
+            jax.ShapeDtypeStruct((rows, cols), LOW),
+        ],
+        compiler_params=pltpu.CompilerParams(vmem_limit_bytes=48 * MIB),
+        cost_estimate=pl.CostEstimate(
+            flops=4 * rows * depth * cols,
+            bytes_accessed=4 * depth * cols + 10 * rows * cols,
+            transcendentals=rows * cols,
+        ),
+        name="feed_up",
+    )(mixed, gate_up, gate_up)
+
+
+def up_back_kernel(grad_ref, down_ref, gate_ref, upper_ref, gate_out_ref, up_out_ref):
+    grad = nn(grad_ref[...], down_ref[...])
+    gate = gate_ref[...]
+    sigmoid = jax.nn.sigmoid(gate)
+    scaled = grad * sigmoid
+    up_out_ref[...] = (scaled * gate).astype(LOW)
+    gate_out_ref[...] = (scaled * upper_ref[...] * (1.0 + gate * (1.0 - sigmoid))).astype(LOW)
+
+
+def feed_up_back(grad_rows, down, gate, upper):
+    rows, depth = grad_rows.shape
+    cols = down.shape[1]
+    tile = min(512, cols)
+    spec = pl.BlockSpec((rows, tile), lambda j: (0, j))
+    out = jax.ShapeDtypeStruct((rows, cols), LOW)
+    return pl.pallas_call(
+        up_back_kernel,
+        grid=(cols // tile,),
+        in_specs=[
+            pl.BlockSpec((rows, depth), lambda j: (0, 0)),
+            pl.BlockSpec((depth, tile), lambda j: (0, j)),
+            spec,
+            spec,
+        ],
+        out_specs=[spec, spec],
+        out_shape=[out, out],
+        compiler_params=pltpu.CompilerParams(vmem_limit_bytes=52 * MIB),
+        cost_estimate=pl.CostEstimate(
+            flops=2 * rows * depth * cols,
+            bytes_accessed=2 * depth * cols + 12 * rows * cols,
+            transcendentals=rows * cols,
+        ),
+        name="feed_up_back",
+    )(grad_rows, down, gate, upper)
+
+
+def weight_grad_kernel(pieces, tiles, has_addend, parity_ref, *refs):
+    x_refs, grad_refs = refs[:pieces], refs[pieces : pieces + len(tiles)]
+    addend_ref = refs[-3] if has_addend else None
+    out_ref, x_half = refs[-2:]
+    depth = x_refs[0].shape[1]
+    step = pl.program_id(0)
+
+    @pl.when(step == 0)
+    def _():
+        for i, ref in enumerate(x_refs):
+            x_half[:, i * depth : (i + 1) * depth] = ref[...]
+
+    first = 0
+    for ref, count in zip(grad_refs, tiles):
+
+        @pl.when(jnp.logical_and(step >= first, step < first + count))
+        def _(ref=ref):
+            total = tn(x_half[...], ref[...])
+            if has_addend:
+                total = total + addend_ref[...].astype(F32)
+            out_ref[...] = total.astype(LOW)
+
+        first += count
+
+
+def weight_grad_half(fsdp, parity, x, grads, addend=None):
+    rows, width = x.shape
+    depth, pieces = width // fsdp, fsdp // 2
+    tile = math.gcd(1024, *[g.shape[1] for g in grads])
+    tiles = [g.shape[1] // tile for g in grads]
+    firsts = [sum(tiles[:i]) for i in range(len(tiles))]
+    cols = tile * sum(tiles)
+
+    def x_spec(i):
+        return pl.BlockSpec((rows, depth), lambda j, parity: (0, 2 * i + parity[0]))
+
+    def grad_spec(first, count):
+        return pl.BlockSpec(
+            (rows, tile), lambda j, parity: (0, jnp.clip(j - first, 0, count - 1))
+        )
+
+    out = pl.BlockSpec((width // 2, tile), lambda j, parity: (0, j))
+    specs = [x_spec(i) for i in range(pieces)]
+    specs += [grad_spec(f, c) for f, c in zip(firsts, tiles)]
+    extra = [] if addend is None else [addend]
+    return pl.pallas_call(
+        functools.partial(weight_grad_kernel, pieces, tiles, addend is not None),
+        grid_spec=pltpu.PrefetchScalarGridSpec(
+            num_scalar_prefetch=1,
+            grid=(sum(tiles),),
+            in_specs=specs + [out] * len(extra),
+            out_specs=out,
+            scratch_shapes=[pltpu.VMEM((rows, width // 2), LOW)],
+        ),
+        out_shape=jax.ShapeDtypeStruct((width // 2, cols), LOW),
+        compiler_params=pltpu.CompilerParams(vmem_limit_bytes=52 * MIB),
+        cost_estimate=pl.CostEstimate(
+            flops=rows * width * cols,
+            bytes_accessed=rows * width + 2 * rows * cols + width * cols,
+            transcendentals=0,
+        ),
+        name="weight_grad",
+    )(parity, *[x] * pieces, *grads, *extra)
+
+
+def project_kernel(tiles, rows_ref, weight_ref, pre_ref, value_ref, query_sq_ref, key_sq_ref):
+    step = pl.program_id(0)
+    result = nn(rows_ref[...], weight_ref[...])
+    squares = jnp.sum(result * result, axis=1, keepdims=True)
+
+    @pl.when(step < 2 * tiles)
+    def _():
+        pre_ref[...] = result
+
+    for first, ref in ((0, query_sq_ref), (tiles, key_sq_ref)):
+
+        @pl.when(step == first)
+        def _(ref=ref):
+            ref[...] = squares
+
+        @pl.when(jnp.logical_and(step > first, step < first + tiles))
+        def _(ref=ref):
+            ref[...] += squares
+
+    @pl.when(step >= 2 * tiles)
+    def _():
+        value_ref[...] = result.astype(LOW)
+
+
+def project(inputs, full):
+    rows, depth = inputs.shape
+    cols = full.shape[1] // 3
+    tile = min(512, cols)
+    tiles = cols // tile
+    column = pl.BlockSpec((rows, 1), lambda j: (0, 0))
+    return pl.pallas_call(
+        functools.partial(project_kernel, tiles),
+        grid=(3 * tiles,),
+        in_specs=[
+            pl.BlockSpec((rows, depth), lambda j: (0, 0)),
+            pl.BlockSpec((depth, tile), lambda j: (0, j)),
+        ],
+        out_specs=[
+            pl.BlockSpec((rows, tile), lambda j: (0, jnp.minimum(j, 2 * tiles - 1))),
+            pl.BlockSpec((rows, tile), lambda j: (0, jnp.maximum(j - 2 * tiles, 0))),
+            column,
+            column,
+        ],
+        out_shape=[
+            jax.ShapeDtypeStruct((rows, 2 * cols), F32),
+            jax.ShapeDtypeStruct((rows, cols), LOW),
+            jax.ShapeDtypeStruct((rows, 1), F32),
+            jax.ShapeDtypeStruct((rows, 1), F32),
+        ],
+        compiler_params=pltpu.CompilerParams(vmem_limit_bytes=48 * MIB),
+        cost_estimate=pl.CostEstimate(
+            flops=6 * rows * depth * cols,
+            bytes_accessed=6 * depth * cols + 10 * rows * cols + 2 * rows * depth,
+            transcendentals=0,
+        ),
+        name="project",
+    )(inputs, full)
+
+
+def attention_specs(heads):
     head = pl.BlockSpec((SEQ_LEN, HEAD_DIM), lambda i, place: (0, i))
+    later = pl.BlockSpec((SEQ_LEN, HEAD_DIM), lambda i, place: (0, i + heads))
     whole = pl.BlockSpec((SEQ_LEN, HEAD_DIM), lambda i, place: (0, 0))
     column = pl.BlockSpec((SEQ_LEN, 1), lambda i, place: (0, 0))
     gain = pl.BlockSpec((1, HEAD_DIM), lambda i, place: (0, i))
     lse = pl.BlockSpec((None, SEQ_LEN, 1), lambda i, place: (i, 0, 0))
-    return head, whole, column, gain, lse
-
-
-def attend(rows, parts, place, query, key, value, invs, gains, tables):
-    width = query.shape[1]
+    return head, later, whole, column, gain, lse
+
+
+def attend(rows, parts, place, pre, value, invs, gains, tables):
+    width = value.shape[1]
     heads = width // HEAD_DIM
-    head, whole, column, gain, lse = attention_specs(width)
+    head, later, whole, column, gain, lse = attention_specs(heads)
     low = jax.ShapeDtypeStruct((SEQ_LEN, width), LOW)
     return pl.pallas_call(
         functools.partial(attend_kernel, rows, parts, 1.0 / math.sqrt(HEAD_DIM)),
         grid_spec=pltpu.PrefetchScalarGridSpec(
             num_scalar_prefetch=1,
             grid=(heads,),
-            in_specs=[head, head, head, column, column, gain, gain, whole, whole],
+            in_specs=[head, later, head, column, column, gain, gain, whole, whole],
             out_specs=[head, head, head, lse],
             scratch_shapes=[
                 pltpu.VMEM((SEQ_LEN, HEAD_DIM), LOW),
@@ -217,13 +635,13 @@
             transcendentals=heads * SEQ_LEN * SEQ_LEN,
         ),
         name="attend",
-    )(place, query, key, value, *invs, *gains, *tables)
-
-
-def attend_back(rows, parts, place, rots, value, grad, lse_all, pres, invs, gains, tables):
+    )(place, pre, pre, value, *invs, *gains, *tables)
+
+
+def attend_back(rows, parts, place, rots, value, grad, lse_all, pre, invs, gains, tables):
     width = value.shape[1]
     heads = width // HEAD_DIM
-    head, whole, column, gain, lse = attention_specs(width)
+    head, later, whole, column, gain, lse = attention_specs(heads)
     full = jax.ShapeDtypeStruct((SEQ_LEN, width), F32)
     gain_out = jax.ShapeDtypeStruct((1, width), F32)
     inner = jax.ShapeDtypeStruct((SEQ_LEN, 1), F32)
@@ -232,7 +650,7 @@
         grid_spec=pltpu.PrefetchScalarGridSpec(
             num_scalar_prefetch=1,
             grid=(heads,),
-            in_specs=[head, head, head, head, lse, head, head]
+            in_specs=[head, head, head, head, lse, head, later]
             + [column, column, gain, gain, whole, whole],
             out_specs=[head, head, head, gain, gain, column, column],
             scratch_shapes=[
@@ -258,7 +676,7 @@
             transcendentals=heads * SEQ_LEN * SEQ_LEN,
         ),
         name="attend_back",
-    )(place, *rots, value, grad, lse_all, *pres, *invs, *gains, *tables)
+    )(place, *rots, value, grad, lse_all, pre, pre, *invs, *gains, *tables)
 
 
 def norm_back(grad_hat, values_hat, inverse, width):
@@ -295,55 +713,56 @@
         ]
         return lax.ppermute(x, "tensor", pairs)
 
-    def to_other_core(x):
-        return lax.ppermute(x, "fsdp", [(f, f ^ 1) for f in range(fsdp)])
-
-    def gather_weight(shard):
-        wide = [shard] + [to_span(shard, s) for s in range(1, spans)]
-        return lax.all_gather(jnp.concatenate(wide, axis=1), "fsdp", axis=0, tiled=True)
+    def gather_shard(shard):
+        return lax.all_gather(shard, "fsdp", axis=0, tiled=True)
 
     def gather_rows(own):
         return jnp.concatenate([own] + [to_part(own, p) for p in range(1, parts)], axis=0)
 
-    def scatter_rows(make):
-        away = [
-            to_part(make(slice(p * rows_here, (p + 1) * rows_here)).astype(LOW), -p)
-            for p in range(1, parts)
+    def product_others(pairs):
+        return [
+            to_part(product_sum(rows_here, p, pairs, LOW), -p) for p in range(1, parts)
         ]
-        total = make(slice(0, rows_here))
-        for piece in away:
+
+    def product_own(pairs, came):
+        total = product_sum(rows_here, 0, pairs, F32)
+        for piece in came:
             total = total + piece.astype(F32)
         return total
 
     def sum_parts(x):
         total = x
         for p in range(1, parts):
-            total = total + jnp.roll(to_part(x, p), p * rows_here, axis=1)
+            total = total + jnp.roll(to_part(x, p), p * rows_here, axis=0)
         return total
 
-    def core_halves(x):
-        split = x.reshape(x.shape[0], fsdp // 2, 2, width // fsdp)
-        return [
-            lax.dynamic_index_in_dim(split, which, 2, keepdims=False).reshape(
-                x.shape[0], width // 2
-            )
-            for which in (core, 1 - core)
-        ]
+    def sum_all(x):
+        for axis, size in (("fsdp", fsdp), ("tensor", tensor)):
+            bit = 1
+            while bit < size:
+                x = x + lax.ppermute(x, axis, [(i, i ^ bit) for i in range(size)])
+                bit *= 2
+        return x
 
     same_core = [list(range(c, fsdp, 2)) for c in range(2)]
-
-    def weight_grad(halves, grads):
-        mine, other = halves
-        sent = to_other_core(tn(other, grads).astype(LOW))
-        total = (tn(mine, grads) + sent.astype(F32)).astype(LOW)
-        total = lax.psum_scatter(
+    mine = jnp.full((1,), core, jnp.int32)
+
+    def weight_grad_away(x, grads):
+        sent = weight_grad_half(fsdp, 1 - mine, x, grads)
+        return sent, lax.ppermute(sent, "fsdp", [(f, f ^ 1) for f in range(fsdp)])
+
+    def weight_grad_here(x, grads, came):
+        total = weight_grad_half(fsdp, mine, x, grads, came)
+        return total, lax.psum_scatter(
             total, "fsdp", scatter_dimension=0, tiled=True, axis_index_groups=same_core
         )
-        cols = total.shape[1] // spans
-        result = total[:, :cols].astype(F32)
+
+    def sum_spans(total, weights):
+        split = total.reshape(total.shape[0], weights, spans, -1)
+        result = split[:, :, 0].astype(F32)
         for s in range(1, spans):
-            result = result + to_span(total[:, s * cols : (s + 1) * cols], -s).astype(F32)
-        return result
+            result = result + to_span(split[:, :, s], -s).astype(F32)
+        return [result[:, w] for w in range(weights)]
 
     def own_columns(s):
         return ((span + spans - s) % spans * parts + place) * head_cols
@@ -361,14 +780,19 @@
             )
         return whole
 
-    inputs = gather_rows(layer_input)
-    full_query = gather_weight(query_weight)
-    full_key = gather_weight(key_weight)
-    full_value = gather_weight(value_weight)
-    full_out = gather_weight(out_weight.T)
-    full_gate = gather_weight(gate_weight)
-    full_up = gather_weight(up_weight)
-    full_down = gather_weight(down_weight.T)
+    gate_up_shard = jnp.concatenate([gate_weight, up_weight], axis=1)
+    down_shard = down_weight.T
+    first = [query_weight, key_weight, value_weight, out_weight.T]
+    shards, plan = [], []
+    for s in range(spans):
+        for w, shard in enumerate(first):
+            shards.append(shard)
+            plan.append((w // 3, s, w % 3 * spans + s, False))
+    (inputs,), (full_qkv, full_out), _ = exchange(
+        0, fsdp, parts, spans, shards, plan, rows=[layer_input]
+    )
+    full_gate_up = [gather_shard(after(gate_up_shard, inputs))]
+    gate_up_came = [to_span(after(gate_up_shard, inputs), s) for s in range(1, spans)]
 
     local = jnp.arange(SEQ_LEN)
     position = (place + parts - local // rows_here) % parts * rows_here + local % rows_here
@@ -379,26 +803,39 @@
     gains = (gain_here(query_gain), gain_here(key_gain))
     place_arr = jnp.full((1,), place, jnp.int32)
 
-    query_pre = nn(inputs, full_query)
-    key_pre = nn(inputs, full_key)
-    value_low = nn(inputs, full_value).astype(LOW)
-    squares = jnp.stack(
-        [jnp.sum(query_pre * query_pre, axis=1), jnp.sum(key_pre * key_pre, axis=1)]
-    )
-    invs = lax.rsqrt(sum_parts(squares) / width + EPSILON)
-    invs = (invs[0][:, None], invs[1][:, None])
+    pre, value_low, query_sq, key_sq = project(inputs, full_qkv)
+    squares = sum_parts(jnp.concatenate([query_sq, key_sq], axis=1))
+    invs = lax.rsqrt(squares / width + EPSILON)
+    invs = (invs[:, :1], invs[:, 1:])
     attended, query_rot, key_rot, lse = attend(
-        rows_here, parts, place_arr, query_pre, key_pre, value_low, invs, gains, tables
-    )
-    branch = scatter_rows(lambda part: nt(attended[part], full_out))
+        rows_here, parts, place_arr, pre, value_low, invs, gains, tables
+    )
+    full_gate_up += [gather_shard(after(came, attended)) for came in gate_up_came]
+    others = product_others([(attended, full_out, 0)])
+    _, (down_own,), (down_came,) = exchange(
+        1, fsdp, parts, spans, [down_shard], [(0, 0, 0, True)], sends=[down_shard], earlier=others
+    )
+    branch = product_own([(attended, full_out, 0)], others)
     branch_inv = lax.rsqrt(jnp.mean(branch * branch, axis=1, keepdims=True) + EPSILON)
     branch_hat = branch * branch_inv
     middle = layer_input.astype(F32) + branch_hat * attn_gain
-    mixed = gather_rows(middle.astype(LOW))
-    gate = nn(mixed, full_gate)
-    upper = nn(mixed, full_up)
-    hidden = (jax.nn.silu(gate) * upper).astype(LOW)
-    second = scatter_rows(lambda part: nt(hidden[part], full_down))
+    middle_low = middle.astype(LOW)
+    mixed_pieces = [to_part(middle_low, p) for p in range(1, parts)]
+    _, full_down, _ = exchange(
+        2,
+        fsdp,
+        parts,
+        spans,
+        [down_came[s] for s in range(spans - 1)],
+        [(s, s + 1, 0, True) for s in range(spans - 1)],
+        earlier=[middle_low, full_gate_up[0]],
+    )
+    full_down = [down_own, *full_down]
+    mixed_pieces = [after(piece, full_down[-1]) for piece in mixed_pieces]
+    mixed = jnp.concatenate([middle_low, *mixed_pieces], axis=0)
+    gates, uppers, hiddens = zip(*[feed_up(mixed, full) for full in full_gate_up])
+    pairs = [(hidden, down, 0) for hidden, down in zip(hiddens, full_down)]
+    second = product_own(pairs, product_others(pairs))
     second_inv = lax.rsqrt(jnp.mean(second * second, axis=1, keepdims=True) + EPSILON)
     second_hat = second * second_inv
     output = (middle + second_hat * ffn_gain).astype(LOW)
@@ -407,23 +844,39 @@
     ffn_gain_part = jnp.sum(grad_out * second_hat, axis=0)
     grad_second = norm_back(grad_out * ffn_gain, second_hat, second_inv, width)
     grad_rows = gather_rows(grad_second.astype(LOW))
-    grad_hidden = nn(grad_rows, full_down)
-    down_grad = weight_grad(core_halves(grad_rows), hidden).T
-    sigmoid = jax.nn.sigmoid(gate)
-    grad_upper = (grad_hidden * gate * sigmoid).astype(LOW)
-    grad_gate = (grad_hidden * upper * sigmoid * (1.0 + gate * (1.0 - sigmoid))).astype(LOW)
-    mixed_halves = core_halves(mixed)
-    gate_grad = weight_grad(mixed_halves, grad_gate)
-    up_grad = weight_grad(mixed_halves, grad_upper)
-    grad_mixed = scatter_rows(
-        lambda part: nt(grad_gate[part], full_gate) + nt(grad_upper[part], full_up)
-    )
-    grad_middle = grad_out + grad_mixed
-    attn_gain_part = jnp.sum(grad_middle * branch_hat, axis=0)
-    grad_branch = norm_back(grad_middle * attn_gain, branch_hat, branch_inv, width)
-    grad_branch_rows = gather_rows(grad_branch.astype(LOW))
+    sent, came = weight_grad_away(grad_rows, hiddens)
+    cols = gate_weight.shape[1]
+    back, now = [], sent
+    for s, (down, gate, upper) in enumerate(zip(full_down, gates, uppers)):
+        back.append(feed_up_back(after(grad_rows, now), down, gate, upper))
+        now = back[-1][0]
+        if s == 0:
+            total, down_grad = weight_grad_here(after(grad_rows, now), hiddens, came)
+            now = total
+
+    pairs = [
+        (grad, full, run) for pair, full in zip(back, full_gate_up) for run, grad in enumerate(pair)
+    ]
+    others = product_others(pairs)
+    grad_mixed = product_sum(rows_here, 0, pairs, F32)
+    now = grad_mixed
+    gate_up_grad = {}
+    for s in reversed(range(spans)):
+        sent, came = weight_grad_away(after(mixed, now), back[s])
+        total, gate_up_grad[s] = weight_grad_here(after(mixed, sent), back[s], came)
+        now = total
+        if s == spans - 1:
+            for piece in others:
+                grad_mixed = grad_mixed + after(piece, now, down_grad).astype(F32)
+            grad_middle = grad_out + grad_mixed
+            attn_gain_part = jnp.sum(grad_middle * branch_hat, axis=0)
+            grad_branch = norm_back(grad_middle * attn_gain, branch_hat, branch_inv, width)
+            grad_branch = grad_branch.astype(LOW)
+            pieces = [to_part(grad_branch, p) for p in range(1, parts)]
+            now = grad_branch
+    grad_branch_rows = jnp.concatenate([grad_branch, *[after(p, now) for p in pieces]], axis=0)
     grad_attended = nn(grad_branch_rows, full_out).astype(LOW)
-    out_grad = weight_grad(core_halves(grad_branch_rows), attended).T
+    sent, came = weight_grad_away(after(grad_branch_rows, grad_attended), [attended])
     (
         query_gained,
         key_gained,
@@ -438,41 +891,46 @@
         place_arr,
         (query_rot, key_rot),
         value_low,
-        grad_attended,
+        after(grad_attended, sent, gate_up_grad[spans - 1]),
         lse,
-        (query_pre, key_pre),
+        pre,
         invs,
         gains,
         tables,
     )
-    inners = sum_parts(jnp.concatenate([query_inner, key_inner], axis=1).T).T / width
-    grad_query = (
-        invs[0] * (query_gained - query_pre * invs[0] * inners[:, :1])
-    ).astype(LOW)
-    grad_key = (invs[1] * (key_gained - key_pre * invs[1] * inners[:, 1:])).astype(LOW)
-    input_grad = grad_middle + scatter_rows(
-        lambda part: nt(grad_query[part], full_query)
-        + nt(grad_key[part], full_key)
-        + nt(grad_value[part], full_value)
-    )
-    input_halves = core_halves(inputs)
-    value_grad = weight_grad(input_halves, grad_value)
-    query_grad = weight_grad(input_halves, grad_query)
-    key_grad = weight_grad(input_halves, grad_key)
-    gain_grads = lax.psum(
-        (gain_whole(query_gain_part), gain_whole(key_gain_part), attn_gain_part, ffn_gain_part),
-        ("fsdp", "tensor"),
-    )
+    total, out_grad = weight_grad_here(after(grad_branch_rows, grad_value), [attended], came)
+    inners = sum_parts(jnp.concatenate([query_inner, key_inner], axis=1)) / width
+    local_width = value_low.shape[1]
+    grad_query = invs[0] * (query_gained - pre[:, :local_width] * invs[0] * inners[:, :1])
+    grad_key = invs[1] * (key_gained - pre[:, local_width:] * invs[1] * inners[:, 1:])
+    grad_qkv = jnp.concatenate(
+        [grad_query.astype(LOW), grad_key.astype(LOW), grad_value], axis=1
+    )
+    sent, came = weight_grad_away(after(inputs, total, gate_up_grad[0]), [grad_qkv])
+    total, qkv_grad = weight_grad_here(after(inputs, sent), [grad_qkv], came)
+    pairs = [(after(grad_qkv, total), full_qkv, 0)]
+    input_grad = grad_middle + product_own(pairs, product_others(pairs))
+    gain_grads = sum_all(
+        jnp.stack(
+            [gain_whole(query_gain_part), gain_whole(key_gain_part), attn_gain_part, ffn_gain_part]
+        )
+    )
+    (down_grad,) = sum_spans(down_grad, 1)
+    gate_up_grad = gate_up_grad[0].astype(F32) + sum(
+        to_span(gate_up_grad[s], -s).astype(F32) for s in range(1, spans)
+    )
+    (out_grad,) = sum_spans(out_grad, 1)
+    query_grad, key_grad, value_grad = sum_spans(qkv_grad, 3)
     return (
         output,
         input_grad,
         query_grad,
         key_grad,
         value_grad,
-        out_grad,
-        gate_grad,
-        up_grad,
-        down_grad,
+        out_grad.T,
+        gate_up_grad[:, :cols],
+        gate_up_grad[:, cols:],
+        down_grad.T,
         *gain_grads,
     )
 

time: 1410 us -> 1260 us (0.89)
  Pallas kernels: 70.3 us -> 633 us
  matrix products: 363 us -> 7.1 us
  waiting for transfers between devices: 611 us -> 461 us
  local copies, waits for them, and re-layouts: 165 us -> 49.6 us
  blocking collectives: 71 us -> 0 us
  other arithmetic: 73.6 us -> 58.1 us
    pallas_call x0 -> x26, Pallas kernels: none -> 563 us  [the longest x3 216 us: exchange(): pl.pallas_call(functools.partial(exchange_kernel, fsdp, parts, spans, pla...]
    ppermute x14 -> x5, waiting for transfers between devices: 338 us -> 90.7 us  [to_span(): return lax.ppermute(x, 'tensor', pairs)]
    dot_general x28 -> x0, matrix products: 241 us -> none  [the longest x14 124 us: nt(): lax.dot_general(a, b, (((1,), (1,)), ((), ())), preferred_element_type=F32)]
    dot_general x7 -> x1, matrix products: 121 us -> 7.1 us  [nn(): lax.dot_general(a, b, (((1,), (0,)), ((), ())), preferred_element_type=F32)]
    ppermute x7 -> x10, waiting for transfers between devices: 22.5 us -> 96.6 us  [the longest x5 59.9 us: sum_all(): x = x + lax.ppermute(x, axis, [(i, i ^ bit) for i in range(size)])]
    psum x1 -> x0, blocking collectives: 71 us -> none  [layer(): lax.psum((gain_whole(query_gain_part), gain_whole(key_gain_part), attn_ga...]
    unnamed x147 -> x91, local copies, waits for them, and re-layouts: 82.1 us -> 27.7 us
    dynamic_slice x4 -> x0, local copies, waits for them, and re-layouts: 36.5 us -> none  [core_halves(): lax.dynamic_index_in_dim(split, which, 2, keepdims=False)]
  transfers between devices with their start and end apart: 45 -> 31, of which waited for: 23 -> 19; matrix products, arithmetic and copies ran while one was open for 30% -> 6% of each run, Pallas kernels for 5% -> 36%
where the time goes in v2:
time: 1260 us; the launch traced here: 1250 us
  Pallas kernels  633 us (50%)
  waiting for transfers between devices  461 us (37%)
  other arithmetic  58.1 us (5%)
  local copies, waits for them, and re-layouts  49.6 us (4%)
  starting transfers between devices  29 us (2%)
  between operations  15 us (1%)
    ppermute x9, waiting for transfers between devices, to_part(): return lax.ppermute(x, 'tensor', pairs)  273 us
    pallas_call x3, Pallas kernels, exchange(): pl.pallas_call(functools.partial(exchange_kernel, fsdp, parts, spans, pla...  216 us
    pallas_call x10, Pallas kernels, weight_grad_half(): pl.pallas_call(functools.partial(weight_grad_kernel, pieces, tiles, adden...  125 us
    pallas_call x8, Pallas kernels, product_sum(): pl.pallas_call(functools.partial(sum_kernel, len(pairs), addend is not No...  117 us
    ppermute x5, waiting for transfers between devices, to_span(): return lax.ppermute(x, 'tensor', pairs)  90.7 us
    ppermute x5, waiting for transfers between devices, sum_all(): x = x + lax.ppermute(x, axis, [(i, i ^ bit) for i in range(size)])  59.9 us
    pallas_call x2, Pallas kernels, feed_up(): pl.pallas_call(up_kernel, grid=(tiles,), in_specs=[pl.BlockSpec((rows, de...  47.9 us
    pallas_call x1, Pallas kernels, attend_back(): pl.pallas_call(functools.partial(attend_back_kernel, rows, parts, 1.0 / m...  41 us
  transfers between devices with their start and end apart: 31, of which 19 were waited for; matrix products, arithmetic and copies ran while one was open for 6% of the time, Pallas kernels for 36%

profile of v2, /device:TPU:0, one launch (start us, length us, event | category | flops | bytes accessed | tf_op | source)
XLA Modules:
  0.0 1252.6 jit_solution(8881698706799699530)
XLA Ops:
  12.1 105.2 %exchange.3 = (bf16[2,512,2048]{2,1,0:T(8,128)(2,1)}, bf16[8,256,3072]{2,1,0:T(8,128)(2,1)}, bf16[8,256,1024]{2,1,0:T(8,128)(2,1)}) custom-call(bf16[512,2048]{1,0:T(8,128)(2,1)} %refs_0_.1, bf16[256,512]{1,0:T(8,128)(2,1)} %refs_5_.1, bf16[256,512]{1,0:T(8,128)(2,1)} %refs_6_.1, bf16[256,512]{1,0:T(8,128)(2,1)} %refs_7_.1, bf16[256,512]{1,0:T(8,128)(2,1)} %bitcast.80, ...), custom_call_target="tpu_custom_call" | custom-call | tf_op jit(solution)/shard_map/exchange/pallas_call | solution.py:351
  117.5 19.5 %project.1 = (f32[1024,2048]{1,0:T(8,128)}, bf16[1024,1024]{1,0:T(8,128)(2,1)S(1)}, f32[1024,1]{1,0:T(8,128)S(1)}, f32[1024,1]{1,0:T(8,128)S(1)}) custom-call(bf16[1024,2048]{1,0:T(8,128)(2,1)} %bitcast.61, bf16[2048,3072]{1,0:T(8,128)(2,1)} %bitcast.96), custom_call_target="tpu_custom_call" | custom-call | flops 12884901888 | bytes 27262976 | tf_op jit(solution)/shard_map/project/pallas_call | solution.py:574
  143.7 20.1 %collective-permute-done = f32[1024,2]{0,1:T(2,128)S(1)} collective-permute-done((f32[1024,2]{0,1:T(2,128)S(1)}, f32[1024,2]{0,1:T(2,128)S(1)}, u32[]{:S(2)}, u32[]{:S(2)}) %collective-permute-start) | collective-permute-done | bytes 8224 | tf_op jit(solution)/shard_map/ppermute | solution.py:706
  167.0 29.3 %attend.1 = (bf16[1024,1024]{1,0:T(8,128)(2,1)S(1)}, bf16[1024,1024]{1,0:T(8,128)(2,1)S(1)}, bf16[1024,1024]{1,0:T(8,128)(2,1)S(1)}, f32[8,1024,1]{2,1,0:T(8,128)}) custom-call(s32[1]{0:T(128)} %bitcast.place_ref, f32[1024,2048]{1,0:T(8,128)} %get-tuple-element.63.query_ref.key_ref, f32[1024,2048]{1,0:T(8,128)} %get-tuple-element.63.query_ref.key_ref, ...), custom_call_target="tpu_custom_call" | custom-call | flops 8589934592 | bytes 16777216 | tf_op jit(solution)/shard_map/attend/pallas_call | solution.py:618
  225.3 40.5 %collective-permute-done.1.refs_2_ = bf16[512,2048]{1,0:T(8,128)(2,1)S(1)} collective-permute-done((bf16[512,2048]{1,0:T(8,128)(2,1)}, bf16[512,2048]{1,0:T(8,128)(2,1)S(1)}, u32[]{:S(2)}, u32[]{:S(2)}) %collective-permute-start.1) | collective-permute-done | bytes 2097184 | tf_op jit(solution)/shard_map/ppermute | solution.py:706
  273.7 65.9 %exchange.4 = (bf16[8,256,2048]{2,1,0:T(8,128)(2,1)}, bf16[1,256,2048]{2,1,0:T(8,128)(2,1)}) custom-call(bf16[256,2048]{1,0:T(8,128)(2,1)} %bitcast.73, bf16[256,2048]{1,0:T(8,128)(2,1)} %bitcast.74, bf16[512,2048]{1,0:T(8,128)(2,1)} %copy-done.30), custom_call_target="tpu_custom_call" | custom-call | tf_op jit(solution)/shard_map/exchange/pallas_call | solution.py:351
  339.6 45.4 %exchange.5 = bf16[8,256,2048]{2,1,0:T(8,128)(2,1)} custom-call(bf16[256,2048]{1,0:T(8,128)(2,1)} %bitcast.84, bf16[512,2048]{1,0:T(8,128)(2,1)} %fusion.6.refs_1_, bf16[2048,4096]{1,0:T(8,128)(2,1)} %all-gather.3.cloned.1.call-done.refs_2_.gate_weight_ref.up_weight_ref.refs_1_.refs_3_), custom_call_target="tpu_custom_call" | custom-call | tf_op jit(solution)/shard_map/exchange/pallas_call | solution.py:351
  389.8 24.0 %feed_up.2 = (f32[1024,2048]{1,0:T(8,128)}, f32[1024,2048]{1,0:T(8,128)}, bf16[1024,2048]{1,0:T(8,128)(2,1)S(1)}) custom-call(bf16[1024,2048]{1,0:T(8,128)(2,1)} %pad_maximum_fusion.1.mixed_ref.refs_0_.refs_1_.refs_2_.refs_3_, bf16[2048,4096]{1,0:T(8,128)(2,1)} %all-gather.3.cloned.1.call-done.refs_2_.gate_weight_ref.up_weight_ref.refs_1_.refs_3_, ...), custom_call_target="tpu_custom_call" | custom-call | flops 17179869184 | bytes 37748736 | tf_op jit(solution)/shard_map/feed_up/pallas_call | solution.py:419
  415.9 23.9 %feed_up.3 = (f32[1024,2048]{1,0:T(8,128)}, f32[1024,2048]{1,0:T(8,128)}, bf16[1024,2048]{1,0:T(8,128)(2,1)S(1)}) custom-call(bf16[1024,2048]{1,0:T(8,128)(2,1)} %pad_maximum_fusion.1.mixed_ref.refs_0_.refs_1_.refs_2_.refs_3_, bf16[2048,4096]{1,0:T(8,128)(2,1)} %all-gather.5.cloned.1.call-done.gate_weight_ref.up_weight_ref.refs_5_.refs_7_, ...), custom_call_target="tpu_custom_call" | custom-call | flops 17179869184 | bytes 37748736 | tf_op jit(solution)/shard_map/feed_up/pallas_call | solution.py:419
  441.7 13.8 %product_sum.11 = bf16[512,2048]{1,0:T(8,128)(2,1)} custom-call(bf16[1024,2048]{1,0:T(8,128)(2,1)} %copy-done.1, bf16[2048,2048]{1,0:T(8,128)(2,1)} %bitcast.99, bf16[1024,2048]{1,0:T(8,128)(2,1)} %copy-done.2, bf16[2048,2048]{1,0:T(8,128)(2,1)} %bitcast.75), custom_call_target="tpu_custom_call" | custom-call | flops 8589934592 | bytes 20971520 | tf_op jit(solution)/shard_map/product_sum/pallas_call | solution.py:391
  458.0 14.5 %product_sum.10 = f32[512,2048]{1,0:T(8,128)} custom-call(bf16[1024,2048]{1,0:T(8,128)(2,1)} %copy-done.1, bf16[2048,2048]{1,0:T(8,128)(2,1)} %bitcast.100, bf16[1024,2048]{1,0:T(8,128)(2,1)} %copy-done.2, bf16[2048,2048]{1,0:T(8,128)(2,1)} %bitcast.76), custom_call_target="tpu_custom_call" | custom-call | flops 8589934592 | bytes 20971520 | tf_op jit(solution)/shard_map/product_sum/pallas_call | solution.py:391
  472.5 31.9 %collective-permute-done.4 = bf16[512,2048]{1,0:T(8,128)(2,1)S(1)} collective-permute-done((bf16[512,2048]{1,0:T(8,128)(2,1)}, bf16[512,2048]{1,0:T(8,128)(2,1)S(1)}, u32[]{:S(2)}, u32[]{:S(2)}) %collective-permute-start.4) | collective-permute-done | bytes 2097184 | tf_op jit(solution)/shard_map/ppermute | solution.py:706
  514.9 45.8 %collective-permute-done.5 = bf16[512,2048]{1,0:T(8,128)(2,1)S(1)} collective-permute-done((bf16[512,2048]{1,0:T(8,128)(2,1)}, bf16[512,2048]{1,0:T(8,128)(2,1)S(1)}, u32[]{:S(2)}, u32[]{:S(2)}) %collective-permute-start.5) | collective-permute-done | bytes 2097184 | tf_op jit(solution)/shard_map/ppermute | solution.py:706
  564.9 14.2 %weight_grad.10 = bf16[1024,4096]{1,0:T(8,128)(2,1)} custom-call(s32[1]{0:T(128)S(6)} %sub.51.parity_ref, bf16[1024,2048]{1,0:T(8,128)(2,1)} %pad_maximum_fusion.2.refs_0_.refs_1_.refs_2_.refs_3_.grad_ref, bf16[1024,2048]{1,0:T(8,128)(2,1)} %pad_maximum_fusion.2.refs_0_.refs_1_.refs_2_.refs_3_.grad_ref, ...), custom_call_target="tpu_custom_call" | custom-call | flops 8589934592 | bytes 18874368 | tf_op jit(solution)/shard_map/weight_grad/pallas_call | solution.py:524
  579.0 18.4 %feed_up_back.2 = (bf16[1024,2048]{1,0:T(8,128)(2,1)}, bf16[1024,2048]{1,0:T(8,128)(2,1)}) custom-call(bf16[1024,2048]{1,0:T(8,128)(2,1)} %pad_maximum_fusion.2.refs_0_.refs_1_.refs_2_.refs_3_.grad_ref, bf16[2048,2048]{1,0:T(8,128)(2,1)} %bitcast.101, f32[1024,2048]{1,0:T(8,128)} %get-tuple-element.77.gate_ref, f32[1024,2048]{1,0:T(8,128)} %get-tuple-element.78.upper_ref), custom_call_target="tpu_custom_call" | custom-call | flops 8589934592 | bytes 33554432 | tf_op jit(solution)/shard_map/feed_up_back/pallas_call | solution.py:458
  600.8 15.3 %weight_grad.11 = bf16[1024,4096]{1,0:T(8,128)(2,1)} custom-call(s32[1]{0:T(128)} %bitcast.11.parity_ref, bf16[1024,2048]{1,0:T(8,128)(2,1)} %pad_maximum_fusion.2.refs_0_.refs_1_.refs_2_.refs_3_.grad_ref, bf16[1024,2048]{1,0:T(8,128)(2,1)} %pad_maximum_fusion.2.refs_0_.refs_1_.refs_2_.refs_3_.grad_ref, ...), custom_call_target="tpu_custom_call" | custom-call | flops 8589934592 | bytes 18874368 | tf_op jit(solution)/shard_map/weight_grad/pallas_call | solution.py:524
  616.2 19.0 %feed_up_back.3 = (bf16[1024,2048]{1,0:T(8,128)(2,1)}, bf16[1024,2048]{1,0:T(8,128)(2,1)}) custom-call(bf16[1024,2048]{1,0:T(8,128)(2,1)} %pad_maximum_fusion.2.refs_0_.refs_1_.refs_2_.refs_3_.grad_ref, bf16[2048,2048]{1,0:T(8,128)(2,1)} %bitcast.77, f32[1024,2048]{1,0:T(8,128)} %get-tuple-element.83.gate_ref, f32[1024,2048]{1,0:T(8,128)} %get-tuple-element.84.upper_ref), custom_call_target="tpu_custom_call" | custom-call | flops 8589934592 | bytes 33554432 | tf_op jit(solution)/shard_map/feed_up_back/pallas_call | solution.py:458
  635.1 26.5 %product_sum.12 = f32[512,2048]{1,0:T(8,128)} custom-call(bf16[1024,2048]{1,0:T(8,128)(2,1)} %get-tuple-element.79.refs_0_.refs_4_, bf16[2048,4096]{1,0:T(8,128)(2,1)} %all-gather.3.cloned.1.call-done.refs_2_.gate_weight_ref.up_weight_ref.refs_1_.refs_3_, bf16[1024,2048]{1,0:T(8,128)(2,1)} %get-tuple-element.80.refs_2_.refs_5_, ...), custom_call_target="tpu_custom_call" | custom-call | flops 17179869184 | bytes 37748736 | tf_op jit(solution)/shard_map/product_sum/pallas_call | solution.py:391
  661.6 14.3 %weight_grad.12 = bf16[1024,4096]{1,0:T(8,128)(2,1)} custom-call(s32[1]{0:T(128)S(6)} %sub.51.parity_ref, bf16[1024,2048]{1,0:T(8,128)(2,1)} %pad_maximum_fusion.1.mixed_ref.refs_0_.refs_1_.refs_2_.refs_3_, bf16[1024,2048]{1,0:T(8,128)(2,1)} %pad_maximum_fusion.1.mixed_ref.refs_0_.refs_1_.refs_2_.refs_3_, ...), custom_call_target="tpu_custom_call" | custom-call | flops 8589934592 | bytes 18874368 | tf_op jit(solution)/shard_map/weight_grad/pallas_call | solution.py:524
  676.4 13.0 %collective-permute-done.8.refs_6_ = bf16[1024,4096]{1,0:T(8,128)(2,1)S(1)} collective-permute-done((bf16[1024,4096]{1,0:T(8,128)(2,1)}, bf16[1024,4096]{1,0:T(8,128)(2,1)S(1)}, u32[]{:S(2)}, u32[]{:S(2)}) %collective-permute-start.8) | collective-permute-done | bytes 8388640 | tf_op jit(solution)/shard_map/ppermute | solution.py:752
  692.7 15.5 %weight_grad.13 = bf16[1024,4096]{1,0:T(8,128)(2,1)} custom-call(s32[1]{0:T(128)} %bitcast.11.parity_ref, bf16[1024,2048]{1,0:T(8,128)(2,1)} %pad_maximum_fusion.1.mixed_ref.refs_0_.refs_1_.refs_2_.refs_3_, bf16[1024,2048]{1,0:T(8,128)(2,1)} %pad_maximum_fusion.1.mixed_ref.refs_0_.refs_1_.refs_2_.refs_3_, ...), custom_call_target="tpu_custom_call" | custom-call | flops 8589934592 | bytes 18874368 | tf_op jit(solution)/shard_map/weight_grad/pallas_call | solution.py:524
  708.4 25.6 %product_sum.13 = bf16[512,2048]{1,0:T(8,128)(2,1)} custom-call(bf16[1024,2048]{1,0:T(8,128)(2,1)} %get-tuple-element.79.refs_0_.refs_4_, bf16[2048,4096]{1,0:T(8,128)(2,1)} %all-gather.3.cloned.1.call-done.refs_2_.gate_weight_ref.up_weight_ref.refs_1_.refs_3_, bf16[1024,2048]{1,0:T(8,128)(2,1)} %get-tuple-element.80.refs_2_.refs_5_, ...), custom_call_target="tpu_custom_call" | custom-call | flops 17179869184 | bytes 37748736 | tf_op jit(solution)/shard_map/product_sum/pallas_call | solution.py:391
  735.5 46.7 %collective-permute-done.7 = bf16[512,2048]{1,0:T(8,128)(2,1)} collective-permute-done((bf16[512,2048]{1,0:T(8,128)(2,1)}, bf16[512,2048]{1,0:T(8,128)(2,1)}, u32[]{:S(2)}, u32[]{:S(2)}) %collective-permute-start.7) | collective-permute-done | bytes 2097184 | tf_op jit(solution)/shard_map/ppermute | solution.py:706
  791.1 14.4 %weight_grad.14 = bf16[1024,4096]{1,0:T(8,128)(2,1)} custom-call(s32[1]{0:T(128)S(6)} %sub.51.parity_ref, bf16[1024,2048]{1,0:T(8,128)(2,1)} %pad_maximum_fusion.1.mixed_ref.refs_0_.refs_1_.refs_2_.refs_3_, bf16[1024,2048]{1,0:T(8,128)(2,1)} %pad_maximum_fusion.1.mixed_ref.refs_0_.refs_1_.refs_2_.refs_3_, ...), custom_call_target="tpu_custom_call" | custom-call | flops 8589934592 | bytes 18874368 | tf_op jit(solution)/shard_map/weight_grad/pallas_call | solution.py:524
  805.5 13.4 %collective-permute-done.10.refs_6_ = bf16[1024,4096]{1,0:T(8,128)(2,1)S(1)} collective-permute-done((bf16[1024,4096]{1,0:T(8,128)(2,1)}, bf16[1024,4096]{1,0:T(8,128)(2,1)S(1)}, u32[]{:S(2)}, u32[]{:S(2)}) %collective-permute-start.10) | collective-permute-done | bytes 8388640 | tf_op jit(solution)/shard_map/ppermute | solution.py:752
  822.1 15.3 %weight_grad.15 = bf16[1024,4096]{1,0:T(8,128)(2,1)} custom-call(s32[1]{0:T(128)} %bitcast.11.parity_ref, bf16[1024,2048]{1,0:T(8,128)(2,1)} %pad_maximum_fusion.1.mixed_ref.refs_0_.refs_1_.refs_2_.refs_3_, bf16[1024,2048]{1,0:T(8,128)(2,1)} %pad_maximum_fusion.1.mixed_ref.refs_0_.refs_1_.refs_2_.refs_3_, ...), custom_call_target="tpu_custom_call" | custom-call | flops 8589934592 | bytes 18874368 | tf_op jit(solution)/shard_map/weight_grad/pallas_call | solution.py:524
  839.1 46.2 %collective-permute-done.9 = bf16[512,2048]{1,0:T(8,128)(2,1)S(1)} collective-permute-done((bf16[512,2048]{1,0:T(8,128)(2,1)S(1)}, bf16[512,2048]{1,0:T(8,128)(2,1)S(1)}, u32[]{:S(2)}, u32[]{:S(2)}) %collective-permute-start.9) | collective-permute-done | bytes 2097184 | tf_op jit(solution)/shard_map/ppermute | solution.py:706
  903.1 41.0 %attend_back.1 = (f32[1024,1024]{1,0:T(8,128)}, f32[1024,1024]{1,0:T(8,128)}, bf16[1024,1024]{1,0:T(8,128)(2,1)S(1)}, f32[1,1024]{1,0:T(1,128)S(1)}, f32[1,1024]...) custom-call(s32[1]{0:T(128)} %bitcast.place_ref, bf16[1024,1024]{1,0:T(8,128)(2,1)} %copy-done.18, ...), custom_call_target="tpu_custom_call" | custom-call | flops 21474836480 | bytes 33554432 | tf_op jit(solution)/shard_map/attend_back/pallas_call | solution.py:648
  1035.6 65.8 %collective-permute-done.18 = bf16[256,1,2048]{0,2,1:T(8,128)(2,1)S(1)} collective-permute-done((bf16[256,1,2048]{0,2,1:T(8,128)(2,1)S(1)}, bf16[256,1,2048]{0,2,1:T(8,128)(2,1)S(1)}, u32[]{:S(2)}, u32[]{:S(2)}) %collective-permute-start.18) | collective-permute-done | bytes 1048608 | tf_op jit(solution)/shard_map/ppermute | solution.py:714
  1103.0 43.4 %collective-permute-done.23 = f32[4,2048]{1,0:T(4,128)S(1)} collective-permute-done((f32[4,2048]{1,0:T(4,128)S(1)}, f32[4,2048]{1,0:T(4,128)S(1)}, u32[]{:S(2)}, u32[]{:S(2)}) %collective-permute-start.23) | collective-permute-done | bytes 32800 | tf_op jit(solution)/shard_map/ppermute | solution.py:743
  1148.4 13.6 %collective-permute-done.16 = bf16[256,1,512]{0,2,1:T(8,128)(2,1)S(1)} collective-permute-done((bf16[256,1,512]{0,2,1:T(8,128)(2,1)S(1)}, bf16[256,1,512]{0,2,1:T(8,128)(2,1)S(1)}, u32[]{:S(2)}, u32[]{:S(2)}) %collective-permute-start.16) | collective-permute-done | bytes 262176 | tf_op jit(solution)/shard_map/ppermute | solution.py:714
  1199.0 40.0 %collective-permute-done.14 = bf16[512,2048]{1,0:T(8,128)(2,1)} collective-permute-done((bf16[512,2048]{1,0:T(8,128)(2,1)}, bf16[512,2048]{1,0:T(8,128)(2,1)}, u32[]{:S(2)}, u32[]{:S(2)}) %collective-permute-start.14) | collective-permute-done | bytes 2097184 | tf_op jit(solution)/shard_map/ppermute | solution.py:706
  (223 shorter events, 256.7 us)
Async XLA Ops:
  7.2 332.5 %all-gather.3.cloned.1.call-start = ((), (), s32[]{:S(2)}) async-start(), calls=%async_computation.5 | async-start | bytes 18874368 | tf_op jit(solution)/shard_map/all_gather | solution.py:717
  117.3 298.6 %all-gather.5.cloned.1.call-start = ((), (), s32[]{:S(2)}) async-start(), calls=%async_computation.6 | async-start | bytes 18874368 | tf_op jit(solution)/shard_map/all_gather | solution.py:717
  117.4 94.3 %collective-permute-start.3 = (bf16[256,4096]{1,0:T(8,128)(2,1)}, bf16[256,4096]{1,0:T(8,128)(2,1)}, u32[]{:S(2)}, u32[]{:S(2)}) collective-permute-start(bf16[256,4096]{1,0:T(8,128)(2,1)} %pad_maximum_fusion.4), channel_id=1, source_target_pairs={{0,2},{1,3},{2,0},{3,1},{4,6},{5,7},{6,4},{7,5},{8,10},{9,11},{10,... | collective-permute-start | bytes 6291464 | tf_op jit(solution)/shard_map/ppermute | solution.py:714
  137.4 26.4 %collective-permute-start = (f32[1024,2]{0,1:T(2,128)S(1)}, f32[1024,2]{0,1:T(2,128)S(1)}, u32[]{:S(2)}, u32[]{:S(2)}) collective-permute-start(f32[1024,2]{0,1:T(2,128)S(1)} %pad_maximum_fusion.8), channel_id=1, source_target_pairs={{0,1},{1,0},{2,3},{3,2},{4,5},{5,4},{6,7},{7,6},{8,9},{9,8},{10,11... | collective-permute-start | bytes 24584 | tf_op jit(solution)/shard_map/ppermute | solution.py:706
  211.7 570.5 %reduce-scatter.6.cloned.1.call-start = ((), (), s32[]{:S(2)}) async-start(), calls=%async_computation.7 | async-start | bytes 10485760 | tf_op jit(solution)/shard_map/reduce_scatter | solution.py:756
  218.4 47.4 %collective-permute-start.1 = (bf16[512,2048]{1,0:T(8,128)(2,1)}, bf16[512,2048]{1,0:T(8,128)(2,1)S(1)}, u32[]{:S(2)}, u32[]{:S(2)}) collective-permute-start(bf16[512,2048]{1,0:T(8,128)(2,1)} %product_sum.9), channel_id=1, source_target_pairs={{0,1},{1,0},{2,3},{3,2},{4,5},{5,4},{6,7},{7,6},{8,9},{9,8},{10,11... | collective-permute-start | bytes 6291464 | tf_op jit(solution)/shard_map/ppermute | solution.py:706
  272.0 113.0 %collective-permute-start.2 = (bf16[512,2048]{1,0:T(8,128)(2,1)}, bf16[512,2048]{1,0:T(8,128)(2,1)}, u32[]{:S(2)}, u32[]{:S(2)}) collective-permute-start(bf16[512,2048]{1,0:T(8,128)(2,1)} %fusion.6.refs_1_), channel_id=1, source_target_pairs={{0,1},{1,0},{2,3},{3,2},{4,5},{5,4},{6,7},{7,6},{8,9},{9,8},{10,11... | collective-permute-start | bytes 6291464 | tf_op jit(solution)/shard_map/ppermute | solution.py:706
  455.5 48.8 %collective-permute-start.4 = (bf16[512,2048]{1,0:T(8,128)(2,1)}, bf16[512,2048]{1,0:T(8,128)(2,1)S(1)}, u32[]{:S(2)}, u32[]{:S(2)}) collective-permute-start(bf16[512,2048]{1,0:T(8,128)(2,1)} %product_sum.11), channel_id=1, source_target_pairs={{0,1},{1,0},{2,3},{3,2},{4,5},{5,4},{6,7},{7,6},{8,9},{9,8},{10,11... | collective-permute-start | bytes 6291464 | tf_op jit(solution)/shard_map/ppermute | solution.py:706
  513.2 47.6 %collective-permute-start.5 = (bf16[512,2048]{1,0:T(8,128)(2,1)}, bf16[512,2048]{1,0:T(8,128)(2,1)S(1)}, u32[]{:S(2)}, u32[]{:S(2)}) collective-permute-start(bf16[512,2048]{1,0:T(8,128)(2,1)} %get-tuple-element.122), channel_id=1, source_target_pairs={{0,1},{1,0},{2,3},{3,2},{4,5},{5,4},{6,7},{7,6},{8,9},{9,8},{10,11... | collective-permute-start | bytes 6291464 | tf_op jit(solution)/shard_map/ppermute | solution.py:706
  579.0 18.4 %collective-permute-start.6 = (bf16[1024,4096]{1,0:T(8,128)(2,1)}, bf16[1024,4096]{1,0:T(8,128)(2,1)S(1)}, u32[]{:S(2)}, u32[]{:S(2)}) collective-permute-start(bf16[1024,4096]{1,0:T(8,128)(2,1)} %weight_grad.10), channel_id=1, source_target_pairs={{0,4},{4,0},{8,12},{12,8},{16,20},{20,16},{24,28},{28,24},{1,5},{5... | collective-permute-start | bytes 25165832 | tf_op jit(solution)/shard_map/ppermute | solution.py:752
  616.1 284.8 %reduce-scatter.8.cloned.1.call-start = ((), (), s32[]{:S(2)}) async-start(), calls=%async_computation.8 | async-start | bytes 10485760 | tf_op jit(solution)/shard_map/reduce_scatter | solution.py:756
  675.9 13.5 %collective-permute-start.8 = (bf16[1024,4096]{1,0:T(8,128)(2,1)}, bf16[1024,4096]{1,0:T(8,128)(2,1)S(1)}, u32[]{:S(2)}, u32[]{:S(2)}) collective-permute-start(bf16[1024,4096]{1,0:T(8,128)(2,1)} %weight_grad.12), channel_id=1, source_target_pairs={{0,4},{4,0},{8,12},{12,8},{16,20},{20,16},{24,28},{28,24},{1,5},{5... | collective-permute-start | bytes 25165832 | tf_op jit(solution)/shard_map/ppermute | solution.py:752
  708.2 74.0 %copy-start.28 = (bf16[512,2048]{1,0:T(8,128)(2,1)S(1)}, bf16[512,2048]{1,0:T(8,128)(2,1)}, u32[]{:S(2)}) copy-start(bf16[512,2048]{1,0:T(8,128)(2,1)} %param.25) | copy-start | bytes 6291460
  708.2 260.6 %reduce-scatter.10.cloned.1.call-start = ((), (), s32[]{:S(2)}) async-start(), calls=%async_computation.9 | async-start | bytes 10485760 | tf_op jit(solution)/shard_map/reduce_scatter | solution.py:756
  734.0 48.2 %collective-permute-start.7 = (bf16[512,2048]{1,0:T(8,128)(2,1)}, bf16[512,2048]{1,0:T(8,128)(2,1)}, u32[]{:S(2)}, u32[]{:S(2)}) collective-permute-start(bf16[512,2048]{1,0:T(8,128)(2,1)} %product_sum.13), channel_id=1, source_target_pairs={{0,1},{1,0},{2,3},{3,2},{4,5},{5,4},{6,7},{7,6},{8,9},{9,8},{10,11... | collective-permute-start | bytes 6291464 | tf_op jit(solution)/shard_map/ppermute | solution.py:706
  805.5 13.4 %collective-permute-start.10 = (bf16[1024,4096]{1,0:T(8,128)(2,1)}, bf16[1024,4096]{1,0:T(8,128)(2,1)S(1)}, u32[]{:S(2)}, u32[]{:S(2)}) collective-permute-start(bf16[1024,4096]{1,0:T(8,128)(2,1)} %weight_grad.14), channel_id=1, source_target_pairs={{0,4},{4,0},{8,12},{12,8},{16,20},{20,16},{24,28},{28,24},{1,5},{5... | collective-permute-start | bytes 25165832 | tf_op jit(solution)/shard_map/ppermute | solution.py:752
  837.5 309.0 %reduce-scatter.14.cloned.1.call-start = ((), (), s32[]{:S(2)}) async-start(), calls=%async_computation.11 | async-start | bytes 2621440 | tf_op jit(solution)/shard_map/reduce_scatter | solution.py:756
  837.5 47.7 %collective-permute-start.9 = (bf16[512,2048]{1,0:T(8,128)(2,1)S(1)}, bf16[512,2048]{1,0:T(8,128)(2,1)S(1)}, u32[]{:S(2)}, u32[]{:S(2)}) collective-permute-start(bf16[512,2048]{1,0:T(8,128)(2,1)S(1)} %multiply_convert_fusion.2), channel_id=1, source_target_pairs={{0,1},{1,0},{2,3},{3,2},{4,5},{5,4},{6,7},{7,6},{8,9},{9,8},{10,11... | collective-permute-start | bytes 6291464 | tf_op jit(solution)/shard_map/ppermute | solution.py:706
  900.9 61.3 %collective-permute-start.12 = (bf16[1024,1024]{1,0:T(8,128)(2,1)}, bf16[1024,1024]{1,0:T(8,128)(2,1)}, u32[]{:S(2)}, u32[]{:S(2)}) collective-permute-start(bf16[1024,1024]{1,0:T(8,128)(2,1)} %weight_grad.16), channel_id=1, source_target_pairs={{0,4},{4,0},{8,12},{12,8},{16,20},{20,16},{24,28},{28,24},{1,5},{5... | collective-permute-start | bytes 6291464 | tf_op jit(solution)/shard_map/ppermute | solution.py:752
  948.1 3.7 collective-permute-start.11
  980.1 10.5 collective-permute-start.13
  980.1 210.5 %reduce-scatter.12.cloned.1.call-start = ((), (), s32[]{:S(2)}) async-start(), calls=%async_computation.10 | async-start | bytes 7864320 | tf_op jit(solution)/shard_map/reduce_scatter | solution.py:756
  1006.3 95.1 %collective-permute-start.18 = (bf16[256,1,2048]{0,2,1:T(8,128)(2,1)S(1)}, bf16[256,1,2048]{0,2,1:T(8,128)(2,1)S(1)}, u32[]{:S(2)}, u32[]{:S(2)}) collective-permute-start(bf16[256,1,2048]{0,2,1:T(8,128)(2,1)S(1)} %slice_bitcast_fusion), channel_id=1, source_target_pairs={{0,2},{1,3},{2,0},{3,1},{4,6},{5,7},{6,4},{7,5},{8,10},{9,11},{10,... | collective-permute-start | bytes 3145736 | tf_op jit(solution)/shard_map/ppermute | solution.py:714
  1009.1 1.3 collective-permute-start.19
  1010.4 6.0 collective-permute-start.20
  1016.5 4.0 collective-permute-start.21
  1020.5 12.7 %collective-permute-start.22 = (f32[4,2048]{1,0:T(4,128)S(1)}, f32[4,2048]{1,0:T(4,128)S(1)}, u32[]{:S(2)}, u32[]{:S(2)}) collective-permute-start(f32[4,2048]{1,0:T(4,128)S(1)} %add.212), channel_id=1, source_target_pairs={{0,1},{1,0},{2,3},{3,2},{4,5},{5,4},{6,7},{7,6},{8,9},{9,8},{10,11... | collective-permute-start | bytes 98312 | tf_op jit(solution)/shard_map/ppermute | solution.py:743
  1021.4 153.0 %collective-permute-start.17 = (bf16[256,4096]{1,0:T(8,128)(2,1)}, bf16[256,4096]{1,0:T(8,128)(2,1)}, u32[]{:S(2)}, u32[]{:S(2)}) collective-permute-start(bf16[256,4096]{1,0:T(8,128)(2,1)} %reduce-scatter.8.cloned.1.call-done), channel_id=1, source_target_pairs={{0,2},{1,3},{2,0},{3,1},{4,6},{5,7},{6,4},{7,5},{8,10},{9,11},{10,... | collective-permute-start | bytes 6291464 | tf_op jit(solution)/shard_map/ppermute | solution.py:714
  1033.3 113.1 %collective-permute-start.23 = (f32[4,2048]{1,0:T(4,128)S(1)}, f32[4,2048]{1,0:T(4,128)S(1)}, u32[]{:S(2)}, u32[]{:S(2)}) collective-permute-start(f32[4,2048]{1,0:T(4,128)S(1)} %add.213), channel_id=1, source_target_pairs={{0,2},{1,3},{2,0},{3,1},{4,6},{5,7},{6,4},{7,5},{8,10},{9,11},{10,... | collective-permute-start | bytes 98312 | tf_op jit(solution)/shard_map/ppermute | solution.py:743
  1147.7 14.3 %collective-permute-start.16 = (bf16[256,1,512]{0,2,1:T(8,128)(2,1)S(1)}, bf16[256,1,512]{0,2,1:T(8,128)(2,1)S(1)}, u32[]{:S(2)}, u32[]{:S(2)}) collective-permute-start(bf16[256,1,512]{0,2,1:T(8,128)(2,1)S(1)} %slice_bitcast_fusion.5), channel_id=1, source_target_pairs={{0,2},{1,3},{2,0},{3,1},{4,6},{5,7},{6,4},{7,5},{8,10},{9,11},{10,... | collective-permute-start | bytes 786440 | tf_op jit(solution)/shard_map/ppermute | solution.py:714
  1174.4 64.6 %collective-permute-start.14 = (bf16[512,2048]{1,0:T(8,128)(2,1)}, bf16[512,2048]{1,0:T(8,128)(2,1)}, u32[]{:S(2)}, u32[]{:S(2)}) collective-permute-start(bf16[512,2048]{1,0:T(8,128)(2,1)} %product_sum.15), channel_id=1, source_target_pairs={{0,1},{1,0},{2,3},{3,2},{4,5},{5,4},{6,7},{7,6},{8,9},{9,8},{10,11... | collective-permute-start | bytes 6291464 | tf_op jit(solution)/shard_map/ppermute | solution.py:706
  1197.2 46.9 %collective-permute-start.15 = (bf16[256,3,512]{2,0,1:T(8,128)(2,1)S(1)}, bf16[256,3,512]{2,0,1:T(8,128)(2,1)S(1)}, u32[]{:S(2)}, u32[]{:S(2)}) collective-permute-start(bf16[256,3,512]{2,0,1:T(8,128)(2,1)S(1)} %bitcast.85), channel_id=1, source_target_pairs={{0,2},{1,3},{2,0},{3,1},{4,6},{5,7},{6,4},{7,5},{8,10},{9,11},{10,... | collective-permute-start | bytes 2359304 | tf_op jit(solution)/shard_map/ppermute | solution.py:714
  (43 other events, 878.6 us)
Sparse Core Ops, SparseCore 0:
  117.5 89.8 all-gather.2
  211.8 106.5 all-gather.4
  616.3 87.3 reduce-scatter.5
  708.3 87.1 reduce-scatter.7
  837.6 87.6 reduce-scatter.9
  980.3 37.2 reduce-scatter.13
  1020.5 70.3 reduce-scatter.11

commit v3 on v2

v3 whole, which is shorter than its diff:
```python
import functools
import math

import jax
import jax.numpy as jnp
from jax import lax
from jax.experimental import pallas as pl
from jax.experimental.pallas import tpu as pltpu
from jax.sharding import PartitionSpec as P

HEAD_DIM = 128
SEQ_LEN = 1024
EPSILON = 1e-06
THETA = 500000.0
BLOCK = 256
LOW = jnp.bfloat16
F32 = jnp.float32


def nn(a, b):
    return lax.dot_general(a, b, (((1,), (0,)), ((), ())), preferred_element_type=F32)


def nt(a, b):
    return lax.dot_general(a, b, (((1,), (1,)), ((), ())), preferred_element_type=F32)


def tn(a, b):
    return lax.dot_general(a, b, (((0,), (0,)), ((), ())), preferred_element_type=F32)


def after(x, *earlier):
    return lax.optimization_barrier((x, *earlier))[0]


def block_start(place, block, rows, parts):
    part = block * BLOCK // rows
    return pl.multiple_of(
        lax.rem(place + parts - part, parts) * rows + block * BLOCK % rows, BLOCK
    )


def masked(scores):
    row = lax.broadcasted_iota(jnp.int32, scores.shape, 0)
    col = lax.broadcasted_iota(jnp.int32, scores.shape, 1)
    return jnp.where(row + (scores.shape[1] - scores.shape[0]) >= col, scores, -1e30)


def attend_kernel(rows, parts, scale, heads, sides, *refs):
    query_ref, key_ref, value_ref, query_inv_ref, key_inv_ref = refs[:5]
    query_gain_ref, key_gain_ref, cos_ref, sin_ref = refs[5:9]
    side_refs, refs = refs[9 : 9 + len(sides.operands)], refs[9 + len(sides.operands) :]
    out_ref, query_rot_ref, key_rot_ref, lse_ref = refs[:4]
    side_outs, refs = refs[4 : 4 + len(sides.out_shapes)], refs[4 + len(sides.out_shapes) :]
    key_seq, value_seq = refs[:2]
    sides_at = (side_refs, side_outs, refs[2:])
    place = lax.rem(lax.axis_index("tensor"), parts)

    @pl.when(pl.program_id(0) == 0)
    def _():
        greet(sides.partners())
        sides.start(*sides_at)
        sides.start_rest(*sides_at)

    half = HEAD_DIM // 2
    for block in range(SEQ_LEN // BLOCK):
        here = pl.ds(block_start(place, block, rows, parts), BLOCK)
        there = pl.ds(block * BLOCK, BLOCK)
        cos, sin = cos_ref[here], sin_ref[here]
        key = key_ref[here] * key_inv_ref[here] * key_gain_ref[...]
        key = (key * cos + pltpu.roll(key, half, 1) * sin).astype(LOW)
        key_rot_ref[here] = key
        key_seq[there] = key
        value_seq[there] = value_ref[here]
        query = query_ref[here] * query_inv_ref[here] * query_gain_ref[...]
        query = (query * cos + pltpu.roll(query, half, 1) * sin).astype(LOW)
        query_rot_ref[here] = query
        span = (block + 1) * BLOCK
        scores = masked(nt(query, key_seq[:span]) * scale)
        top = jnp.max(scores, axis=1, keepdims=True)
        exps = jnp.exp(scores - top)
        total = jnp.sum(exps, axis=1, keepdims=True)
        weights = (exps * (1.0 / total)).astype(LOW)
        out_ref[here] = nn(weights, value_seq[:span]).astype(LOW)
        lse_ref[here] = top + jnp.log(total)

    @pl.when(pl.program_id(0) == heads - 1)
    def _():
        sides.finish(*sides_at)


def attend_back_kernel(rows, parts, scale, heads, sides, *refs):
    query_rot_ref, key_rot_ref, value_ref, grad_ref, lse_ref, query_ref, key_ref = refs[:7]
    query_inv_ref, key_inv_ref, query_gain_ref, key_gain_ref, cos_ref, sin_ref = refs[7:13]
    side_refs, refs = refs[13 : 13 + len(sides.operands)], refs[13 + len(sides.operands) :]
    query_out_ref, key_out_ref, value_out_ref = refs[:3]
    query_gain_out_ref, key_gain_out_ref, query_inner_ref, key_inner_ref = refs[3:7]
    side_outs, refs = refs[7 : 7 + len(sides.out_shapes)], refs[7 + len(sides.out_shapes) :]
    key_seq, value_seq, key_acc, value_acc = refs[:4]
    sides_at = (side_refs, side_outs, refs[4:])
    place = lax.rem(lax.axis_index("tensor"), parts)
    half = HEAD_DIM // 2
    count = SEQ_LEN // BLOCK

    @pl.when(pl.program_id(0) == 0)
    def _():
        greet(sides.partners())
        sides.start(*sides_at)
        sides.start_rest(*sides_at)
        query_inner_ref[...] = jnp.zeros_like(query_inner_ref)
        key_inner_ref[...] = jnp.zeros_like(key_inner_ref)

    def finish(grad, here, values_ref, inv_ref, gain_ref, out_ref, inner_ref):
        back = grad * cos_ref[here] - pltpu.roll(grad, half, 1) * sin_ref[here]
        hat = values_ref[here] * inv_ref[here]
        gained = back * gain_ref[...]
        out_ref[here] = gained
        inner_ref[here] += jnp.sum(gained * hat, axis=1, keepdims=True)
        return jnp.sum(back * hat, axis=0, keepdims=True)

    query_gain_sum = jnp.zeros((1, HEAD_DIM), F32)
    for block in range(count):
        here = pl.ds(block_start(place, block, rows, parts), BLOCK)
        there = pl.ds(block * BLOCK, BLOCK)
        key_seq[there] = key_rot_ref[here]
        value_seq[there] = value_ref[here]
        query, grad = query_rot_ref[here], grad_ref[here]
        span = (block + 1) * BLOCK
        scores = masked(nt(query, key_seq[:span]) * scale)
        probs = jnp.exp(scores - lse_ref[here])
        weights = probs.astype(LOW)
        grad_probs = nt(grad, value_seq[:span])
        delta = jnp.sum(probs * grad_probs, axis=1, keepdims=True)
        grad_scores = (probs * (grad_probs - delta) * scale).astype(LOW)
        value_part = tn(weights, grad)
        key_part = tn(grad_scores, query)
        past = block * BLOCK
        if block:
            key_acc[:past] += key_part[:past]
            value_acc[:past] += value_part[:past]
        key_acc[past:span] = key_part[past:]
        value_acc[past:span] = value_part[past:]
        query_gain_sum += finish(
            nn(grad_scores, key_seq[:span]),
            here,
            query_ref,
            query_inv_ref,
            query_gain_ref,
            query_out_ref,
            query_inner_ref,
        )
    query_gain_out_ref[...] = query_gain_sum
    key_gain_sum = jnp.zeros((1, HEAD_DIM), F32)
    for block in range(count):
        here = pl.ds(block_start(place, block, rows, parts), BLOCK)
        there = pl.ds(block * BLOCK, BLOCK)
        value_out_ref[here] = value_acc[there].astype(LOW)
        key_gain_sum += finish(
            key_acc[there],
            here,
            key_ref,
            key_inv_ref,
            key_gain_ref,
            key_out_ref,
            key_inner_ref,
        )
    key_gain_out_ref[...] = key_gain_sum

    @pl.when(pl.program_id(0) == heads - 1)
    def _():
        sides.finish(*sides_at)


MESH = pl.DeviceIdType.MESH
MIB = 2**20


def flip(index, bit):
    return index + bit - 2 * bit * lax.rem(lax.div(index, bit), 2)


def row_shares(rows, count):
    units = rows // 16
    sizes = [16 * (units // count + (i < units % count)) for i in range(count)]
    starts = [sum(sizes[:i]) for i in range(count)]
    return list(zip(starts, sizes))


def call(kernel, operands, in_specs, earlier=(), **options):
    count = len(operands)

    def body(*refs):
        kernel(*refs[:count], *refs[count + len(earlier) :])

    specs = [*in_specs, *[pl.BlockSpec(memory_space=pl.ANY)] * len(earlier)]
    return pl.pallas_call(body, in_specs=specs, **options)(*operands, *earlier)


def greet(partners):
    barrier = pltpu.get_barrier_semaphore()
    for partner in partners:
        pl.semaphore_signal(barrier, inc=1, device_id=partner, device_id_type=MESH)
    pl.semaphore_wait(barrier, len(partners))


def remote(src, dst, send_sem, recv_sem, **device):
    return pltpu.make_async_remote_copy(
        src_ref=src,
        dst_ref=dst,
        send_sem=send_sem,
        recv_sem=recv_sem,
        device_id=device,
        device_id_type=MESH,
    )


class Copies:
    def __init__(self, send_sems, recv_sems):
        self.send_sems, self.recv_sems = send_sems, recv_sems
        self.used = 0
        self.open = []
        self.moves = []

    def send(self, src, dst, **device):
        copy = remote(
            src, dst, self.send_sems.at[self.used], self.recv_sems.at[self.used], **device
        )
        self.used += 1
        copy.start()
        self.open.append(copy.wait_send)
        return copy

    def move(self, src, hold, dst):
        load = pltpu.make_async_copy(src, hold, self.send_sems.at[self.used])
        store = pltpu.make_async_copy(hold, dst, self.recv_sems.at[self.used])
        self.used += 1
        load.start()
        self.moves.append((load, store))

    def finish(self):
        for load, store in self.moves:
            load.wait()
            store.start()
        for wait in self.open:
            wait()
        for _, store in self.moves:
            store.wait()


class Rows:
    def __init__(self, parts, gather=None, deliver=None):
        self.parts, self.gather = parts, gather is not None
        self.half = (gather if self.gather else deliver[0]).shape[0] // 2
        self.operands = [gather] if self.gather else list(deliver)
        first = self.operands[0]
        count = parts if self.gather else parts - 1
        self.out_shapes = [jax.ShapeDtypeStruct((count, *first.shape), LOW)]
        count = 2 * parts
        self.scratch = [pltpu.SemaphoreType.DMA((count,)), pltpu.SemaphoreType.DMA((count,))]
        if self.gather:
            self.scratch.append(pltpu.VMEM(first.shape, LOW))

    def ranks(self):
        rank = lax.axis_index("tensor")
        place = lax.rem(rank, self.parts)
        shifts = range(1, self.parts)
        if not self.gather:
            shifts = [self.parts - p for p in shifts]
        return [rank - place + lax.rem(place + p, self.parts) for p in shifts]

    def partners(self):
        return [{"tensor": rank} for rank in self.ranks()]

    def copies(self, halves, refs, outs, send_sems, recv_sems, hold=None):
        made = []
        for half in halves:
            rows = pl.ds(half * self.half, self.half)
            for i, rank in enumerate(self.ranks()):
                src = refs[0] if self.gather else refs[i]
                dst = outs[0].at[i + 1] if self.gather else outs[0].at[i]
                sem = 2 * i + half
                made.append(
                    remote(
                        src.at[rows], dst.at[rows], send_sems.at[sem], recv_sems.at[sem], tensor=rank
                    )
                )
        return made

    def load(self, refs, outs, send_sems, recv_sems, hold):
        return pltpu.make_async_copy(refs[0], hold, send_sems.at[2 * self.parts - 1])

    def store(self, refs, outs, send_sems, recv_sems, hold):
        return pltpu.make_async_copy(hold, outs[0].at[0], recv_sems.at[2 * self.parts - 1])

    def start(self, *where):
        for copy in self.copies([0], *where):
            copy.start()
        if self.gather:
            self.load(*where).start()

    def start_rest(self, *where):
        for copy in self.copies([1], *where):
            copy.start()

    def finish(self, *where):
        if self.gather:
            self.load(*where).wait()
            self.store(*where).start()
            self.store(*where).wait()
        for copy in self.copies([0, 1], *where):
            copy.wait()

    def results(self, outs):
        out = outs[0]
        if self.gather:
            return out.reshape(-1, out.shape[2])
        return [out[i] for i in range(self.parts - 1)]


class Spans:
    def __init__(self, parts, spans, terms):
        self.parts, self.spans, self.terms = parts, spans, terms
        self.operands = [array for array, *_ in terms]
        self.out_shapes = [
            jax.ShapeDtypeStruct((array.shape[0], width), LOW) for array, _, width, _ in terms
        ]
        count = max(1, len(terms))
        self.scratch = [pltpu.SemaphoreType.DMA((count,)), pltpu.SemaphoreType.DMA((count,))]

    def rank(self, back):
        rank = lax.axis_index("tensor")
        place, span = lax.rem(rank, self.parts), lax.div(rank, self.parts)
        return lax.rem(span + self.spans - back, self.spans) * self.parts + place

    def partners(self):
        return [{"tensor": self.rank(s)} for s in range(1, self.spans)]

    def copies(self, refs, outs, send_sems, recv_sems):
        return [
            remote(
                ref.at[:, pl.ds(run * width, width)],
                out,
                send_sems.at[i],
                recv_sems.at[i],
                tensor=self.rank(back),
            )
            for i, (ref, out, (_, run, width, back)) in enumerate(zip(refs, outs, self.terms))
        ]

    def start(self, *where):
        for copy in self.copies(*where):
            copy.start()

    def start_rest(self, *where):
        pass

    def finish(self, *where):
        for copy in self.copies(*where):
            copy.wait()

    def results(self, outs):
        return list(outs)


class Sides:
    def __init__(self, *jobs):
        self.jobs = jobs
        self.operands = [x for job in jobs for x in job.operands]
        self.out_shapes = [x for job in jobs for x in job.out_shapes]
        self.scratch = [x for job in jobs for x in job.scratch]

    def partners(self):
        return [partner for job in self.jobs for partner in job.partners()]

    def each(self, refs, outs, scratch):
        for job in self.jobs:
            counts = len(job.operands), len(job.out_shapes), len(job.scratch)
            yield job, (refs[: counts[0]], outs[: counts[1]], *scratch[: counts[2]])
            refs, outs, scratch = refs[counts[0] :], outs[counts[1] :], scratch[counts[2] :]

    def start(self, *where):
        for job, own in self.each(*where):
            job.start(*own)

    def start_rest(self, *where):
        for job, own in self.each(*where):
            job.start_rest(*own)

    def finish(self, *where):
        for job, own in self.each(*where):
            job.finish(*own)

    def results(self, outs):
        return [job.results(own) for job, (_, own, *_) in self.each([], outs, [])]

    def options(self, number):
        return {"collective_id": number, "has_side_effects": True} if self.jobs else {}


NO_SIDES = Sides()


def exchange_kernel(fsdp, parts, spans, plan, counts, *refs):
    sides, shard_count, send_count, full_count = counts
    rows_count = len(sides.operands)
    rows_refs, refs = refs[:rows_count], refs[rows_count:]
    shard_refs, refs = refs[:shard_count], refs[shard_count:]
    span_refs, refs = refs[:send_count], refs[send_count:]
    full_refs, refs = refs[:full_count], refs[full_count:]
    span_outs, refs = refs[:send_count], refs[send_count:]
    side_outs, refs = refs[: len(sides.out_shapes)], refs[len(sides.out_shapes) :]
    hold_refs, refs = refs[: len(plan)], refs[len(plan) :]
    sides_at = (rows_refs, side_outs, refs[:-2])
    copies = Copies(*refs[-2:])
    me, rank = lax.axis_index("fsdp"), lax.axis_index("tensor")
    place, span = lax.rem(rank, parts), lax.div(rank, parts)
    bits = [1 << b for b in range(1, fsdp.bit_length() - 1)]
    span_ranks = [lax.rem(span + s, spans) * parts + place for s in range(1, spans)]
    partners = [{"fsdp": flip(me, bit)} for bit in [1, *bits]] if plan else []
    partners += sides.partners()
    if send_count or any(s and not here for _, s, _, here in plan):
        partners += [{"tensor": r} for r in span_ranks]
    greet(partners)

    def slot(job, mask, share=None):
        group, s, position, _ = plan[job]
        which = me
        for bit in [1, *bits]:
            if mask & bit:
                which = flip(which, bit)
        cols = shard_refs[job].shape[1]
        ref = full_refs[group].at[which, :, pl.ds(position * cols, cols)]
        return ref if share is None else ref.at[pl.ds(*share)]

    depth = shard_refs[0].shape[0] if plan else 16
    shares = row_shares(depth, len(bits))
    jobs = range(len(plan))
    away = [s and not here for _, s, _, here in plan]
    sides.start(*sides_at)
    from_span = {
        job: copies.send(shard_refs[job], slot(job, 0), tensor=span_ranks[plan[job][1] - 1])
        for job in jobs
        if away[job]
    }
    sides.start_rest(*sides_at)
    over = []
    for ref, out in zip(span_refs, span_outs):
        for s, r in enumerate(span_ranks):
            over.append(copies.send(ref, out.at[s], tensor=r))
    for job in jobs:
        if not away[job]:
            copies.move(shard_refs[job], hold_refs[job], slot(job, 0))

    arriving = {}
    held = {(job, p): [0] for job in jobs for p in range(len(shares))}

    def source(job, mask, share):
        if mask == 0 and not away[job]:
            return shard_refs[job].at[pl.ds(*share)]
        return slot(job, mask, share)

    def send_step(job, step):
        for p, share in enumerate(shares):
            bit = bits[(p + step) % len(bits)]
            for mask in held[job, p]:
                arriving[job, p, mask | bit] = copies.send(
                    source(job, mask, share), slot(job, mask, share), fsdp=flip(me, bit)
                )

    def take_step(job, step):
        for p in range(len(shares)):
            bit = bits[(p + step) % len(bits)]
            came = [mask | bit for mask in held[job, p]]
            for mask in came:
                arriving[job, p, mask].wait_recv()
            held[job, p] += came

    for step in range(len(bits) + 1):
        for job in jobs:
            if step == 0 and away[job]:
                from_span[job].wait_recv()
            if step:
                take_step(job, step - 1)
            if step < len(bits):
                send_step(job, step)
            else:
                for mask in range(0, fsdp, 2):
                    whole = (0, depth)
                    over.append(
                        copies.send(
                            source(job, mask, whole), slot(job, mask), fsdp=flip(me, 1)
                        )
                    )
    for copy in over:
        copy.wait_recv()
    copies.finish()
    sides.finish(*sides_at)


def exchange(number, fsdp, parts, spans, shards=(), plan=(), sides=NO_SIDES, sends=(), earlier=()):
    bits = fsdp.bit_length() - 2
    per_job = 2 + bits * (2**bits - 1) + 2**bits
    count = len(plan) * per_job + len(sends) * spans + 1
    hbm = pl.BlockSpec(memory_space=pl.ANY)
    full_count = 1 + max([group for group, *_ in plan], default=-1)
    widths = [0] * full_count
    for shard, (group, *_) in zip(shards, plan):
        widths[group] += shard.shape[1]
    depth = shards[0].shape[0] if plan else 0
    outs = [jax.ShapeDtypeStruct((fsdp, depth, width), LOW) for width in widths]
    outs += [jax.ShapeDtypeStruct((spans - 1, *x.shape), LOW) for x in sends]
    inputs = [*shards, *sends]
    scratch = [pltpu.SemaphoreType.DMA((count,)), pltpu.SemaphoreType.DMA((count,))]
    inputs = [*sides.operands, *inputs]
    outs += sides.out_shapes
    scratch = [*sides.scratch, *scratch]
    scratch = [
        *[pltpu.VMEM(x.shape if here or not s else (16, 128), LOW) for x, (_, s, _, here) in zip(shards, plan)],
        *scratch,
    ]
    results = call(
        functools.partial(
            exchange_kernel,
            fsdp,
            parts,
            spans,
            plan,
            (sides, len(shards), len(sends), full_count),
        ),
        inputs,
        [hbm] * len(inputs),
        earlier,
        out_shape=outs,
        out_specs=[hbm] * len(outs),
        scratch_shapes=scratch,
        compiler_params=pltpu.CompilerParams(collective_id=number, has_side_effects=True),
        name="exchange",
    )
    full = [r.reshape(fsdp * depth, -1) for r in results[:full_count]]
    came = results[full_count : full_count + len(sends)]
    return full, came, *sides.results(results[full_count + len(sends) :])


def sum_kernel(pairs, sides, steps, *refs):
    step = pl.program_id(0)
    count = 2 * pairs + len(sides.operands)
    out_ref, outs = refs[count], refs[count + 1 : count + 1 + len(sides.out_shapes)]
    sides_at = (refs[2 * pairs : count], outs, refs[count + 1 + len(sides.out_shapes) :])
    if sides.jobs:

        @pl.when(step == 0)
        def _():
            greet(sides.partners())
            sides.start(*sides_at)
            sides.start_rest(*sides_at)

    total = None
    for i in range(pairs):
        term = nt(refs[2 * i][...], refs[2 * i + 1][...])
        total = term if total is None else total + term
    out_ref[...] = total.astype(out_ref.dtype)
    if sides.jobs:

        @pl.when(step == steps - 1)
        def _():
            sides.finish(*sides_at)


def product_sum(count, block, pairs, kind, earlier=(), number=None, sides=NO_SIDES):
    width = pairs[0][1].shape[0]
    tile = min(512, width)
    specs, operands, flops = [], [], 0
    for a, b, run in pairs:
        depth = a.shape[1]
        specs.append(pl.BlockSpec((count, depth), lambda j: (block, 0)))
        specs.append(pl.BlockSpec((tile, depth), lambda j, run=run: (j, run)))
        operands += [a, b]
        flops += 2 * count * depth * width
    hbm = pl.BlockSpec(memory_space=pl.ANY)
    outs = [jax.ShapeDtypeStruct((count, width), kind)]
    out_specs = [pl.BlockSpec((count, tile), lambda j: (0, j))]
    operands += sides.operands
    specs += [hbm] * len(sides.operands)
    outs += sides.out_shapes
    out_specs += [hbm] * len(sides.out_shapes)
    steps = width // tile
    results = call(
        functools.partial(sum_kernel, len(pairs), sides, steps),
        operands,
        specs,
        earlier,
        grid=(steps,),
        out_specs=out_specs,
        out_shape=outs,
        scratch_shapes=sides.scratch,
        compiler_params=pltpu.CompilerParams(
            vmem_limit_bytes=56 * MIB, **sides.options(number)
        ),
        cost_estimate=pl.CostEstimate(
            flops=flops, bytes_accessed=flops // count + 4 * count * width, transcendentals=0
        ),
        name="product_sum",
    )
    return results[0], *sides.results(results[1:])


def up_kernel(mixed_ref, gate_weight_ref, up_weight_ref, gate_ref, upper_ref, hidden_ref):
    gate = nn(mixed_ref[...], gate_weight_ref[...])
    upper = nn(mixed_ref[...], up_weight_ref[...])
    gate_ref[...] = gate
    upper_ref[...] = upper
    hidden_ref[...] = (gate * jax.nn.sigmoid(gate) * upper).astype(LOW)


def feed_up(mixed, gate_up, cols, earlier=()):
    rows, depth = mixed.shape
    (gate_weight, gate_run), (up_weight, up_run) = gate_up
    tile = min(256, cols)
    tiles = cols // tile
    out = pl.BlockSpec((rows, tile), lambda j: (0, j))
    return call(
        up_kernel,
        [mixed, gate_weight, up_weight],
        [
            pl.BlockSpec((rows, depth), lambda j: (0, 0)),
            pl.BlockSpec((depth, tile), lambda j: (0, j + gate_run * tiles)),
            pl.BlockSpec((depth, tile), lambda j: (0, j + up_run * tiles)),
        ],
        earlier,
        grid=(tiles,),
        out_specs=[out, out, out],
        out_shape=[
            jax.ShapeDtypeStruct((rows, cols), F32),
            jax.ShapeDtypeStruct((rows, cols), F32),
            jax.ShapeDtypeStruct((rows, cols), LOW),
        ],
        compiler_params=pltpu.CompilerParams(vmem_limit_bytes=48 * MIB),
        cost_estimate=pl.CostEstimate(
            flops=4 * rows * depth * cols,
            bytes_accessed=4 * depth * cols + 10 * rows * cols,
            transcendentals=rows * cols,
        ),
        name="feed_up",
    )


def up_back_kernel(grad_ref, down_ref, gate_ref, upper_ref, gate_out_ref, up_out_ref):
    grad = nn(grad_ref[...], down_ref[...])
    gate = gate_ref[...]
    sigmoid = jax.nn.sigmoid(gate)
    scaled = grad * sigmoid
    up_out_ref[...] = (scaled * gate).astype(LOW)
    gate_out_ref[...] = (scaled * upper_ref[...] * (1.0 + gate * (1.0 - sigmoid))).astype(LOW)


def feed_up_back(grad_rows, down, gate, upper, earlier=()):
    rows, depth = grad_rows.shape
    cols = down.shape[1]
    tile = min(512, cols)
    spec = pl.BlockSpec((rows, tile), lambda j: (0, j))
    out = jax.ShapeDtypeStruct((rows, cols), LOW)
    return call(
        up_back_kernel,
        [grad_rows, down, gate, upper],
        [
            pl.BlockSpec((rows, depth), lambda j: (0, 0)),
            pl.BlockSpec((depth, tile), lambda j: (0, j)),
            spec,
            spec,
        ],
        earlier,
        grid=(cols // tile,),
        out_specs=[spec, spec],
        out_shape=[out, out],
        compiler_params=pltpu.CompilerParams(vmem_limit_bytes=52 * MIB),
        cost_estimate=pl.CostEstimate(
            flops=2 * rows * depth * cols,
            bytes_accessed=2 * depth * cols + 12 * rows * cols,
            transcendentals=rows * cols,
        ),
        name="feed_up_back",
    )


def weight_grad_kernel(fsdp, tiles, sides, *refs):
    x_ref, grad_refs, refs = refs[0], refs[1 : 1 + len(tiles)], refs[1 + len(tiles) :]
    count, outs = len(sides.operands), len(sides.out_shapes)
    side_refs, out_ref, refs = refs[:count], refs[count], refs[count + 1 :]
    side_outs, refs = refs[:outs], refs[outs:]
    x_half, sent, came, send_sems, recv_sems = refs[:5]
    sides_at = (side_refs, side_outs, refs[5:])
    me = lax.axis_index("fsdp")
    core = lax.rem(me, 2)
    total_tiles = sum(tiles)
    depth = x_ref.shape[1] // fsdp
    step = pl.program_id(0)

    def load(which):
        for i in range(fsdp // 2):
            first = pl.multiple_of((2 * i + which) * depth, depth)
            x_half[:, i * depth : (i + 1) * depth] = x_ref[:, pl.ds(first, depth)]

    def copy(tile):
        slot = lax.rem(tile, 2)
        return remote(
            sent.at[slot], came.at[tile], send_sems.at[slot], recv_sems.at[tile], fsdp=flip(me, 1)
        )

    @pl.when(step == 0)
    def _():
        load(1 - core)
        greet([{"fsdp": flip(me, 1)}, *sides.partners()])
        sides.start(*sides_at)
        sides.start_rest(*sides_at)

    @pl.when(step == total_tiles)
    def _():
        load(core)

    @pl.when(jnp.logical_and(step >= 2, step < total_tiles))
    def _():
        copy(step - 2).wait_send()

    tile = lax.rem(step, total_tiles)
    first = 0
    for ref, count in zip(grad_refs, tiles):
        here = jnp.logical_and(tile >= first, tile < first + count)

        @pl.when(jnp.logical_and(here, step < total_tiles))
        def _(ref=ref):
            sent[lax.rem(step, 2)] = tn(x_half[...], ref[...]).astype(LOW)

        @pl.when(jnp.logical_and(here, step >= total_tiles))
        def _(ref=ref):
            total = tn(x_half[...], ref[...])
            copy(tile).wait_recv()
            out_ref[...] = (total + came[tile].astype(F32)).astype(LOW)

        first += count

    @pl.when(step < total_tiles)
    def _():
        copy(step).start()

    @pl.when(step == 2 * total_tiles - 1)
    def _():
        for last in range(max(0, total_tiles - 2), total_tiles):
            copy(last).wait_send()
        sides.finish(*sides_at)


def weight_grad_half(number, fsdp, x, grads, earlier=(), sides=NO_SIDES):
    count, width = x.shape
    tile = math.gcd(1024, *[g.shape[1] for g in grads])
    tiles = [g.shape[1] // tile for g in grads]
    total_tiles = sum(tiles)
    firsts = [sum(tiles[:i]) for i in range(len(tiles))]
    cols = tile * total_tiles

    def grad_spec(first, runs):
        return pl.BlockSpec(
            (count, tile),
            lambda j: (0, jnp.clip(lax.rem(j, total_tiles) - first, 0, runs - 1)),
        )

    hbm = pl.BlockSpec(memory_space=pl.ANY)
    operands = [x, *grads]
    specs = [pl.BlockSpec((count, width), lambda j: (0, 0))]
    specs += [grad_spec(f, c) for f, c in zip(firsts, tiles)]
    outs = [jax.ShapeDtypeStruct((width // 2, cols), LOW)]
    out_specs = [pl.BlockSpec((width // 2, tile), lambda j: (0, jnp.maximum(j - total_tiles, 0)))]
    scratch = [
        pltpu.VMEM((count, width // 2), LOW),
        pltpu.VMEM((2, width // 2, tile), LOW),
        pltpu.VMEM((total_tiles, width // 2, tile), LOW),
        pltpu.SemaphoreType.DMA((2,)),
        pltpu.SemaphoreType.DMA((total_tiles,)),
    ]
    operands += sides.operands
    specs += [hbm] * len(sides.operands)
    outs += sides.out_shapes
    out_specs += [hbm] * len(sides.out_shapes)
    scratch += sides.scratch
    results = call(
        functools.partial(weight_grad_kernel, fsdp, tiles, sides),
        operands,
        specs,
        earlier,
        grid=(2 * total_tiles,),
        out_specs=out_specs,
        out_shape=outs,
        scratch_shapes=scratch,
        compiler_params=pltpu.CompilerParams(
            collective_id=number, has_side_effects=True, vmem_limit_bytes=56 * MIB
        ),
        cost_estimate=pl.CostEstimate(
            flops=2 * count * width * cols,
            bytes_accessed=2 * count * width + 4 * count * cols + width * cols,
            transcendentals=0,
        ),
        name="weight_grad",
    )
    return results[0], *sides.results(results[1:])


def column_shares(cols, count):
    return [(8 * start, 8 * size) for start, size in row_shares(cols // 8, count)]


def grad_scatter_kernel(fsdp, parts, spans, tiles, sides, *refs):
    x_ref, grad_ref, refs = refs[0], refs[1], refs[2:]
    count, outs = len(sides.operands), len(sides.out_shapes)
    side_refs, out_ref, refs = refs[:count], refs[count], refs[count + 1 :]
    side_outs, refs = refs[:outs], refs[outs:]
    x_half, sent, held, send_sems, recv_sems, chip_sends, chip_recvs = refs[:7]
    span_came, span_sends, span_recvs, refs = *refs[7:10], refs[10:]
    bits = [1 << b for b in range(fsdp.bit_length() - 2)]
    turns = len(bits)
    chip_came, side_scratch = refs[: turns * turns], refs[turns * turns :]
    sides_at = (side_refs, side_outs, side_scratch)
    me, rank = lax.axis_index("fsdp"), lax.axis_index("tensor")
    core, chip = lax.rem(me, 2), lax.div(me, 2)
    place, span = lax.rem(rank, parts), lax.div(rank, parts)
    depth = x_ref.shape[1] // fsdp
    tile_cols = grad_ref.shape[1]
    own_cols = tile_cols // spans
    shares = column_shares(tile_cols, turns)
    step = pl.program_id(0)

    def load(which):
        for i in range(fsdp // 2):
            first = pl.multiple_of((2 * i + which) * depth, depth)
            x_half[:, i * depth : (i + 1) * depth] = x_ref[:, pl.ds(first, depth)]

    def core_copy(tile):
        slot = lax.rem(tile, 2)
        return remote(
            sent.at[slot], held.at[tile], send_sems.at[slot], recv_sems.at[tile], fsdp=flip(me, 1)
        )

    def turned(mask):
        which = chip
        for bit in bits:
            if mask & bit:
                which = flip(which, bit)
        return pl.ds(pl.multiple_of(which * depth, depth), depth)

    def swaps(share, turn):
        order = [bits[(share + i) % turns] for i in range(turns)]
        stay = [0]
        for bit in order[turn + 1 :]:
            stay += [mask | bit for mask in stay]
        return order[turn], [(mask | order[turn], mask, i) for i, mask in enumerate(stay)]

    def chip_copies(tile, turn):
        made, number = [], 0
        for share, (start, size) in enumerate(shares):
            for earlier in range(turns):
                bit, moves = swaps(share, earlier)
                for goes, _, slot in moves:
                    if earlier == turn:
                        made.append(
                            remote(
                                held.at[tile, turned(goes), pl.ds(start, size)],
                                chip_came[share * turns + turn].at[tile, slot],
                                chip_sends.at[tile, number],
                                chip_recvs.at[tile, number],
                                fsdp=flip(me, 2 * bit),
                            )
                        )
                    number += 1
        return made

    def span_copies(tile):
        return [
            remote(
                held.at[tile, turned(0), pl.ds(s * own_cols, own_cols)],
                span_came.at[tile, s - 1],
                span_sends.at[tile, s - 1],
                span_recvs.at[tile, s - 1],
                tensor=lax.rem(span + spans - s, spans) * parts + place,
            )
            for s in range(1, spans)
        ]

    @pl.when(step == 0)
    def _():
        load(1 - core)
        partners = [{"fsdp": flip(me, 1)}] + [{"fsdp": flip(me, 2 * bit)} for bit in bits]
        partners += [
            {"tensor": lax.rem(span + s, spans) * parts + place} for s in range(1, spans)
        ]
        side_partners = sides.partners()
        greet(partners + side_partners)
        sides.start(*sides_at)
        sides.start_rest(*sides_at)

    @pl.when(step == tiles)
    def _():
        load(core)

    @pl.when(step < tiles)
    def _():
        @pl.when(step >= 2)
        def _():
            core_copy(step - 2).wait_send()

        sent[lax.rem(step, 2)] = tn(x_half[...], grad_ref[...]).astype(LOW)
        core_copy(step).start()

    @pl.when(jnp.logical_and(step >= tiles, step < 2 * tiles))
    def _():
        tile = step - tiles
        total = tn(x_half[...], grad_ref[...])
        core_copy(tile).wait_recv()
        held[tile] = (total + held[tile].astype(F32)).astype(LOW)
        for copy in chip_copies(tile, 0):
            copy.start()

    for turn in range(1, turns + 2):
        tile = step - tiles - turn

        @pl.when(jnp.logical_and(tile >= 0, tile < tiles))
        def _(turn=turn, tile=tile):
            if turn <= turns:
                for copy in chip_copies(tile, turn - 1):
                    copy.wait()
                for share, (start, size) in enumerate(shares):
                    _, moves = swaps(share, turn - 1)
                    for _, stays, slot in moves:
                        where = (tile, turned(stays), pl.ds(start, size))
                        came = chip_came[share * turns + turn - 1][tile, slot]
                        held[where] = (held[where].astype(F32) + came.astype(F32)).astype(LOW)
                for copy in chip_copies(tile, turn) if turn < turns else span_copies(tile):
                    copy.start()
            else:
                total = held[tile, turned(0), :own_cols].astype(F32)
                for s, copy in enumerate(span_copies(tile)):
                    copy.wait()
                    total = total + span_came[tile, s].astype(F32)
                out_ref[...] = total

    @pl.when(step == 2 * tiles + turns)
    def _():
        for last in range(max(0, tiles - 2), tiles):
            core_copy(last).wait_send()
        sides.finish(*sides_at)


def grad_scatter(number, fsdp, parts, spans, x, grads, tiles, earlier=(), sides=NO_SIDES):
    count, width = x.shape
    depth = width // fsdp
    tile = grads.shape[1] // tiles
    own = tile // spans
    turns = fsdp.bit_length() - 2
    shares = column_shares(tile, turns)
    hbm = pl.BlockSpec(memory_space=pl.ANY)
    swapped = turns * (2**turns - 1)
    results = call(
        functools.partial(grad_scatter_kernel, fsdp, parts, spans, tiles, sides),
        [x, grads, *sides.operands],
        [
            pl.BlockSpec((count, width), lambda j: (0, 0)),
            pl.BlockSpec(
                (count, tile),
                lambda j: (0, jnp.where(j < tiles, j, jnp.minimum(j - tiles, tiles - 1))),
            ),
            *[hbm] * len(sides.operands),
        ],
        earlier,
        grid=(2 * tiles + turns + 1,),
        out_specs=[
            pl.BlockSpec((depth, own), lambda j: (0, jnp.maximum(j - (tiles + turns + 1), 0))),
            *[hbm] * len(sides.out_shapes),
        ],
        out_shape=[jax.ShapeDtypeStruct((depth, own * tiles), F32), *sides.out_shapes],
        scratch_shapes=[
            pltpu.VMEM((count, width // 2), LOW),
            pltpu.VMEM((2, width // 2, tile), LOW),
            pltpu.VMEM((tiles, width // 2, tile), LOW),
            pltpu.SemaphoreType.DMA((2,)),
            pltpu.SemaphoreType.DMA((tiles,)),
            pltpu.SemaphoreType.DMA((tiles, swapped)),
            pltpu.SemaphoreType.DMA((tiles, swapped)),
            pltpu.VMEM((tiles, spans - 1, depth, own), LOW),
            pltpu.SemaphoreType.DMA((tiles, spans - 1)),
            pltpu.SemaphoreType.DMA((tiles, spans - 1)),
            *[
                pltpu.VMEM((tiles, 2 ** (turns - 1 - turn), depth, size), LOW)
                for _, size in shares
                for turn in range(turns)
            ],
            *sides.scratch,
        ],
        compiler_params=pltpu.CompilerParams(
            collective_id=number, has_side_effects=True, vmem_limit_bytes=56 * MIB
        ),
        cost_estimate=pl.CostEstimate(
            flops=2 * count * width * tile * tiles,
            bytes_accessed=2 * count * width + 4 * count * tile * tiles,
            transcendentals=0,
        ),
        name="grad_scatter",
    )
    return results[0], *sides.results(results[1:])


def project_kernel(tiles, rows_ref, weight_ref, pre_ref, value_ref, query_sq_ref, key_sq_ref):
    step = pl.program_id(0)
    result = nn(rows_ref[...], weight_ref[...])
    squares = jnp.sum(result * result, axis=1, keepdims=True)

    @pl.when(step < 2 * tiles)
    def _():
        pre_ref[...] = result

    for first, ref in ((0, query_sq_ref), (tiles, key_sq_ref)):

        @pl.when(step == first)
        def _(ref=ref):
            ref[...] = squares

        @pl.when(jnp.logical_and(step > first, step < first + tiles))
        def _(ref=ref):
            ref[...] += squares

    @pl.when(step >= 2 * tiles)
    def _():
        value_ref[...] = result.astype(LOW)


def project(inputs, full):
    rows, depth = inputs.shape
    cols = full.shape[1] // 3
    tile = min(512, cols)
    tiles = cols // tile
    column = pl.BlockSpec((rows, 1), lambda j: (0, 0))
    return pl.pallas_call(
        functools.partial(project_kernel, tiles),
        grid=(3 * tiles,),
        in_specs=[
            pl.BlockSpec((rows, depth), lambda j: (0, 0)),
            pl.BlockSpec((depth, tile), lambda j: (0, j)),
        ],
        out_specs=[
            pl.BlockSpec((rows, tile), lambda j: (0, jnp.minimum(j, 2 * tiles - 1))),
            pl.BlockSpec((rows, tile), lambda j: (0, jnp.maximum(j - 2 * tiles, 0))),
            column,
            column,
        ],
        out_shape=[
            jax.ShapeDtypeStruct((rows, 2 * cols), F32),
            jax.ShapeDtypeStruct((rows, cols), LOW),
            jax.ShapeDtypeStruct((rows, 1), F32),
            jax.ShapeDtypeStruct((rows, 1), F32),
        ],
        compiler_params=pltpu.CompilerParams(vmem_limit_bytes=48 * MIB),
        cost_estimate=pl.CostEstimate(
            flops=6 * rows * depth * cols,
            bytes_accessed=6 * depth * cols + 10 * rows * cols + 2 * rows * depth,
            transcendentals=0,
        ),
        name="project",
    )(inputs, full)


def attention_specs(heads):
    return (
        pl.BlockSpec((SEQ_LEN, HEAD_DIM), lambda i: (0, i)),
        pl.BlockSpec((SEQ_LEN, HEAD_DIM), lambda i: (0, i + heads)),
        pl.BlockSpec((SEQ_LEN, HEAD_DIM), lambda i: (0, 0)),
        pl.BlockSpec((SEQ_LEN, 1), lambda i: (0, 0)),
        pl.BlockSpec((1, HEAD_DIM), lambda i: (0, i)),
        pl.BlockSpec((None, SEQ_LEN, 1), lambda i: (i, 0, 0)),
        pl.BlockSpec(memory_space=pl.ANY),
    )


def attend(number, rows, parts, pre, value, invs, gains, tables, sides):
    width = value.shape[1]
    heads = width // HEAD_DIM
    head, later, whole, column, gain, lse, hbm = attention_specs(heads)
    low = jax.ShapeDtypeStruct((SEQ_LEN, width), LOW)
    results = call(
        functools.partial(attend_kernel, rows, parts, 1.0 / math.sqrt(HEAD_DIM), heads, sides),
        [pre, pre, value, *invs, *gains, *tables, *sides.operands],
        [head, later, head, column, column, gain, gain, whole, whole]
        + [hbm] * len(sides.operands),
        grid=(heads,),
        out_specs=[head, head, head, lse, *[hbm] * len(sides.out_shapes)],
        out_shape=[
            low,
            low,
            low,
            jax.ShapeDtypeStruct((heads, SEQ_LEN, 1), F32),
            *sides.out_shapes,
        ],
        scratch_shapes=[
            pltpu.VMEM((SEQ_LEN, HEAD_DIM), LOW),
            pltpu.VMEM((SEQ_LEN, HEAD_DIM), LOW),
            *sides.scratch,
        ],
        compiler_params=pltpu.CompilerParams(
            vmem_limit_bytes=40 * MIB, **sides.options(number)
        ),
        cost_estimate=pl.CostEstimate(
            flops=8 * heads * SEQ_LEN * SEQ_LEN * HEAD_DIM,
            bytes_accessed=16 * SEQ_LEN * width,
            transcendentals=heads * SEQ_LEN * SEQ_LEN,
        ),
        name="attend",
    )
    return *results[:4], *sides.results(results[4:])


def attend_back(
    number, rows, parts, rots, value, grad, lse_all, pre, invs, gains, tables, earlier, sides
):
    width = value.shape[1]
    heads = width // HEAD_DIM
    head, later, whole, column, gain, lse, hbm = attention_specs(heads)
    full = jax.ShapeDtypeStruct((SEQ_LEN, width), F32)
    low = jax.ShapeDtypeStruct((SEQ_LEN, width), LOW)
    gain_out = jax.ShapeDtypeStruct((1, width), F32)
    inner = jax.ShapeDtypeStruct((SEQ_LEN, 1), F32)
    results = call(
        functools.partial(
            attend_back_kernel, rows, parts, 1.0 / math.sqrt(HEAD_DIM), heads, sides
        ),
        [*rots, value, grad, lse_all, pre, pre, *invs, *gains, *tables, *sides.operands],
        [head, head, head, head, lse, head, later, column, column, gain, gain, whole, whole]
        + [hbm] * len(sides.operands),
        earlier,
        grid=(heads,),
        out_specs=[head, head, head, gain, gain, column, column, *[hbm] * len(sides.out_shapes)],
        out_shape=[full, full, low, gain_out, gain_out, inner, inner, *sides.out_shapes],
        scratch_shapes=[
            pltpu.VMEM((SEQ_LEN, HEAD_DIM), LOW),
            pltpu.VMEM((SEQ_LEN, HEAD_DIM), LOW),
            pltpu.VMEM((SEQ_LEN, HEAD_DIM), F32),
            pltpu.VMEM((SEQ_LEN, HEAD_DIM), F32),
            *sides.scratch,
        ],
        compiler_params=pltpu.CompilerParams(
            vmem_limit_bytes=48 * MIB, **sides.options(number)
        ),
        cost_estimate=pl.CostEstimate(
            flops=20 * heads * SEQ_LEN * SEQ_LEN * HEAD_DIM,
            bytes_accessed=32 * SEQ_LEN * width,
            transcendentals=heads * SEQ_LEN * SEQ_LEN,
        ),
        name="attend_back",
    )
    return *results[:7], *sides.results(results[7:])


def norm_back(grad_hat, values_hat, inverse, width):
    inner = jnp.sum(grad_hat * values_hat, axis=1, keepdims=True) / width
    return inverse * (grad_hat - values_hat * inner)


def layer(fsdp, tensor, *arguments):
    layer_input, query_weight, key_weight, value_weight, out_weight = arguments[:5]
    gate_weight, up_weight, down_weight = arguments[5:8]
    query_gain, key_gain, attn_gain, ffn_gain, out_cotangent = arguments[8:]
    rows_here, width = layer_input.shape
    head_cols = query_weight.shape[1]
    parts = SEQ_LEN // rows_here
    spans = tensor // parts
    rank = lax.axis_index("tensor")
    place, span = rank % parts, rank // parts

    def to_part(x, shift):
        pairs = [
            (s * parts + p, s * parts + (p + shift) % parts)
            for s in range(spans)
            for p in range(parts)
        ]
        return lax.ppermute(x, "tensor", pairs)

    def to_span(x, shift):
        pairs = [
            (s * parts + p, (s + shift) % spans * parts + p)
            for s in range(spans)
            for p in range(parts)
        ]
        return lax.ppermute(x, "tensor", pairs)

    def gather_shard(shard):
        return lax.all_gather(shard, "fsdp", axis=0, tiled=True)

    def product_others(pairs, earlier=()):
        return [product_sum(rows_here, p, pairs, LOW, earlier)[0] for p in range(1, parts)]

    def product_own(number, pairs, others, earlier=()):
        sides = Sides(Rows(parts, deliver=others))
        total, came = product_sum(rows_here, 0, pairs, F32, earlier, number, sides)
        return add_pieces(total, came)

    def add_pieces(total, came):
        for piece in came:
            total = total + piece.astype(F32)
        return total

    def sum_parts(x):
        total = x
        for p in range(1, parts):
            total = total + jnp.roll(to_part(x, p), p * rows_here, axis=0)
        return total

    def sum_all(x):
        for axis, size in (("fsdp", fsdp), ("tensor", tensor)):
            bit = 1
            while bit < size:
                x = x + lax.ppermute(x, axis, [(i, i ^ bit) for i in range(size)])
                bit *= 2
        return x

    same_core = [list(range(c, fsdp, 2)) for c in range(2)]

    def scatter(total):
        return lax.psum_scatter(
            total, "fsdp", scatter_dimension=0, tiled=True, axis_index_groups=same_core
        )

    def sum_spans(total, weights):
        split = total.reshape(total.shape[0], weights, spans, -1)
        result = split[:, :, 0].astype(F32)
        for s in range(1, spans):
            result = result + to_span(split[:, :, s], -s).astype(F32)
        return [result[:, w] for w in range(weights)]

    def own_columns(s):
        return ((span + spans - s) % spans * parts + place) * head_cols

    def gain_here(gain):
        return jnp.concatenate(
            [lax.dynamic_slice_in_dim(gain, own_columns(s), head_cols) for s in range(spans)]
        )[None, :]

    def gain_whole(part):
        whole = jnp.zeros((width,), F32)
        for s in range(spans):
            whole = lax.dynamic_update_slice_in_dim(
                whole, part[0, s * head_cols : (s + 1) * head_cols], own_columns(s), 0
            )
        return whole

    gate_up_shard = jnp.concatenate([gate_weight, up_weight], axis=1)
    down_shard = down_weight.T
    out_shard = out_weight.T
    cols = gate_weight.shape[1]
    shards, plan = [], []
    for s in range(spans):
        for w, shard in enumerate([query_weight, key_weight, value_weight, out_shard]):
            shards.append(shard)
            plan.append((w // 3, s, w % 3 * spans + s, False))
    (full_qkv, full_out), _, inputs = exchange(
        0,
        fsdp,
        parts,
        spans,
        shards,
        plan,
        sides=Sides(Rows(parts, gather=layer_input)),
    )
    gate_up_first = gather_shard(after(gate_up_shard, inputs))

    local = jnp.arange(SEQ_LEN)
    position = (place + parts - local // rows_here) % parts * rows_here + local % rows_here
    inverse = THETA ** (-jnp.arange(0, HEAD_DIM, 2).astype(F32) / HEAD_DIM)
    angles = position.astype(F32)[:, None] * inverse[None, :]
    cos, sin = jnp.cos(angles), jnp.sin(angles)
    tables = (jnp.concatenate([cos, cos], axis=1), jnp.concatenate([-sin, sin], axis=1))
    gains = (gain_here(query_gain), gain_here(key_gain))

    pre, value_low, query_sq, key_sq = project(inputs, full_qkv)
    squares = sum_parts(jnp.concatenate([query_sq, key_sq], axis=1))
    invs = lax.rsqrt(squares / width + EPSILON)
    invs = (invs[:, :1], invs[:, 1:])
    others_spans = range(1, spans)
    sides = Sides(Spans(parts, spans, [(gate_up_shard, 0, cols, spans - s) for s in others_spans]))
    attended, query_rot, key_rot, lse, gate_came = attend(
        13, rows_here, parts, pre, value_low, invs, gains, tables, sides
    )
    pairs = [(attended, full_out, 0)]
    others = product_others(pairs)
    sides = Sides(
        Rows(parts, deliver=others),
        Spans(parts, spans, [(gate_up_shard, 1, cols, spans - s) for s in others_spans]),
    )
    full_gate, _, came, up_came = exchange(
        1, fsdp, parts, spans, gate_came, [(s - 1, s, 0, True) for s in others_spans], sides
    )
    came, down_shard = lax.optimization_barrier((came, down_shard))
    full_down = [gather_shard(down_shard)]
    total = product_sum(rows_here, 0, pairs, F32, [*others, gate_up_first])[0]
    branch = add_pieces(total, came)
    branch_inv = lax.rsqrt(jnp.mean(branch * branch, axis=1, keepdims=True) + EPSILON)
    branch_hat = branch * branch_inv
    middle = layer_input.astype(F32) + branch_hat * attn_gain
    sides = Sides(
        Rows(parts, gather=middle.astype(LOW)),
        Spans(parts, spans, [(down_shard, 0, cols, spans - s) for s in others_spans]),
    )
    full_up, _, mixed, down_came = exchange(
        2, fsdp, parts, spans, up_came, [(s - 1, s, 0, True) for s in others_spans], sides
    )
    full_gate_up = [((gate_up_first, 0), (gate_up_first, 1))]
    full_gate_up += [((gate, 0), (up, 0)) for gate, up in zip(full_gate, full_up)]
    full_down += [gather_shard(piece) for piece in down_came]
    gates, uppers, hiddens = zip(
        *[feed_up(mixed, pair, cols, full_down[:1]) for pair in full_gate_up]
    )
    pairs = [(hidden, down, 0) for hidden, down in zip(hiddens, full_down)]
    second = product_own(3, pairs, product_others(pairs))
    second_inv = lax.rsqrt(jnp.mean(second * second, axis=1, keepdims=True) + EPSILON)
    second_hat = second * second_inv
    output = (middle + second_hat * ffn_gain).astype(LOW)

    grad_out = out_cotangent.astype(F32)
    ffn_gain_part = jnp.sum(grad_out * second_hat, axis=0)
    grad_second = norm_back(grad_out * ffn_gain, second_hat, second_inv, width)
    _, _, grad_rows = exchange(
        4, fsdp, parts, spans, sides=Sides(Rows(parts, gather=grad_second.astype(LOW)))
    )
    (now,) = weight_grad_half(5, fsdp, grad_rows, hiddens)
    down_terms = scatter(now)
    back, gate_up_grad = {}, {}
    for s in reversed(range(spans)):
        back[s] = feed_up_back(grad_rows, full_down[s], gates[s], uppers[s], [now])
        now = back[s][0]
        if s:
            (now,) = weight_grad_half(6, fsdp, mixed, back[s])
            gate_up_grad[s] = scatter(now)
    pairs = [
        (grad, *full) for s in range(spans) for grad, full in zip(back[s], full_gate_up[s])
    ]
    grad_mixed = product_own(7, pairs, product_others(pairs), [down_terms])
    grad_middle = grad_out + grad_mixed
    attn_gain_part = jnp.sum(grad_middle * branch_hat, axis=0)
    grad_branch = norm_back(grad_middle * attn_gain, branch_hat, branch_inv, width)
    sides = Sides(
        Rows(parts, gather=grad_branch.astype(LOW)),
        Spans(parts, spans, [(down_terms, s, cols, s) for s in others_spans]),
    )
    now, grad_branch_rows, down_came = weight_grad_half(8, fsdp, mixed, back[0], sides=sides)
    gate_up_grad[0] = scatter(now)
    grad_attended = nn(grad_branch_rows, full_out).astype(LOW)
    (
        query_gained,
        key_gained,
        grad_value,
        query_gain_part,
        key_gain_part,
        query_inner,
        key_inner,
        gate_came,
    ) = attend_back(
        12,
        rows_here,
        parts,
        (query_rot, key_rot),
        value_low,
        grad_attended,
        lse,
        pre,
        invs,
        gains,
        tables,
        [],
        Sides(Spans(parts, spans, [(gate_up_grad[s], 0, cols, s) for s in others_spans])),
    )
    down_grad = add_pieces(down_terms[:, :cols].astype(F32), down_came)
    (out_total,) = weight_grad_half(9, fsdp, grad_branch_rows, [attended], [grad_value])
    inners = sum_parts(jnp.concatenate([query_inner, key_inner], axis=1)) / width
    local_width = value_low.shape[1]
    grad_query = invs[0] * (query_gained - pre[:, :local_width] * invs[0] * inners[:, :1])
    grad_key = invs[1] * (key_gained - pre[:, local_width:] * invs[1] * inners[:, 1:])
    grad_qkv = jnp.concatenate(
        [grad_query.astype(LOW), grad_key.astype(LOW), grad_value], axis=1
    )
    pairs = [(grad_qkv, full_qkv, 0)]
    others = product_others(pairs, [out_total, gate_up_grad[0]])
    others[0], out_total = lax.optimization_barrier((others[0], out_total))
    out_terms = scatter(out_total)
    sides = Sides(
        Rows(parts, deliver=others),
        Spans(parts, spans, [(gate_up_grad[s], 1, cols, s) for s in others_spans]),
    )
    qkv_grad, came, up_came = grad_scatter(
        10, fsdp, parts, spans, inputs, grad_qkv, 3, [], sides
    )
    total = product_sum(rows_here, 0, pairs, F32, [qkv_grad])[0]
    input_grad = grad_middle + add_pieces(total, came)
    gate_grad = add_pieces(gate_up_grad[0][:, :cols].astype(F32), gate_came)
    up_grad = add_pieces(gate_up_grad[0][:, cols:].astype(F32), up_came)
    gain_grads = sum_all(
        jnp.stack(
            [gain_whole(query_gain_part), gain_whole(key_gain_part), attn_gain_part, ffn_gain_part]
        )
    )
    (out_grad,) = sum_spans(out_terms, 1)
    query_grad, key_grad, value_grad = jnp.split(qkv_grad, 3, axis=1)
    return (
        output,
        input_grad,
        query_grad,
        key_grad,
        value_grad,
        out_grad.T,
        gate_grad,
        up_grad,
        down_grad.T,
        *gain_grads,
    )


def solution(mesh):
    columns, rows = P("fsdp", "tensor"), P("tensor", "fsdp")
    tokens = P(("fsdp", "tensor"), None)
    weights = (columns, columns, columns, rows, columns, columns, rows)
    return jax.shard_map(
        functools.partial(layer, mesh.shape["fsdp"], mesh.shape["tensor"]),
        mesh=mesh,
        in_specs=(tokens, *weights, P(), P(), P(), P(), tokens),
        out_specs=(tokens, tokens, *weights, P(), P(), P(), P()),
        check_vma=False,
    )
```

time: 1260 us -> 1080 us (0.86)
  waiting for transfers between devices: 461 us -> 17.9 us
  Pallas kernels: 633 us -> 919 us
  other arithmetic: 58.1 us -> 45.5 us
    pallas_call x27 -> x23, Pallas kernels: 614 us -> 900 us  [call(): return pl.pallas_call(body, in_specs=specs, **options)(*operands, *earlier)]
    ppermute x9 -> x2, waiting for transfers between devices: 273 us -> 0.01 us  [to_part(): return lax.ppermute(x, 'tensor', pairs)]
    ppermute x5 -> x1, waiting for transfers between devices: 90.7 us -> 11.4 us  [to_span(): return lax.ppermute(x, 'tensor', pairs)]
    ppermute x5, waiting for transfers between devices: 59.9 us -> 3.49 us  [sum_all(): x = x + lax.ppermute(x, axis, [(i, i ^ bit) for i in range(size)])]
    ppermute x5 -> x0, waiting for transfers between devices: 36.8 us -> none  [weight_grad_away(): return (sent, lax.ppermute(sent, 'fsdp', [(f, f ^ 1) for f in range(fsdp)]))]
    concatenate x4 -> x1, other arithmetic: 14.5 us -> 0.2 us  [layer(): jnp.concatenate([-sin, sin], axis=1)]
    unnamed x91 -> x88, local copies, waits for them, and re-layouts: 27.7 us -> 28.2 us
  transfers between devices with their start and end apart: 31 -> 15, of which waited for: 19 -> 4; matrix products, arithmetic and copies ran while one was open for 6% -> 5% of each run, Pallas kernels for 36% -> 64%
where the time goes in v3:
time: 1080 us
  Pallas kernels  919 us (85%)
  other arithmetic  45.5 us (4%)
  local copies, waits for them, and re-layouts  37.5 us (3%)
  starting transfers between devices  30.6 us (3%)
  waiting for transfers between devices  17.9 us (2%)
  between operations  15.3 us (1%)
    pallas_call x23, Pallas kernels, call(): return pl.pallas_call(body, in_specs=specs, **options)(*operands, *earlier)  900 us
    unnamed x88, local copies, waits for them, and re-layouts  28.2 us
    ppermute x2, starting transfers between devices, to_part(): return lax.ppermute(x, 'tensor', pairs)  24.1 us
  transfers between devices with their start and end apart: 15, of which 4 were waited for; matrix products, arithmetic and copies ran while one was open for 5% of the time, Pallas kernels for 64%

profile of v3, /device:TPU:0, one launch (start us, length us, event | category | flops | bytes accessed | tf_op | source)
XLA Modules:
  0.0 1075.6 jit_solution(4768422797224278362)
XLA Ops:
  11.6 84.1 %exchange.4 = (bf16[8,256,3072]{2,1,0:T(8,128)(2,1)}, bf16[8,256,1024]{2,1,0:T(8,128)(2,1)}, bf16[2,512,2048]{2,1,0:T(8,128)(2,1)}) custom-call(bf16[512,2048]{1,0:T(8,128)(2,1)} %refs_0_.1, bf16[256,512]{1,0:T(8,128)(2,1)} %refs_5_.1, bf16[256,512]{1,0:T(8,128)(2,1)} %refs_6_.1, bf16[256,512]{1,0:T(8,128)(2,1)} %refs_7_.1, bf16[256,512]{1,0:T(8,128)(2,1)} %bitcast.76, ...), custom_call_target="tpu_custom_call" | custom-call | tf_op jit(solution)/shard_map/exchange/pallas_call | solution.py:196
  95.9 19.4 %project.1 = (f32[1024,2048]{1,0:T(8,128)}, bf16[1024,1024]{1,0:T(8,128)(2,1)S(1)}, f32[1024,1]{1,0:T(8,128)S(1)}, f32[1024,1]{1,0:T(8,128)S(1)}) custom-call(bf16[1024,2048]{1,0:T(8,128)(2,1)} %bitcast.91, bf16[2048,3072]{1,0:T(8,128)(2,1)} %bitcast.59), custom_call_target="tpu_custom_call" | custom-call | flops 12884901888 | bytes 27262976 | tf_op jit(solution)/shard_map/project/pallas_call | solution.py:1038
  117.0 24.1 %collective-permute-start = (f32[1024,2]{0,1:T(2,128)S(1)}, f32[1024,2]{0,1:T(2,128)S(1)}, u32[]{:S(2)}, u32[]{:S(2)}) collective-permute-start(f32[1024,2]{0,1:T(2,128)S(1)} %pad_maximum_fusion.4), channel_id=1, source_target_pairs={{0,1},{1,0},{2,3},{3,2},{4,5},{5,4},{6,7},{7,6},{8,9},{9,8},{10,11... | collective-permute-start | bytes 24584 | tf_op jit(solution)/shard_map/ppermute | solution.py:1179
  151.3 51.2 %attend.1 = (bf16[1024,1024]{1,0:T(8,128)(2,1)S(1)}, bf16[1024,1024]{1,0:T(8,128)(2,1)S(1)}, bf16[1024,1024]{1,0:T(8,128)(2,1)S(1)}, f32[8,1024,1]{2,1,0:T(8,128)}, bf16[256,2048]{1,0:T(8,128)(2,1)S(1)}) custom-call(f32[1024,2048]{1,0:T(8,128)} %get-tuple-element.66.refs_0_.refs_1_.refs_5_.refs_6_, ...), custom_call_target="tpu_custom_call" | custom-call | flops 8589934592 | bytes 16777216 | tf_op jit(solution)/shard_map/attend/pallas_call | solution.py:196
  207.6 6.1 product_sum.8.refs_2_.refs_0_
  213.7 70.8 %exchange.5 = (bf16[8,256,2048]{2,1,0:T(8,128)(2,1)}, bf16[1,512,2048]{2,1,0:T(8,128)(2,1)}, bf16[256,2048]{1,0:T(8,128)(2,1)}) custom-call(bf16[512,2048]{1,0:T(8,128)(2,1)} %product_sum.8.refs_2_.refs_0_, bf16[256,4096]{1,0:T(8,128)(2,1)} %copy-done, bf16[256,2048]{1,0:T(8,128)(2,1)} %copy-done.3), custom_call_target="tpu_custom_call" | custom-call | tf_op jit(solution)/shard_map/exchange/pallas_call | solution.py:196
  285.0 6.5 product_sum.9
  291.5 4.0 multiply_reduce_fusion.3
  298.1 76.3 %exchange.6 = (bf16[8,256,2048]{2,1,0:T(8,128)(2,1)}, bf16[2,512,2048]{2,1,0:T(8,128)(2,1)}, bf16[256,2048]{1,0:T(8,128)(2,1)}) custom-call(bf16[512,2048]{1,0:T(8,128)(2,1)} %fusion.7.refs_0_, bf16[256,2048]{1,0:T(8,128)(2,1)} %bitcast.75, bf16[256,2048]{1,0:T(8,128)(2,1)} %get-tuple-element.77.refs_2_), custom_call_target="tpu_custom_call" | custom-call | tf_op jit(solution)/shard_map/exchange/pallas_call | solution.py:196
  374.5 24.0 %feed_up.2 = (f32[1024,2048]{1,0:T(8,128)}, f32[1024,2048]{1,0:T(8,128)}, bf16[1024,2048]{1,0:T(8,128)(2,1)S(1)}) custom-call(bf16[1024,2048]{1,0:T(8,128)(2,1)} %bitcast.93, bf16[2048,4096]{1,0:T(8,128)(2,1)} %all-gather.4.cloned.1.call-done.refs_3_.refs_1_.refs_2_, bf16[2048,4096]{1,0:T(8,128)(2,1)} %all-gather.4.cloned.1.call-done.refs_3_.refs_1_.refs_2_, ...), custom_call_target="tpu_custom_call" | custom-call | flops 17179869184 | bytes 37748736 | tf_op jit(solution)/shard_map/feed_up/pallas_call | solution.py:196
  400.5 23.9 %feed_up.3 = (f32[1024,2048]{1,0:T(8,128)}, f32[1024,2048]{1,0:T(8,128)}, bf16[1024,2048]{1,0:T(8,128)(2,1)S(1)}) custom-call(bf16[1024,2048]{1,0:T(8,128)(2,1)} %bitcast.94, bf16[2048,2048]{1,0:T(8,128)(2,1)} %bitcast.65, bf16[2048,2048]{1,0:T(8,128)(2,1)} %bitcast.68, bf16[2048,2048]{1,0:T(8,128)(2,1)} %all-gather.6.cloned.1.call-done.refs_3_.refs_1_), custom_call_target="tpu_custom_call" | custom-call | flops 17179869184 | bytes 37748736 | tf_op jit(solution)/shard_map/feed_up/pallas_call | solution.py:196
  429.3 13.8 %product_sum.10.refs_4_ = bf16[512,2048]{1,0:T(8,128)(2,1)} custom-call(bf16[1024,2048]{1,0:T(8,128)(2,1)} %copy-done.12, bf16[2048,2048]{1,0:T(8,128)(2,1)} %all-gather.6.cloned.1.call-done.refs_3_.refs_1_, bf16[1024,2048]{1,0:T(8,128)(2,1)} %copy-done.13, bf16[2048,2048]{1,0:T(8,128)(2,1)} %all-gather.8.cloned.1.call-done.refs_3_.refs_1_), custom_call_target="tpu_custom_call" | custom-call | flops 8589934592 | bytes 20971520 | tf_op jit(solution)/shard_map/product_sum/pallas_call | solution.py:196
  443.1 52.8 %product_sum.11 = (f32[512,2048]{1,0:T(8,128)}, bf16[1,512,2048]{2,1,0:T(8,128)(2,1)}) custom-call(bf16[1024,2048]{1,0:T(8,128)(2,1)} %copy-done.12, bf16[2048,2048]{1,0:T(8,128)(2,1)} %all-gather.6.cloned.1.call-done.refs_3_.refs_1_, bf16[1024,2048]{1,0:T(8,128)(2,1)} %copy-done.13, bf16[2048,2048]{1,0:T(8,128)(2,1)} %all-gather.8.cloned.1.call-done.refs_3_.refs_1_, ...), custom_call_target="tpu_custom_call" | custom-call | flops 8589934592 | bytes 20971520 | tf_op jit(solution)/shard_map/product_sum/pallas_call | solution.py:196
  496.0 3.6 multiply_reduce_fusion.2
  502.9 3.8 fusion.4
  506.7 47.4 %exchange.7 = bf16[2,512,2048]{2,1,0:T(8,128)(2,1)} custom-call(bf16[512,2048]{1,0:T(8,128)(2,1)} %get-tuple-element.180.refs_0_), custom_call_target="tpu_custom_call" | custom-call | tf_op jit(solution)/shard_map/exchange/pallas_call | solution.py:196
  554.0 28.2 %weight_grad.4.refs_4_ = bf16[1024,4096]{1,0:T(8,128)(2,1)} custom-call(bf16[1024,2048]{1,0:T(8,128)(2,1)} %bitcast.62, bf16[1024,2048]{1,0:T(8,128)(2,1)} %copy-done.12, bf16[1024,2048]{1,0:T(8,128)(2,1)} %copy-done.13), custom_call_target="tpu_custom_call" | custom-call | flops 17179869184 | bytes 29360128 | tf_op jit(solution)/shard_map/weight_grad/pallas_call | solution.py:196
  582.3 18.9 %feed_up_back.2 = (bf16[1024,2048]{1,0:T(8,128)(2,1)}, bf16[1024,2048]{1,0:T(8,128)(2,1)}) custom-call(bf16[1024,2048]{1,0:T(8,128)(2,1)} %bitcast.63, bf16[2048,2048]{1,0:T(8,128)(2,1)} %all-gather.8.cloned.1.call-done.refs_3_.refs_1_, f32[1024,2048]{1,0:T(8,128)} %get-tuple-element.88.refs_2_, f32[1024,2048]{1,0:T(8,128)} %get-tuple-element.89.refs_3_, ...), custom_call_target="tpu_custom_call" | custom-call | flops 8589934592 | bytes 33554432 | tf_op jit(solution)/shard_map/feed_up_back/pallas_call | solution.py:196
  601.2 28.8 %weight_grad.5.refs_4_ = bf16[1024,4096]{1,0:T(8,128)(2,1)} custom-call(bf16[1024,2048]{1,0:T(8,128)(2,1)} %bitcast.95, bf16[1024,2048]{1,0:T(8,128)(2,1)} %get-tuple-element.90.refs_1_.refs_4_, bf16[1024,2048]{1,0:T(8,128)(2,1)} %get-tuple-element.91.refs_2_.refs_6_), custom_call_target="tpu_custom_call" | custom-call | flops 17179869184 | bytes 29360128 | tf_op jit(solution)/shard_map/weight_grad/pallas_call | solution.py:196
  630.0 19.7 %feed_up_back.3 = (bf16[1024,2048]{1,0:T(8,128)(2,1)}, bf16[1024,2048]{1,0:T(8,128)(2,1)}) custom-call(bf16[1024,2048]{1,0:T(8,128)(2,1)} %bitcast.64, bf16[2048,2048]{1,0:T(8,128)(2,1)} %all-gather.6.cloned.1.call-done.refs_3_.refs_1_, f32[1024,2048]{1,0:T(8,128)} %get-tuple-element.86.refs_2_, f32[1024,2048]{1,0:T(8,128)} %get-tuple-element.87.refs_3_, ...), custom_call_target="tpu_custom_call" | custom-call | flops 8589934592 | bytes 33554432 | tf_op jit(solution)/shard_map/feed_up_back/pallas_call | solution.py:196
  649.7 26.0 %product_sum.12.refs_8_ = bf16[512,2048]{1,0:T(8,128)(2,1)} custom-call(bf16[1024,2048]{1,0:T(8,128)(2,1)} %get-tuple-element.92.refs_0_.refs_1_, bf16[2048,4096]{1,0:T(8,128)(2,1)} %all-gather.4.cloned.1.call-done.refs_3_.refs_1_.refs_2_, bf16[1024,2048]{1,0:T(8,128)(2,1)} %get-tuple-element.93.refs_2_, ...), custom_call_target="tpu_custom_call" | custom-call | flops 17179869184 | bytes 37748736 | tf_op jit(solution)/shard_map/product_sum/pallas_call | solution.py:196
  675.7 56.4 %product_sum.13 = (f32[512,2048]{1,0:T(8,128)}, bf16[1,512,2048]{2,1,0:T(8,128)(2,1)}) custom-call(bf16[1024,2048]{1,0:T(8,128)(2,1)} %get-tuple-element.92.refs_0_.refs_1_, bf16[2048,4096]{1,0:T(8,128)(2,1)} %all-gather.4.cloned.1.call-done.refs_3_.refs_1_.refs_2_, bf16[1024,2048]{1,0:T(8,128)(2,1)} %get-tuple-element.93.refs_2_, ...), custom_call_target="tpu_custom_call" | custom-call | flops 17179869184 | bytes 37748736 | tf_op jit(solution)/shard_map/product_sum/pallas_call | solution.py:196
  732.2 4.7 multiply_reduce_fusion
  741.1 77.5 %weight_grad.6 = (bf16[1024,4096]{1,0:T(8,128)(2,1)}, bf16[2,512,2048]{2,1,0:T(8,128)(2,1)}, bf16[256,2048]{1,0:T(8,128)(2,1)}) custom-call(bf16[1024,2048]{1,0:T(8,128)(2,1)} %bitcast.96, bf16[1024,2048]{1,0:T(8,128)(2,1)} %get-tuple-element.92.refs_0_.refs_1_, bf16[1024,2048]{1,0:T(8,128)(2,1)} %get-tuple-element.93.refs_2_, ...), custom_call_target="tpu_custom_call" | custom-call | flops 17179869184 | bytes 29360128 | tf_op jit(solution)/shard_map/weight_grad/pallas_call | solution.py:196
  818.7 9.3 convolution_convert_fusion.refs_3_
  830.1 50.9 %attend_back.1 = (f32[1024,1024]{1,0:T(8,128)}, f32[1024,1024]{1,0:T(8,128)}, bf16[1024,1024]{1,0:T(8,128)(2,1)}, f32[1,1024]{1,0:T(1,128)S(1)}, f32[1,1024]{1,0...) custom-call(bf16[1024,1024]{1,0:T(8,128)(2,1)} %copy-done.16, ...), custom_call_target="tpu_custom_call" | custom-call | flops 21474836480 | bytes 33554432 | tf_op jit(solution)/shard_map/attend_back/pallas_call | solution.py:196
  881.7 13.7 %weight_grad.7.refs_2_ = bf16[1024,1024]{1,0:T(8,128)(2,1)} custom-call(bf16[1024,2048]{1,0:T(8,128)(2,1)} %bitcast.98, bf16[1024,1024]{1,0:T(8,128)(2,1)} %copy-done.2, bf16[1024,1024]{1,0:T(8,128)(2,1)} %get-tuple-element.104.refs_2_), custom_call_target="tpu_custom_call" | custom-call | flops 4294967296 | bytes 10485760 | tf_op jit(solution)/shard_map/weight_grad/pallas_call | solution.py:196
  902.2 6.8 multiply_convert_fusion.1
  915.3 11.5 %product_sum.14.refs_2_ = bf16[512,2048]{1,0:T(8,128)(2,1)} custom-call(bf16[1024,3072]{1,0:T(8,128)(2,1)} %pad_maximum_fusion.refs_0_.refs_1_, bf16[2048,3072]{1,0:T(8,128)(2,1)} %bitcast.60, bf16[1024,1024]{1,0:T(8,128)(2,1)} %weight_grad.7.refs_2_, bf16[256,4096]{1,0:T(8,128)(2,1)} %reduce-scatter.9.cloned.1.call-done.refs_3_), custom_call_target="tpu_custom_call" | custom-call | flops 6442450944 | bytes 16777216 | tf_op jit(solution)/shard_map/product_sum/pallas_call | solution.py:196
  933.3 99.7 %grad_scatter.1 = (f32[256,1536]{1,0:T(8,128)}, bf16[1,512,2048]{2,1,0:T(8,128)(2,1)}, bf16[256,2048]{1,0:T(8,128)(2,1)}) custom-call(bf16[1024,2048]{1,0:T(8,128)(2,1)} %bitcast.92, bf16[1024,3072]{1,0:T(8,128)(2,1)} %pad_maximum_fusion.refs_0_.refs_1_, bf16[512,2048]{1,0:T(8,128)(2,1)} %product_sum.14.refs_2_, ...), custom_call_target="tpu_custom_call" | custom-call | flops 12884901888 | bytes 16777216 | tf_op jit(solution)/shard_map/grad_scatter/pallas_call | solution.py:196
  1033.1 11.9 %product_sum.15 = f32[512,2048]{1,0:T(8,128)} custom-call(bf16[1024,3072]{1,0:T(8,128)(2,1)} %pad_maximum_fusion.refs_0_.refs_1_, bf16[2048,3072]{1,0:T(8,128)(2,1)} %bitcast.61, f32[256,1536]{1,0:T(8,128)} %get-tuple-element.107.refs_2_), custom_call_target="tpu_custom_call" | custom-call | flops 6442450944 | bytes 16777216 | tf_op jit(solution)/shard_map/product_sum/pallas_call | solution.py:196
  1056.0 11.4 %collective-permute-done.2 = bf16[256,1,512]{0,2,1:T(8,128)(2,1)S(1)} collective-permute-done((bf16[256,1,512]{0,2,1:T(8,128)(2,1)S(1)}, bf16[256,1,512]{0,2,1:T(8,128)(2,1)S(1)}, u32[]{:S(2)}, u32[]{:S(2)}) %collective-permute-start.2) | collective-permute-done | bytes 262176 | tf_op jit(solution)/shard_map/ppermute | solution.py:1187
  (176 shorter events, 73.2 us)
Async XLA Ops:
  7.2 277.8 %all-gather.4.cloned.1.call-start = ((), (), s32[]{:S(2)}) async-start(), calls=%async_computation.4 | async-start | bytes 18874368 | tf_op jit(solution)/shard_map/all_gather | solution.py:1190
  11.6 84.1 %copy-start = (bf16[256,4096]{1,0:T(8,128)(2,1)}, bf16[256,4096]{1,0:T(8,128)(2,1)S(1)}, u32[]{:S(2)}) copy-start(bf16[256,4096]{1,0:T(8,128)(2,1)S(1)} %constant_dynamic-update-slice_fusion.refs_9_.refs_1_) | copy-start | bytes 6291460
  95.8 278.7 %all-gather.6.cloned.1.call-start = ((), (), s32[]{:S(2)}) async-start(), calls=%async_computation.5 | async-start | bytes 9437184 | tf_op jit(solution)/shard_map/all_gather | solution.py:1190
  95.8 45.2 %copy-start.40 = (f32[2048]{0:T(1024)S(1)}, f32[2048]{0:T(1024)}, u32[]{:S(2)}) copy-start(f32[2048]{0:T(1024)} %param.21) | copy-start | bytes 24580
  95.9 45.3 %copy-start.41 = (f32[2048]{0:T(1024)S(1)}, f32[2048]{0:T(1024)}, u32[]{:S(2)}) copy-start(f32[2048]{0:T(1024)} %param.22) | copy-start | bytes 24580
  117.0 29.1 %collective-permute-start = (f32[1024,2]{0,1:T(2,128)S(1)}, f32[1024,2]{0,1:T(2,128)S(1)}, u32[]{:S(2)}, u32[]{:S(2)}) collective-permute-start(f32[1024,2]{0,1:T(2,128)S(1)} %pad_maximum_fusion.4), channel_id=1, source_target_pairs={{0,1},{1,0},{2,3},{3,2},{4,5},{5,4},{6,7},{7,6},{8,9},{9,8},{10,11... | collective-permute-start | bytes 24584 | tf_op jit(solution)/shard_map/ppermute | solution.py:1179
  143.6 58.9 %copy-start.10 = (f32[1024]{0:T(1024)}, f32[1024]{0:T(1024)S(1)}, u32[]{:S(2)}) copy-start(f32[1024]{0:T(1024)S(1)} %pad_maximum_fusion.7) | copy-start | bytes 12292
  149.4 53.2 %copy-start.4 = (f32[1024,1]{1,0:T(8,128)}, f32[1024,1]{1,0:T(8,128)S(1)}, u32[]{:S(2)}) copy-start(f32[1024,1]{1,0:T(8,128)S(1)} %get-tuple-element.187.refs_4_.refs_8_) | copy-start | bytes 12292
  149.4 53.2 %copy-start.6 = (f32[1024,1]{1,0:T(8,128)}, f32[1024,1]{1,0:T(8,128)S(1)}, u32[]{:S(2)}) copy-start(f32[1024,1]{1,0:T(8,128)S(1)} %get-tuple-element.188.refs_3_.refs_7_) | copy-start | bytes 12292
  284.5 144.8 %all-gather.8.cloned.1.call-start = ((), (), s32[]{:S(2)}) async-start(), calls=%async_computation.6 | async-start | bytes 9437184 | tf_op jit(solution)/shard_map/all_gather | solution.py:1190
  374.4 301.3 %reduce-scatter.5.cloned.1.call-start = ((), (), s32[]{:S(2)}) async-start(), calls=%async_computation.7 | async-start | bytes 10485760 | tf_op jit(solution)/shard_map/reduce_scatter | solution.py:1222
  443.1 56.5 %copy-start.26 = (bf16[512,2048]{1,0:T(8,128)(2,1)S(1)}, bf16[512,2048]{1,0:T(8,128)(2,1)}, u32[]{:S(2)}) copy-start(bf16[512,2048]{1,0:T(8,128)(2,1)} %param.25) | copy-start | bytes 6291460
  582.3 245.7 %reduce-scatter.7.cloned.1.call-start = ((), (), s32[]{:S(2)}) async-start(), calls=%async_computation.8 | async-start | bytes 10485760 | tf_op jit(solution)/shard_map/reduce_scatter | solution.py:1222
  630.0 285.4 %reduce-scatter.9.cloned.1.call-start = ((), (), s32[]{:S(2)}) async-start(), calls=%async_computation.9 | async-start | bytes 10485760 | tf_op jit(solution)/shard_map/reduce_scatter | solution.py:1222
  675.7 56.5 %copy-start.27 = (bf16[512,2048]{1,0:T(8,128)(2,1)S(1)}, bf16[512,2048]{1,0:T(8,128)(2,1)}, u32[]{:S(2)}) copy-start(bf16[512,2048]{1,0:T(8,128)(2,1)} %param.25) | copy-start | bytes 6291460
  675.7 56.5 %copy-start.20 = (f32[512,2048]{1,0:T(8,128)S(1)}, f32[512,2048]{1,0:T(8,128)}, u32[]{:S(2)}) copy-start(f32[512,2048]{1,0:T(8,128)} %copy-done.18) | copy-start | bytes 12582916
  818.7 234.8 %reduce-scatter.11.cloned.1.call-start = ((), (), s32[]{:S(2)}) async-start(), calls=%async_computation.10 | async-start | bytes 2621440 | tf_op jit(solution)/shard_map/reduce_scatter | solution.py:1222
  818.7 9.3 copy-start.9
  881.5 14.1 %collective-permute-start.1 = (f32[1024,2]{0,1:T(2,128)S(1)}, f32[1024,2]{0,1:T(2,128)S(1)}, u32[]{:S(2)}, u32[]{:S(2)}) collective-permute-start(f32[1024,2]{0,1:T(2,128)S(1)} %pad_maximum_fusion.5), channel_id=1, source_target_pairs={{0,1},{1,0},{2,3},{3,2},{4,5},{5,4},{6,7},{7,6},{8,9},{9,8},{10,11... | collective-permute-start | bytes 24584 | tf_op jit(solution)/shard_map/ppermute | solution.py:1179
  881.6 13.8 %copy-start.35 = (f32[2048]{0:T(1024)S(1)}, f32[2048]{0:T(1024)}, u32[]{:S(2)}) copy-start(f32[2048]{0:T(1024)} %get-tuple-element.169) | copy-start | bytes 24580
  881.6 20.6 %copy-start.38 = (f32[1024]{0:T(1024)S(1)}, f32[1024]{0:T(1024)}, u32[]{:S(2)}) copy-start(f32[1024]{0:T(1024)} %get-tuple-element.171) | copy-start | bytes 12292
  881.6 20.6 %copy-start.39 = (f32[1024]{0:T(1024)S(1)}, f32[1024]{0:T(1024)}, u32[]{:S(2)}) copy-start(f32[1024]{0:T(1024)} %get-tuple-element.172) | copy-start | bytes 12292
  895.4 1.3 collective-permute-start.3
  896.8 4.7 collective-permute-start.4
  901.5 7.5 collective-permute-start.5
  909.1 5.2 collective-permute-start.6
  914.3 12.6 %copy-start.33 = (bf16[256,2048]{1,0:T(8,128)(2,1)S(1)}, bf16[256,2048]{1,0:T(8,128)(2,1)}, u32[]{:S(2)}) copy-start(bf16[256,2048]{1,0:T(8,128)(2,1)} %get-tuple-element.112) | copy-start | bytes 3145732
  914.3 18.3 %collective-permute-start.7 = (f32[4,2048]{1,0:T(4,128)S(1)}, f32[4,2048]{1,0:T(4,128)S(1)}, u32[]{:S(2)}, u32[]{:S(2)}) collective-permute-start(f32[4,2048]{1,0:T(4,128)S(1)} %add.207), channel_id=1, source_target_pairs={{0,2},{1,3},{2,0},{3,1},{4,6},{5,7},{6,4},{7,5},{8,10},{9,11},{10,... | collective-permute-start | bytes 98312 | tf_op jit(solution)/shard_map/ppermute | solution.py:1215
  1033.1 11.9 %copy-start.29 = (bf16[256,4096]{1,0:T(8,128)(2,1)S(1)}, bf16[256,4096]{1,0:T(8,128)(2,1)}, u32[]{:S(2)}) copy-start(bf16[256,4096]{1,0:T(8,128)(2,1)} %reduce-scatter.9.cloned.1.call-done.refs_3_) | copy-start | bytes 6291460
  1033.1 11.9 %copy-start.34 = (bf16[256,2048]{1,0:T(8,128)(2,1)S(1)}, bf16[256,2048]{1,0:T(8,128)(2,1)}, u32[]{:S(2)}) copy-start(bf16[256,2048]{1,0:T(8,128)(2,1)} %get-tuple-element.111) | copy-start | bytes 3145732
  1033.1 14.8 %copy-start.31 = (bf16[1,512,2048]{2,1,0:T(8,128)(2,1)S(1)}, bf16[1,512,2048]{2,1,0:T(8,128)(2,1)}, u32[]{:S(2)}) copy-start(bf16[1,512,2048]{2,1,0:T(8,128)(2,1)} %get-tuple-element.108) | copy-start | bytes 6291460
  1054.7 12.7 %collective-permute-start.2 = (bf16[256,1,512]{0,2,1:T(8,128)(2,1)S(1)}, bf16[256,1,512]{0,2,1:T(8,128)(2,1)S(1)}, u32[]{:S(2)}, u32[]{:S(2)}) collective-permute-start(bf16[256,1,512]{0,2,1:T(8,128)(2,1)S(1)} %slice_bitcast_fusion), channel_id=1, source_target_pairs={{0,2},{1,3},{2,0},{3,1},{4,6},{5,7},{6,4},{7,5},{8,10},{9,11},{10,... | collective-permute-start | bytes 786440 | tf_op jit(solution)/shard_map/ppermute | solution.py:1187
  (25 other events, 88.7 us)
Sparse Core Ops, SparseCore 0:
  95.9 111.4 all-gather.3
  284.6 81.6 all-gather.5
  374.5 54.6 all-gather.7
  582.4 86.5 reduce-scatter.4
  672.2 86.4 reduce-scatter.6
  818.8 85.1 reduce-scatter.8
  927.0 40.1 reduce-scatter.10

commit v4 on v3

--- a/solution.py
+++ b/solution.py
@@ -59,9 +59,8 @@
     @pl.when(pl.program_id(0) == 0)
     def _():
         greet(sides.partners())
-        sides.start(*sides_at)
-        sides.start_rest(*sides_at)
-
+
+    sides.start_over(pl.program_id(0), heads, *sides_at)
     half = HEAD_DIM // 2
     for block in range(SEQ_LEN // BLOCK):
         here = pl.ds(block_start(place, block, rows, parts), BLOCK)
@@ -104,11 +103,12 @@
 
     @pl.when(pl.program_id(0) == 0)
     def _():
-        greet(sides.partners())
-        sides.start(*sides_at)
-        sides.start_rest(*sides_at)
+        if sides.jobs:
+            greet(sides.partners())
         query_inner_ref[...] = jnp.zeros_like(query_inner_ref)
         key_inner_ref[...] = jnp.zeros_like(key_inner_ref)
+
+    sides.start_over(pl.program_id(0), heads, *sides_at)
 
     def finish(grad, here, values_ref, inv_ref, gain_ref, out_ref, inner_ref):
         back = grad * cos_ref[here] - pltpu.roll(grad, half, 1) * sin_ref[here]
@@ -173,6 +173,7 @@
 
 MESH = pl.DeviceIdType.MESH
 MIB = 2**20
+CHUNKS = 4
 
 
 def flip(index, bit):
@@ -250,15 +251,16 @@
 class Rows:
     def __init__(self, parts, gather=None, deliver=None):
         self.parts, self.gather = parts, gather is not None
-        self.half = (gather if self.gather else deliver[0]).shape[0] // 2
-        self.operands = [gather] if self.gather else list(deliver)
-        first = self.operands[0]
+        self.operands = [gather if self.gather else deliver]
+        rows, width = self.operands[0].shape
+        self.rows = rows if self.gather else rows // parts
+        self.chunk = self.rows // CHUNKS
         count = parts if self.gather else parts - 1
-        self.out_shapes = [jax.ShapeDtypeStruct((count, *first.shape), LOW)]
-        count = 2 * parts
+        self.out_shapes = [jax.ShapeDtypeStruct((count, self.rows, width), LOW)]
+        count = CHUNKS * parts
         self.scratch = [pltpu.SemaphoreType.DMA((count,)), pltpu.SemaphoreType.DMA((count,))]
         if self.gather:
-            self.scratch.append(pltpu.VMEM(first.shape, LOW))
+            self.scratch.append(pltpu.VMEM((rows, width), LOW))
 
     def ranks(self):
         rank = lax.axis_index("tensor")
@@ -271,35 +273,30 @@
     def partners(self):
         return [{"tensor": rank} for rank in self.ranks()]
 
-    def copies(self, halves, refs, outs, send_sems, recv_sems, hold=None):
+    def copies(self, chunks, refs, outs, send_sems, recv_sems, hold=None):
         made = []
-        for half in halves:
-            rows = pl.ds(half * self.half, self.half)
+        for chunk in chunks:
             for i, rank in enumerate(self.ranks()):
-                src = refs[0] if self.gather else refs[i]
+                first = 0 if self.gather else (i + 1) * self.rows
+                src = refs[0].at[pl.ds(first + chunk * self.chunk, self.chunk)]
                 dst = outs[0].at[i + 1] if self.gather else outs[0].at[i]
-                sem = 2 * i + half
+                dst = dst.at[pl.ds(chunk * self.chunk, self.chunk)]
+                sem = CHUNKS * i + chunk
                 made.append(
-                    remote(
-                        src.at[rows], dst.at[rows], send_sems.at[sem], recv_sems.at[sem], tensor=rank
-                    )
+                    remote(src, dst, send_sems.at[sem], recv_sems.at[sem], tensor=rank)
                 )
         return made
 
     def load(self, refs, outs, send_sems, recv_sems, hold):
-        return pltpu.make_async_copy(refs[0], hold, send_sems.at[2 * self.parts - 1])
+        return pltpu.make_async_copy(refs[0], hold, send_sems.at[CHUNKS * self.parts - 1])
 
     def store(self, refs, outs, send_sems, recv_sems, hold):
-        return pltpu.make_async_copy(hold, outs[0].at[0], recv_sems.at[2 * self.parts - 1])
-
-    def start(self, *where):
-        for copy in self.copies([0], *where):
-            copy.start()
-        if self.gather:
+        return pltpu.make_async_copy(hold, outs[0].at[0], recv_sems.at[CHUNKS * self.parts - 1])
+
+    def start(self, chunk, *where):
+        if self.gather and chunk == 0:
             self.load(*where).start()
-
-    def start_rest(self, *where):
-        for copy in self.copies([1], *where):
+        for copy in self.copies([chunk], *where):
             copy.start()
 
     def finish(self, *where):
@@ -307,7 +304,7 @@
             self.load(*where).wait()
             self.store(*where).start()
             self.store(*where).wait()
-        for copy in self.copies([0, 1], *where):
+        for copy in self.copies(range(CHUNKS), *where):
             copy.wait()
 
     def results(self, outs):
@@ -324,7 +321,7 @@
         self.out_shapes = [
             jax.ShapeDtypeStruct((array.shape[0], width), LOW) for array, _, width, _ in terms
         ]
-        count = max(1, len(terms))
+        count = CHUNKS * max(1, len(terms))
         self.scratch = [pltpu.SemaphoreType.DMA((count,)), pltpu.SemaphoreType.DMA((count,))]
 
     def rank(self, back):
@@ -335,31 +332,89 @@
     def partners(self):
         return [{"tensor": self.rank(s)} for s in range(1, self.spans)]
 
-    def copies(self, refs, outs, send_sems, recv_sems):
-        return [
-            remote(
-                ref.at[:, pl.ds(run * width, width)],
-                out,
-                send_sems.at[i],
-                recv_sems.at[i],
-                tensor=self.rank(back),
-            )
-            for i, (ref, out, (_, run, width, back)) in enumerate(zip(refs, outs, self.terms))
-        ]
-
-    def start(self, *where):
-        for copy in self.copies(*where):
+    def copies(self, chunks, refs, outs, send_sems, recv_sems):
+        made = []
+        for chunk in chunks:
+            for i, (ref, out, (array, run, width, back)) in enumerate(zip(refs, outs, self.terms)):
+                size = array.shape[0] // CHUNKS
+                rows, sem = pl.ds(chunk * size, size), CHUNKS * i + chunk
+                made.append(
+                    remote(
+                        ref.at[rows, pl.ds(run * width, width)],
+                        out.at[rows],
+                        send_sems.at[sem],
+                        recv_sems.at[sem],
+                        tensor=self.rank(back),
+                    )
+                )
+        return made
+
+    def start(self, chunk, *where):
+        for copy in self.copies([chunk], *where):
             copy.start()
 
-    def start_rest(self, *where):
-        pass
-
     def finish(self, *where):
-        for copy in self.copies(*where):
+        for copy in self.copies(range(CHUNKS), *where):
             copy.wait()
 
     def results(self, outs):
         return list(outs)
+
+
+class SumAll:
+    def __init__(self, fsdp, tensor, array):
+        self.operands = [array]
+        self.out_shapes = [jax.ShapeDtypeStruct(array.shape, F32)]
+        self.turns = [
+            (axis, 1 << b)
+            for axis, size in (("fsdp", fsdp), ("tensor", tensor))
+            for b in range(size.bit_length() - 1)
+        ]
+        count = len(self.turns)
+        self.scratch = [
+            pltpu.SemaphoreType.DMA((count + 1,)),
+            pltpu.SemaphoreType.DMA((count,)),
+            pltpu.VMEM(array.shape, F32),
+            pltpu.VMEM((count, *array.shape), F32),
+        ]
+
+    def partners(self):
+        return [{axis: flip(lax.axis_index(axis), bit)} for axis, bit in self.turns]
+
+    def copy(self, turn, refs, outs, send_sems, recv_sems, total, came):
+        axis, bit = self.turns[turn]
+        device = {axis: flip(lax.axis_index(axis), bit)}
+        return remote(total, came.at[turn], send_sems.at[turn], recv_sems.at[turn], **device)
+
+    def take(self, turn, *where):
+        self.copy(turn, *where).wait()
+        total, came = where[-2:]
+        total[...] += came[turn]
+
+    def start(self, chunk, *where):
+        refs, _, send_sems, _, total, _ = where
+        if chunk == 0:
+            load = pltpu.make_async_copy(refs[0], total, send_sems.at[len(self.turns)])
+            load.start()
+            load.wait()
+        elif chunk < len(self.turns):
+            self.take(chunk - 1, *where)
+        if chunk < len(self.turns):
+            self.copy(chunk, *where).start()
+
+    def finish(self, *where):
+        _, outs, send_sems, _, total, _ = where
+        count = len(self.turns)
+        for turn in range(min(CHUNKS, count) - 1, count):
+            self.take(turn, *where)
+            if turn + 1 < count:
+                self.copy(turn + 1, *where).start()
+        store = pltpu.make_async_copy(total, outs[0], send_sems.at[count])
+        store.start()
+        store.wait()
+
+    def results(self, outs):
+        return outs[0]
 
 
 class Sides:
@@ -378,13 +433,22 @@
             yield job, (refs[: counts[0]], outs[: counts[1]], *scratch[: counts[2]])
             refs, outs, scratch = refs[counts[0] :], outs[counts[1] :], scratch[counts[2] :]
 
-    def start(self, *where):
+    def start(self, chunk, *where):
         for job, own in self.each(*where):
-            job.start(*own)
-
-    def start_rest(self, *where):
+            job.start(chunk, *own)
+
+    def start_over(self, step, steps, *where):
         for job, own in self.each(*where):
-            job.start_rest(*own)
+            stride = steps // CHUNKS
+            if stride < 2 and isinstance(job, Spans):
+                stride = 0
+            elif stride == 0:
+                stride = 1
+            for chunk in range(CHUNKS):
+
+                @pl.when(step == min(chunk * stride, steps - 1))
+                def _(job=job, own=own, chunk=chunk):
+                    job.start(chunk, *own)
 
     def finish(self, *where):
         for job, own in self.each(*where):
@@ -436,13 +500,15 @@
     shares = row_shares(depth, len(bits))
     jobs = range(len(plan))
     away = [s and not here for _, s, _, here in plan]
-    sides.start(*sides_at)
+    for chunk in range(CHUNKS // 2):
+        sides.start(chunk, *sides_at)
     from_span = {
         job: copies.send(shard_refs[job], slot(job, 0), tensor=span_ranks[plan[job][1] - 1])
         for job in jobs
         if away[job]
     }
-    sides.start_rest(*sides_at)
+    for chunk in range(CHUNKS // 2, CHUNKS):
+        sides.start(chunk, *sides_at)
     over = []
     for ref, out in zip(span_refs, span_outs):
         for s, r in enumerate(span_ranks):
@@ -541,24 +607,25 @@
     return full, came, *sides.results(results[full_count + len(sends) :])
 
 
-def sum_kernel(pairs, sides, steps, *refs):
+def sum_kernel(pairs, own, sides, steps, *refs):
     step = pl.program_id(0)
     count = 2 * pairs + len(sides.operands)
-    out_ref, outs = refs[count], refs[count + 1 : count + 1 + len(sides.out_shapes)]
-    sides_at = (refs[2 * pairs : count], outs, refs[count + 1 + len(sides.out_shapes) :])
+    own_ref, low_ref, outs = refs[count], refs[count + 1], refs[count + 2 :]
+    outs, scratch = outs[: len(sides.out_shapes)], outs[len(sides.out_shapes) :]
+    sides_at = (refs[2 * pairs : count], outs, scratch)
     if sides.jobs:
 
         @pl.when(step == 0)
         def _():
             greet(sides.partners())
-            sides.start(*sides_at)
-            sides.start_rest(*sides_at)
-
+
+    sides.start_over(step, steps, *sides_at)
     total = None
     for i in range(pairs):
         term = nt(refs[2 * i][...], refs[2 * i + 1][...])
         total = term if total is None else total + term
-    out_ref[...] = total.astype(out_ref.dtype)
+    own_ref[...] = total[:own]
+    low_ref[...] = total.astype(LOW)
     if sides.jobs:
 
         @pl.when(step == steps - 1)
@@ -566,113 +633,189 @@
             sides.finish(*sides_at)
 
 
-def product_sum(count, block, pairs, kind, earlier=(), number=None, sides=NO_SIDES):
-    width = pairs[0][1].shape[0]
-    tile = min(512, width)
+def product_sum(parts, pairs, earlier=(), number=None, sides=NO_SIDES):
+    rows, width = pairs[0][0].shape[0], pairs[0][2].shape[0]
+    own = rows // parts
+    tile = min(512 if rows * sum(depth for *_, depth in pairs) < 5 * MIB else 256, width)
     specs, operands, flops = [], [], 0
-    for a, b, run in pairs:
-        depth = a.shape[1]
-        specs.append(pl.BlockSpec((count, depth), lambda j: (block, 0)))
-        specs.append(pl.BlockSpec((tile, depth), lambda j, run=run: (j, run)))
+    for a, a_run, b, b_run, depth in pairs:
+        specs.append(pl.BlockSpec((rows, depth), lambda j, run=a_run: (0, run)))
+        specs.append(pl.BlockSpec((tile, depth), lambda j, run=b_run: (j, run)))
         operands += [a, b]
-        flops += 2 * count * depth * width
+        flops += 2 * rows * depth * width
     hbm = pl.BlockSpec(memory_space=pl.ANY)
-    outs = [jax.ShapeDtypeStruct((count, width), kind)]
-    out_specs = [pl.BlockSpec((count, tile), lambda j: (0, j))]
-    operands += sides.operands
-    specs += [hbm] * len(sides.operands)
-    outs += sides.out_shapes
-    out_specs += [hbm] * len(sides.out_shapes)
     steps = width // tile
     results = call(
-        functools.partial(sum_kernel, len(pairs), sides, steps),
-        operands,
-        specs,
+        functools.partial(sum_kernel, len(pairs), own, sides, steps),
+        [*operands, *sides.operands],
+        [*specs, *[hbm] * len(sides.operands)],
         earlier,
         grid=(steps,),
-        out_specs=out_specs,
-        out_shape=outs,
+        out_specs=[
+            pl.BlockSpec((own, tile), lambda j: (0, j)),
+            pl.BlockSpec((rows, tile), lambda j: (0, j)),
+            *[hbm] * len(sides.out_shapes),
+        ],
+        out_shape=[
+            jax.ShapeDtypeStruct((own, width), F32),
+            jax.ShapeDtypeStruct((rows, width), LOW),
+            *sides.out_shapes,
+        ],
         scratch_shapes=sides.scratch,
         compiler_params=pltpu.CompilerParams(
             vmem_limit_bytes=56 * MIB, **sides.options(number)
         ),
         cost_estimate=pl.CostEstimate(
-            flops=flops, bytes_accessed=flops // count + 4 * count * width, transcendentals=0
+            flops=flops, bytes_accessed=flops // rows + 4 * rows * width, transcendentals=0
         ),
         name="product_sum",
     )
-    return results[0], *sides.results(results[1:])
-
-
-def up_kernel(mixed_ref, gate_weight_ref, up_weight_ref, gate_ref, upper_ref, hidden_ref):
-    gate = nn(mixed_ref[...], gate_weight_ref[...])
-    upper = nn(mixed_ref[...], up_weight_ref[...])
-    gate_ref[...] = gate
-    upper_ref[...] = upper
-    hidden_ref[...] = (gate * jax.nn.sigmoid(gate) * upper).astype(LOW)
-
-
-def feed_up(mixed, gate_up, cols, earlier=()):
+    return *results[:2], *sides.results(results[2:])
+
+
+def up_kernel(spans, tiles, sides, *refs):
+    mixed_ref, weight_refs = refs[0], refs[1 : 1 + 2 * spans]
+    refs = refs[1 + 2 * spans :]
+    side_refs, refs = refs[: len(sides.operands)], refs[len(sides.operands) :]
+    gate_ref, upper_ref, hidden_ref, outs = *refs[:3], refs[3:]
+    outs, scratch = outs[: len(sides.out_shapes)], outs[len(sides.out_shapes) :]
+    sides_at = (side_refs, outs, scratch)
+    step = pl.program_id(0)
+    if sides.jobs:
+
+        @pl.when(step == 0)
+        def _():
+            greet(sides.partners())
+
+    sides.start_over(step, spans * tiles, *sides_at)
+    for s in range(spans):
+
+        @pl.when(jnp.logical_and(step >= s * tiles, step < (s + 1) * tiles))
+        def _(s=s):
+            gate = nn(mixed_ref[...], weight_refs[2 * s][...])
+            upper = nn(mixed_ref[...], weight_refs[2 * s + 1][...])
+            gate_ref[...] = gate
+            upper_ref[...] = upper
+            hidden_ref[...] = (gate * jax.nn.sigmoid(gate) * upper).astype(LOW)
+
+    if sides.jobs:
+
+        @pl.when(step == spans * tiles - 1)
+        def _():
+            sides.finish(*sides_at)
+
+
+def feed_up(mixed, gate_ups, cols, number=None, sides=NO_SIDES):
     rows, depth = mixed.shape
-    (gate_weight, gate_run), (up_weight, up_run) = gate_up
-    tile = min(256, cols)
+    spans = len(gate_ups)
+    tile = min(512, cols)
     tiles = cols // tile
+    hbm = pl.BlockSpec(memory_space=pl.ANY)
     out = pl.BlockSpec((rows, tile), lambda j: (0, j))
-    return call(
-        up_kernel,
-        [mixed, gate_weight, up_weight],
+    operands, specs = [mixed], [pl.BlockSpec((rows, depth), lambda j: (0, 0))]
+    for s, pair in enumerate(gate_ups):
+        for array, run in pair:
+            operands.append(array)
+            specs.append(
+                pl.BlockSpec(
+                    (depth, tile),
+                    lambda j, s=s, run=run: (0, jnp.clip(j - s * tiles, 0, tiles - 1) + run * tiles),
+                )
+            )
+    whole = (rows, spans * cols)
+    results = call(
+        functools.partial(up_kernel, spans, tiles, sides),
+        [*operands, *sides.operands],
+        [*specs, *[hbm] * len(sides.operands)],
+        grid=(spans * tiles,),
+        out_specs=[out, out, out, *[hbm] * len(sides.out_shapes)],
+        out_shape=[
+            jax.ShapeDtypeStruct(whole, F32),
+            jax.ShapeDtypeStruct(whole, F32),
+            jax.ShapeDtypeStruct(whole, LOW),
+            *sides.out_shapes,
+        ],
+        scratch_shapes=sides.scratch,
+        compiler_params=pltpu.CompilerParams(
+            vmem_limit_bytes=56 * MIB, **sides.options(number)
+        ),
+        cost_estimate=pl.CostEstimate(
+            flops=4 * rows * depth * spans * cols,
+            bytes_accessed=4 * depth * spans * cols + 10 * rows * spans * cols,
+            transcendentals=rows * spans * cols,
+        ),
+        name="feed_up",
+    )
+    return *results[:3], *sides.results(results[3:])
+
+
+def up_back_kernel(spans, tiles, sides, *refs):
+    steps = spans * tiles
+    grad_ref, down_refs, refs = refs[0], refs[1 : 1 + spans], refs[1 + spans :]
+    gate_ref, upper_ref, refs = refs[0], refs[1], refs[2:]
+    side_refs, refs = refs[: len(sides.operands)], refs[len(sides.operands) :]
+    gate_out_ref, up_out_ref, outs = refs[0], refs[1], refs[2:]
+    outs, scratch = outs[: len(sides.out_shapes)], outs[len(sides.out_shapes) :]
+    sides_at = (side_refs, outs, scratch)
+    step = pl.program_id(0)
+    if sides.jobs:
+
+        @pl.when(step == 0)
+        def _():
+            greet(sides.partners())
+
+    sides.start_over(step, steps, *sides_at)
+    for s, down_ref in enumerate(down_refs):
+
+        @pl.when(jnp.logical_and(step >= s * tiles, step < (s + 1) * tiles))
+        def _(down_ref=down_ref):
+            grad = nn(grad_ref[...], down_ref[...])
+            gate = gate_ref[...]
+            sigmoid = jax.nn.sigmoid(gate)
+            scaled = grad * sigmoid
+            slope = 1.0 + gate * (1.0 - sigmoid)
+            up_out_ref[...] = (scaled * gate).astype(LOW)
+            gate_out_ref[...] = (scaled * upper_ref[...] * slope).astype(LOW)
+
+    if sides.jobs:
+
+        @pl.when(step == steps - 1)
+        def _():
+            sides.finish(*sides_at)
+
+
+def feed_up_back(grad_rows, down, gate, upper, earlier=(), number=None, sides=NO_SIDES):
+    rows, depth = grad_rows.shape
+    downs, spans = [down], 1
+    tile = min(512, downs[0].shape[1])
+    tiles = downs[0].shape[1] // tile
+    cols = spans * tiles * tile
+    hbm = pl.BlockSpec(memory_space=pl.ANY)
+    spec = pl.BlockSpec((rows, tile), lambda j: (0, j))
+    out = jax.ShapeDtypeStruct((rows, cols), LOW)
+    results = call(
+        functools.partial(up_back_kernel, spans, tiles, sides),
+        [grad_rows, *downs, gate, upper, *sides.operands],
         [
             pl.BlockSpec((rows, depth), lambda j: (0, 0)),
-            pl.BlockSpec((depth, tile), lambda j: (0, j + gate_run * tiles)),
-            pl.BlockSpec((depth, tile), lambda j: (0, j + up_run * tiles)),
-        ],
-        earlier,
-        grid=(tiles,),
-        out_specs=[out, out, out],
-        out_shape=[
-            jax.ShapeDtypeStruct((rows, cols), F32),
-            jax.ShapeDtypeStruct((rows, cols), F32),
-            jax.ShapeDtypeStruct((rows, cols), LOW),
-        ],
-        compiler_params=pltpu.CompilerParams(vmem_limit_bytes=48 * MIB),
-        cost_estimate=pl.CostEstimate(
-            flops=4 * rows * depth * cols,
-            bytes_accessed=4 * depth * cols + 10 * rows * cols,
-            transcendentals=rows * cols,
-        ),
-        name="feed_up",
-    )
-
-
-def up_back_kernel(grad_ref, down_ref, gate_ref, upper_ref, gate_out_ref, up_out_ref):
-    grad = nn(grad_ref[...], down_ref[...])
-    gate = gate_ref[...]
-    sigmoid = jax.nn.sigmoid(gate)
-    scaled = grad * sigmoid
-    up_out_ref[...] = (scaled * gate).astype(LOW)
-    gate_out_ref[...] = (scaled * upper_ref[...] * (1.0 + gate * (1.0 - sigmoid))).astype(LOW)
-
-
-def feed_up_back(grad_rows, down, gate, upper, earlier=()):
-    rows, depth = grad_rows.shape
-    cols = down.shape[1]
-    tile = min(512, cols)
-    spec = pl.BlockSpec((rows, tile), lambda j: (0, j))
-    out = jax.ShapeDtypeStruct((rows, cols), LOW)
-    return call(
-        up_back_kernel,
-        [grad_rows, down, gate, upper],
-        [
-            pl.BlockSpec((rows, depth), lambda j: (0, 0)),
-            pl.BlockSpec((depth, tile), lambda j: (0, j)),
+            *[
+                pl.BlockSpec(
+                    (depth, tile), lambda j, s=s: (0, jnp.clip(j - s * tiles, 0, tiles - 1))
+                )
+                for s in range(spans)
+            ],
             spec,
             spec,
+            *[hbm] * len(sides.operands),
         ],
         earlier,
         grid=(cols // tile,),
-        out_specs=[spec, spec],
-        out_shape=[out, out],
-        compiler_params=pltpu.CompilerParams(vmem_limit_bytes=52 * MIB),
+        out_specs=[spec, spec, *[hbm] * len(sides.out_shapes)],
+        out_shape=[out, out, *sides.out_shapes],
+        scratch_shapes=sides.scratch,
+        compiler_params=pltpu.CompilerParams(
+            vmem_limit_bytes=52 * MIB, **sides.options(number)
+        ),
         cost_estimate=pl.CostEstimate(
             flops=2 * rows * depth * cols,
             bytes_accessed=2 * depth * cols + 12 * rows * cols,
@@ -680,10 +823,13 @@
         ),
         name="feed_up_back",
     )
-
-
-def weight_grad_kernel(fsdp, tiles, sides, *refs):
-    x_ref, grad_refs, refs = refs[0], refs[1 : 1 + len(tiles)], refs[1 + len(tiles) :]
+    return *results[:2], *sides.results(results[2:])
+
+
+def weight_grad_kernel(fsdp, chunks, tiles, sides, *refs):
+    x_refs, refs = refs[:chunks], refs[chunks:]
+    grad_refs, refs = refs[: chunks * len(tiles)], refs[chunks * len(tiles) :]
+    rows = x_refs[0].shape[0]
     count, outs = len(sides.operands), len(sides.out_shapes)
     side_refs, out_ref, refs = refs[:count], refs[count], refs[count + 1 :]
     side_outs, refs = refs[:outs], refs[outs:]
@@ -692,13 +838,23 @@
     me = lax.axis_index("fsdp")
     core = lax.rem(me, 2)
     total_tiles = sum(tiles)
-    depth = x_ref.shape[1] // fsdp
+    depth = x_refs[0].shape[1] // fsdp
     step = pl.program_id(0)
 
     def load(which):
-        for i in range(fsdp // 2):
-            first = pl.multiple_of((2 * i + which) * depth, depth)
-            x_half[:, i * depth : (i + 1) * depth] = x_ref[:, pl.ds(first, depth)]
+        for c, x_ref in enumerate(x_refs):
+            for i in range(fsdp // 2):
+                first = pl.multiple_of((2 * i + which) * depth, depth)
+                x_half[c * rows : (c + 1) * rows, i * depth : (i + 1) * depth] = x_ref[
+                    :, pl.ds(first, depth)
+                ]
+
+    def product(entry):
+        total = None
+        for c, ref in enumerate(grad_refs[entry * chunks : (entry + 1) * chunks]):
+            term = tn(x_half[c * rows : (c + 1) * rows], ref[...])
+            total = term if total is None else total + term
+        return total
 
     def copy(tile):
         slot = lax.rem(tile, 2)
@@ -710,8 +866,8 @@
     def _():
         load(1 - core)
         greet([{"fsdp": flip(me, 1)}, *sides.partners()])
-        sides.start(*sides_at)
-        sides.start_rest(*sides_at)
+
+    sides.start_over(step, 2 * total_tiles, *sides_at)
 
     @pl.when(step == total_tiles)
     def _():
@@ -723,16 +879,16 @@
 
     tile = lax.rem(step, total_tiles)
     first = 0
-    for ref, count in zip(grad_refs, tiles):
+    for entry, count in enumerate(tiles):
         here = jnp.logical_and(tile >= first, tile < first + count)
 
         @pl.when(jnp.logical_and(here, step < total_tiles))
-        def _(ref=ref):
-            sent[lax.rem(step, 2)] = tn(x_half[...], ref[...]).astype(LOW)
+        def _(entry=entry):
+            sent[lax.rem(step, 2)] = product(entry).astype(LOW)
 
         @pl.when(jnp.logical_and(here, step >= total_tiles))
-        def _(ref=ref):
-            total = tn(x_half[...], ref[...])
+        def _(entry=entry):
+            total = product(entry)
             copy(tile).wait_recv()
             out_ref[...] = (total + came[tile].astype(F32)).astype(LOW)
 
@@ -749,28 +905,30 @@
         sides.finish(*sides_at)
 
 
-def weight_grad_half(number, fsdp, x, grads, earlier=(), sides=NO_SIDES):
-    count, width = x.shape
-    tile = math.gcd(1024, *[g.shape[1] for g in grads])
-    tiles = [g.shape[1] // tile for g in grads]
+def weight_grad_half(number, fsdp, xs, grads, earlier=(), sides=NO_SIDES):
+    chunks = len(xs)
+    count, width = xs[0].shape
+    tile = math.gcd(1024, *[cols for _, _, cols in grads])
+    tiles = [cols // tile for _, _, cols in grads]
     total_tiles = sum(tiles)
     firsts = [sum(tiles[:i]) for i in range(len(tiles))]
     cols = tile * total_tiles
 
-    def grad_spec(first, runs):
+    def grad_spec(first, runs, base):
         return pl.BlockSpec(
             (count, tile),
-            lambda j: (0, jnp.clip(lax.rem(j, total_tiles) - first, 0, runs - 1)),
+            lambda j: (0, base + jnp.clip(lax.rem(j, total_tiles) - first, 0, runs - 1)),
         )
 
     hbm = pl.BlockSpec(memory_space=pl.ANY)
-    operands = [x, *grads]
-    specs = [pl.BlockSpec((count, width), lambda j: (0, 0))]
-    specs += [grad_spec(f, c) for f, c in zip(firsts, tiles)]
+    operands = [*xs, *[array for arrays, _, _ in grads for array in arrays]]
+    specs = [pl.BlockSpec((count, width), lambda j: (0, 0))] * chunks
+    for first, runs, (_, start, _) in zip(firsts, tiles, grads):
+        specs += [grad_spec(first, runs, start // tile)] * chunks
     outs = [jax.ShapeDtypeStruct((width // 2, cols), LOW)]
     out_specs = [pl.BlockSpec((width // 2, tile), lambda j: (0, jnp.maximum(j - total_tiles, 0)))]
     scratch = [
-        pltpu.VMEM((count, width // 2), LOW),
+        pltpu.VMEM((chunks * count, width // 2), LOW),
         pltpu.VMEM((2, width // 2, tile), LOW),
         pltpu.VMEM((total_tiles, width // 2, tile), LOW),
         pltpu.SemaphoreType.DMA((2,)),
@@ -782,7 +940,7 @@
     out_specs += [hbm] * len(sides.out_shapes)
     scratch += sides.scratch
     results = call(
-        functools.partial(weight_grad_kernel, fsdp, tiles, sides),
+        functools.partial(weight_grad_kernel, fsdp, chunks, tiles, sides),
         operands,
         specs,
         earlier,
@@ -794,8 +952,8 @@
             collective_id=number, has_side_effects=True, vmem_limit_bytes=56 * MIB
         ),
         cost_estimate=pl.CostEstimate(
-            flops=2 * count * width * cols,
-            bytes_accessed=2 * count * width + 4 * count * cols + width * cols,
+            flops=2 * chunks * count * width * cols,
+            bytes_accessed=chunks * (2 * count * width + 4 * count * cols) + width * cols,
             transcendentals=0,
         ),
         name="weight_grad",
@@ -892,8 +1050,8 @@
         ]
         side_partners = sides.partners()
         greet(partners + side_partners)
-        sides.start(*sides_at)
-        sides.start_rest(*sides_at)
+
+    sides.start_over(step, 2 * tiles, *sides_at)
 
     @pl.when(step == tiles)
     def _():
@@ -1189,14 +1347,6 @@
     def gather_shard(shard):
         return lax.all_gather(shard, "fsdp", axis=0, tiled=True)
 
-    def product_others(pairs, earlier=()):
-        return [product_sum(rows_here, p, pairs, LOW, earlier)[0] for p in range(1, parts)]
-
-    def product_own(number, pairs, others, earlier=()):
-        sides = Sides(Rows(parts, deliver=others))
-        total, came = product_sum(rows_here, 0, pairs, F32, earlier, number, sides)
-        return add_pieces(total, came)
-
     def add_pieces(total, came):
         for piece in came:
             total = total + piece.astype(F32)
@@ -1208,27 +1358,12 @@
             total = total + jnp.roll(to_part(x, p), p * rows_here, axis=0)
         return total
 
-    def sum_all(x):
-        for axis, size in (("fsdp", fsdp), ("tensor", tensor)):
-            bit = 1
-            while bit < size:
-                x = x + lax.ppermute(x, axis, [(i, i ^ bit) for i in range(size)])
-                bit *= 2
-        return x
-
     same_core = [list(range(c, fsdp, 2)) for c in range(2)]
 
     def scatter(total):
         return lax.psum_scatter(
             total, "fsdp", scatter_dimension=0, tiled=True, axis_index_groups=same_core
         )
-
-    def sum_spans(total, weights):
-        split = total.reshape(total.shape[0], weights, spans, -1)
-        result = split[:, :, 0].astype(F32)
-        for s in range(1, spans):
-            result = result + to_span(split[:, :, s], -s).astype(F32)
-        return [result[:, w] for w in range(weights)]
 
     def own_columns(s):
         return ((span + spans - s) % spans * parts + place) * head_cols
@@ -1255,7 +1390,7 @@
         for w, shard in enumerate([query_weight, key_weight, value_weight, out_shard]):
             shards.append(shard)
             plan.append((w // 3, s, w % 3 * spans + s, False))
-    (full_qkv, full_out), _, inputs = exchange(
+    (full_qkv, full_out), (down_came,), inputs = exchange(
         0,
         fsdp,
         parts,
@@ -1263,6 +1398,7 @@
         shards,
         plan,
         sides=Sides(Rows(parts, gather=layer_input)),
+        sends=[down_shard],
     )
     gate_up_first = gather_shard(after(gate_up_shard, inputs))
 
@@ -1283,70 +1419,151 @@
     attended, query_rot, key_rot, lse, gate_came = attend(
         13, rows_here, parts, pre, value_low, invs, gains, tables, sides
     )
-    pairs = [(attended, full_out, 0)]
-    others = product_others(pairs)
+    branch, low = product_sum(parts, [(attended, 0, full_out, 0, full_out.shape[1])])
+    down_shards = jnp.concatenate([down_shard, *[down_came[s - 1] for s in others_spans]], axis=1)
+    gate_up_first, low, down_shards = lax.optimization_barrier((gate_up_first, low, down_shards))
+    full_down = gather_shard(down_shards)
     sides = Sides(
-        Rows(parts, deliver=others),
+        Rows(parts, deliver=low),
         Spans(parts, spans, [(gate_up_shard, 1, cols, spans - s) for s in others_spans]),
     )
     full_gate, _, came, up_came = exchange(
-        1, fsdp, parts, spans, gate_came, [(s - 1, s, 0, True) for s in others_spans], sides
-    )
-    came, down_shard = lax.optimization_barrier((came, down_shard))
-    full_down = [gather_shard(down_shard)]
-    total = product_sum(rows_here, 0, pairs, F32, [*others, gate_up_first])[0]
-    branch = add_pieces(total, came)
+        1, fsdp, parts, spans, gate_came, [(s - 1, s, 0, True) for s in others_spans], sides=sides
+    )
+    branch = add_pieces(branch, came)
     branch_inv = lax.rsqrt(jnp.mean(branch * branch, axis=1, keepdims=True) + EPSILON)
     branch_hat = branch * branch_inv
     middle = layer_input.astype(F32) + branch_hat * attn_gain
-    sides = Sides(
-        Rows(parts, gather=middle.astype(LOW)),
-        Spans(parts, spans, [(down_shard, 0, cols, spans - s) for s in others_spans]),
-    )
-    full_up, _, mixed, down_came = exchange(
-        2, fsdp, parts, spans, up_came, [(s - 1, s, 0, True) for s in others_spans], sides
+    half = rows_here // 2
+    halves = [slice(0, half), slice(half, rows_here)]
+    middle_low = [middle[h].astype(LOW) for h in halves]
+    grad_out = out_cotangent.astype(F32)
+    full_up, _, mixed_first = exchange(
+        2,
+        fsdp,
+        parts,
+        spans,
+        up_came,
+        [(s - 1, s, 0, True) for s in others_spans],
+        sides=Sides(Rows(parts, gather=middle_low[0])),
     )
     full_gate_up = [((gate_up_first, 0), (gate_up_first, 1))]
     full_gate_up += [((gate, 0), (up, 0)) for gate, up in zip(full_gate, full_up)]
-    full_down += [gather_shard(piece) for piece in down_came]
-    gates, uppers, hiddens = zip(
-        *[feed_up(mixed, pair, cols, full_down[:1]) for pair in full_gate_up]
-    )
-    pairs = [(hidden, down, 0) for hidden, down in zip(hiddens, full_down)]
-    second = product_own(3, pairs, product_others(pairs))
-    second_inv = lax.rsqrt(jnp.mean(second * second, axis=1, keepdims=True) + EPSILON)
-    second_hat = second * second_inv
-    output = (middle + second_hat * ffn_gain).astype(LOW)
-
-    grad_out = out_cotangent.astype(F32)
-    ffn_gain_part = jnp.sum(grad_out * second_hat, axis=0)
-    grad_second = norm_back(grad_out * ffn_gain, second_hat, second_inv, width)
-    _, _, grad_rows = exchange(
-        4, fsdp, parts, spans, sides=Sides(Rows(parts, gather=grad_second.astype(LOW)))
-    )
-    (now,) = weight_grad_half(5, fsdp, grad_rows, hiddens)
+    mixed = [mixed_first, None]
+    gates, uppers, hiddens = [None] * 2, [None] * 2, [None] * 2
+    back, outputs, ffn_gain_parts, grad_middles, attn_gain_parts = [None] * 2, [], [], [], []
+
+    def down_pairs(c):
+        return [(hiddens[c], s, full_down, s, cols) for s in range(spans)]
+
+    def up_pairs(c):
+        return [
+            (grad, s, array, run, cols)
+            for s in range(spans)
+            for grad, (array, run) in zip(back[c], full_gate_up[s])
+        ]
+
+    def turn(c, total, came):
+        second = add_pieces(total, came)
+        second_inv = lax.rsqrt(jnp.mean(second * second, axis=1, keepdims=True) + EPSILON)
+        second_hat = second * second_inv
+        outputs.append((middle[halves[c]] + second_hat * ffn_gain).astype(LOW))
+        grad = grad_out[halves[c]]
+        ffn_gain_parts.append(jnp.sum(grad * second_hat, axis=0))
+        return norm_back(grad * ffn_gain, second_hat, second_inv, width).astype(LOW)
+
+    part_cols = cols // 2
+
+    def to_spans(array, run, width):
+        each = array.shape[1] // spans // width
+        return Spans(parts, spans, [(array, s * each + run, width, s) for s in others_spans])
+
+    def back_to_branch(c, total, came):
+        grad_middle = grad_out[halves[c]] + add_pieces(total, came)
+        hat = branch_hat[halves[c]]
+        grad_middles.append(grad_middle)
+        attn_gain_parts.append(jnp.sum(grad_middle * hat, axis=0))
+        return norm_back(grad_middle * attn_gain, hat, branch_inv[halves[c]], width).astype(LOW)
+
+    gates[0], uppers[0], hiddens[0], mixed[1] = feed_up(
+        mixed[0], full_gate_up, cols, 3, Sides(Rows(parts, gather=middle_low[1]))
+    )
+    second_first, low = product_sum(parts, down_pairs(0))
+    gates[1], uppers[1], hiddens[1], came = feed_up(
+        mixed[1], full_gate_up, cols, 4, Sides(Rows(parts, deliver=low))
+    )
+    grad_second = turn(0, second_first, came)
+    second_last, low, grad_rows_first = product_sum(
+        parts, down_pairs(1), [], 5, Sides(Rows(parts, gather=grad_second))
+    )
+    *back[0], came = feed_up_back(
+        grad_rows_first, full_down, gates[0], uppers[0], [], 6, Sides(Rows(parts, deliver=low))
+    )
+    grad_second = turn(1, second_last, came)
+    mixed_grad_first, low, grad_rows_last = product_sum(
+        parts, up_pairs(0), [], 7, Sides(Rows(parts, gather=grad_second))
+    )
+    grad_rows = [grad_rows_first, grad_rows_last]
+    now, came = weight_grad_half(
+        8,
+        fsdp,
+        grad_rows,
+        [(hiddens, 0, spans * cols)],
+        sides=Sides(Rows(parts, deliver=low)),
+    )
     down_terms = scatter(now)
-    back, gate_up_grad = {}, {}
+    grad_branch = back_to_branch(0, mixed_grad_first, came)
+    *back[1], branch_first = feed_up_back(
+        grad_rows_last,
+        full_down,
+        gates[1],
+        uppers[1],
+        [now],
+        9,
+        Sides(Rows(parts, gather=grad_branch)),
+    )
+    mixed_grad_last, low = product_sum(parts, up_pairs(1))
+    backs = list(zip(*back))
+    gate_up_grad = {}
     for s in reversed(range(spans)):
-        back[s] = feed_up_back(grad_rows, full_down[s], gates[s], uppers[s], [now])
-        now = back[s][0]
+        entries = [(list(arrays), s * cols, cols) for arrays in backs]
+        if s == spans - 1:
+            jobs = [Rows(parts, deliver=low)]
+        elif s:
+            jobs = []
+        else:
+            jobs = [Rows(parts, gather=grad_branch), to_spans(down_terms, 0, part_cols)]
+        now, *results = weight_grad_half(10 + s, fsdp, mixed, entries, [now], Sides(*jobs))
         if s:
-            (now,) = weight_grad_half(6, fsdp, mixed, back[s])
             gate_up_grad[s] = scatter(now)
-    pairs = [
-        (grad, *full) for s in range(spans) for grad, full in zip(back[s], full_gate_up[s])
-    ]
-    grad_mixed = product_own(7, pairs, product_others(pairs), [down_terms])
-    grad_middle = grad_out + grad_mixed
-    attn_gain_part = jnp.sum(grad_middle * branch_hat, axis=0)
-    grad_branch = norm_back(grad_middle * attn_gain, branch_hat, branch_inv, width)
-    sides = Sides(
-        Rows(parts, gather=grad_branch.astype(LOW)),
-        Spans(parts, spans, [(down_terms, s, cols, s) for s in others_spans]),
-    )
-    now, grad_branch_rows, down_came = weight_grad_half(8, fsdp, mixed, back[0], sides=sides)
-    gate_up_grad[0] = scatter(now)
+        if s == spans - 1:
+            grad_branch = back_to_branch(1, mixed_grad_last, results[0])
+    branch_last, down_came_first = results
+    output = jnp.concatenate(outputs, axis=0)
+    ffn_gain_part, attn_gain_part = sum(ffn_gain_parts), sum(attn_gain_parts)
+    grad_middle = jnp.concatenate(grad_middles, axis=0)
+    grad_branch_rows = jnp.concatenate(
+        [
+            piece[p * half : (p + 1) * half]
+            for p in range(parts)
+            for piece in (branch_first, branch_last)
+        ],
+        axis=0,
+    )
     grad_attended = nn(grad_branch_rows, full_out).astype(LOW)
+    out_total, down_came_last = weight_grad_half(
+        30,
+        fsdp,
+        [grad_branch_rows],
+        [([attended], 0, attended.shape[1])],
+        [grad_attended],
+        Sides(to_spans(down_terms, 1, part_cols)),
+    )
+    *away, out_total = lax.optimization_barrier(
+        (*[gate_up_grad[s] for s in others_spans], out_total)
+    )
+    gate_up_grad.update(zip(others_spans, away))
+    out_terms = scatter(out_total)
     (
         query_gained,
         key_gained,
@@ -1368,11 +1585,13 @@
         invs,
         gains,
         tables,
-        [],
+        [out_total],
         Sides(Spans(parts, spans, [(gate_up_grad[s], 0, cols, s) for s in others_spans])),
     )
+    out_terms, now, grad_value = lax.optimization_barrier((out_terms, now, grad_value))
+    gate_up_grad[0] = scatter(now)
+    down_came = [jnp.concatenate(pair, axis=1) for pair in zip(down_came_first, down_came_last)]
     down_grad = add_pieces(down_terms[:, :cols].astype(F32), down_came)
-    (out_total,) = weight_grad_half(9, fsdp, grad_branch_rows, [attended], [grad_value])
     inners = sum_parts(jnp.concatenate([query_inner, key_inner], axis=1)) / width
     local_width = value_low.shape[1]
     grad_query = invs[0] * (query_gained - pre[:, :local_width] * invs[0] * inners[:, :1])
@@ -1380,27 +1599,25 @@
     grad_qkv = jnp.concatenate(
         [grad_query.astype(LOW), grad_key.astype(LOW), grad_value], axis=1
     )
-    pairs = [(grad_qkv, full_qkv, 0)]
-    others = product_others(pairs, [out_total, gate_up_grad[0]])
-    others[0], out_total = lax.optimization_barrier((others[0], out_total))
-    out_terms = scatter(out_total)
+    sides = Sides(Spans(parts, spans, [(gate_up_grad[s], 2, part_cols, s) for s in others_spans]))
+    total, low, up_came_first = product_sum(
+        parts, [(grad_qkv, 0, full_qkv, 0, full_qkv.shape[1])], [], 32, sides
+    )
+    gain_parts = [gain_whole(query_gain_part), gain_whole(key_gain_part)]
     sides = Sides(
-        Rows(parts, deliver=others),
-        Spans(parts, spans, [(gate_up_grad[s], 1, cols, s) for s in others_spans]),
-    )
-    qkv_grad, came, up_came = grad_scatter(
-        10, fsdp, parts, spans, inputs, grad_qkv, 3, [], sides
-    )
-    total = product_sum(rows_here, 0, pairs, F32, [qkv_grad])[0]
+        SumAll(fsdp, tensor, jnp.stack([*gain_parts, attn_gain_part, ffn_gain_part])),
+        Rows(parts, deliver=low),
+        Spans(parts, spans, [(out_terms, s, head_cols, s) for s in others_spans]),
+        Spans(parts, spans, [(gate_up_grad[s], 3, part_cols, s) for s in others_spans]),
+    )
+    qkv_grad, gain_grads, came, out_came, up_came_last = grad_scatter(
+        31, fsdp, parts, spans, inputs, grad_qkv, 3, [], sides
+    )
     input_grad = grad_middle + add_pieces(total, came)
+    out_grad = add_pieces(out_terms[:, :head_cols].astype(F32), out_came)
+    up_came = [jnp.concatenate(pair, axis=1) for pair in zip(up_came_first, up_came_last)]
     gate_grad = add_pieces(gate_up_grad[0][:, :cols].astype(F32), gate_came)
     up_grad = add_pieces(gate_up_grad[0][:, cols:].astype(F32), up_came)
-    gain_grads = sum_all(
-        jnp.stack(
-            [gain_whole(query_gain_part), gain_whole(key_gain_part), attn_gain_part, ffn_gain_part]
-        )
-    )
-    (out_grad,) = sum_spans(out_terms, 1)
     query_grad, key_grad, value_grad = jnp.split(qkv_grad, 3, axis=1)
     return (
         output,

time: 1080 us -> 1020 us (0.944)
  Pallas kernels: 919 us -> 862 us
  starting transfers between devices: 30.6 us -> 11.2 us
  other arithmetic: 45.5 us -> 64.6 us
  waiting for transfers between devices: 17.9 us -> 0.17 us
    pallas_call x23 -> x20, Pallas kernels: 900 us -> 842 us  [call(): return pl.pallas_call(body, in_specs=specs, **options)(*operands, *earlier)]
    ppermute x6 -> x0, waiting for transfers between devices: 14.9 us -> none  [the longest x1 11.4 us: to_span(): return lax.ppermute(x, 'tensor', pairs)]
    ppermute x2, starting transfers between devices: 24.1 us -> 10.2 us  [to_part(): return lax.ppermute(x, 'tensor', pairs)]
    unnamed x88 -> x111, local copies, waits for them, and re-layouts: 28.2 us -> 33.6 us
  transfers between devices with their start and end apart: 15 -> 8, of which waited for: 4 -> 0; matrix products, arithmetic and copies ran while one was open for 5% -> 8% of each run, Pallas kernels for 64% -> 59%
where the time goes in v4:
time: 1020 us; the launch traced here: 1010 us
  Pallas kernels  862 us (85%)
  other arithmetic  64.6 us (6%)
  local copies, waits for them, and re-layouts  45.9 us (4%)
  between operations  15.4 us (2%)
  starting transfers between devices  11.2 us (1%)
    pallas_call x20, Pallas kernels, call(): return pl.pallas_call(body, in_specs=specs, **options)(*operands, *earlier)  842 us
    unnamed x111, local copies, waits for them, and re-layouts  33.6 us
  transfers between devices with their start and end apart: 8, of which 0 were waited for; matrix products, arithmetic and copies ran while one was open for 8% of the time, Pallas kernels for 59%

profile of v4, /device:TPU:0, one launch (start us, length us, event | category | flops | bytes accessed | tf_op | source)
XLA Modules:
  0.0 1007.6 jit_solution(17957151945260850658)
XLA Ops:
  12.7 98.2 %exchange.3 = (bf16[8,256,3072]{2,1,0:T(8,128)(2,1)}, bf16[8,256,1024]{2,1,0:T(8,128)(2,1)}, bf16[1,256,2048]{2,1,0:T(8,128)(2,1)}, bf16[2,512,2048]{2,1,0:T(8,128)(2,1)}) custom-call(bf16[512,2048]{1,0:T(8,128)(2,1)} %refs_0_.1, bf16[256,512]{1,0:T(8,128)(2,1)} %refs_5_.1, bf16[256,512]{1,0:T(8,128)(2,1)} %refs_6_.1, bf16[256,512]{1,0:T(8,128)(2,1)} %refs_7_.1, ...), custom_call_target="tpu_custom_call" | custom-call | tf_op jit(solution)/shard_map/exchange/pallas_call | solution.py:197
  111.1 19.4 %project.1 = (f32[1024,2048]{1,0:T(8,128)}, bf16[1024,1024]{1,0:T(8,128)(2,1)S(1)}, f32[1024,1]{1,0:T(8,128)S(1)}, f32[1024,1]{1,0:T(8,128)S(1)}) custom-call(bf16[1024,2048]{1,0:T(8,128)(2,1)} %bitcast.104, bf16[2048,3072]{1,0:T(8,128)(2,1)} %bitcast.102), custom_call_target="tpu_custom_call" | custom-call | flops 12884901888 | bytes 27262976 | tf_op jit(solution)/shard_map/project/pallas_call | solution.py:1196
  132.2 10.1 %collective-permute-start = (f32[1024,2]{0,1:T(2,128)S(1)}, f32[1024,2]{0,1:T(2,128)S(1)}, u32[]{:S(2)}, u32[]{:S(2)}) collective-permute-start(f32[1024,2]{0,1:T(2,128)S(1)} %pad_maximum_fusion.7), channel_id=1, source_target_pairs={{0,1},{1,0},{2,3},{3,2},{4,5},{5,4},{6,7},{7,6},{8,9},{9,8},{10,11... | collective-permute-start | bytes 24584 | tf_op jit(solution)/shard_map/ppermute | solution.py:1337
  151.7 51.2 %attend.1 = (bf16[1024,1024]{1,0:T(8,128)(2,1)S(1)}, bf16[1024,1024]{1,0:T(8,128)(2,1)S(1)}, bf16[1024,1024]{1,0:T(8,128)(2,1)S(1)}, f32[8,1024,1]{2,1,0:T(8,128)}, bf16[256,2048]{1,0:T(8,128)(2,1)S(1)}) custom-call(f32[1024,2048]{1,0:T(8,128)} %get-tuple-element.93.refs_0_.refs_1_.refs_5_.refs_6_, ...), custom_call_target="tpu_custom_call" | custom-call | flops 8589934592 | bytes 16777216 | tf_op jit(solution)/shard_map/attend/pallas_call | solution.py:197
  208.0 8.9 product_sum.6
  221.1 71.1 %exchange.4 = (bf16[8,256,2048]{2,1,0:T(8,128)(2,1)}, bf16[1,512,2048]{2,1,0:T(8,128)(2,1)}, bf16[256,2048]{1,0:T(8,128)(2,1)}) custom-call(bf16[1024,2048]{1,0:T(8,128)(2,1)} %get-tuple-element.103.refs_0_, bf16[256,4096]{1,0:T(8,128)(2,1)} %copy-done, bf16[256,2048]{1,0:T(8,128)(2,1)} %copy-done.2), custom_call_target="tpu_custom_call" | custom-call | tf_op jit(solution)/shard_map/exchange/pallas_call | solution.py:197
  292.2 3.6 multiply_reduce_fusion
  297.0 5.0 multiply_add_fusion
  304.6 63.6 %exchange.5 = (bf16[8,256,2048]{2,1,0:T(8,128)(2,1)}, bf16[2,256,2048]{2,1,0:T(8,128)(2,1)}) custom-call(bf16[256,2048]{1,0:T(8,128)(2,1)} %get-tuple-element.242.refs_0_, bf16[256,2048]{1,0:T(8,128)(2,1)} %get-tuple-element.106.refs_1_), custom_call_target="tpu_custom_call" | custom-call | tf_op jit(solution)/shard_map/exchange/pallas_call | solution.py:197
  368.2 32.7 %feed_up.2 = (f32[512,4096]{1,0:T(8,128)}, f32[512,4096]{1,0:T(8,128)}, bf16[512,4096]{1,0:T(8,128)(2,1)}, bf16[2,256,2048]{2,1,0:T(8,128)(2,1)}) custom-call(bf16[512,2048]{1,0:T(8,128)(2,1)} %bitcast.108, bf16[2048,4096]{1,0:T(8,128)(2,1)} %all-gather.3.cloned.1.call-done.refs_1_.refs_2_.refs_3_, ...), custom_call_target="tpu_custom_call" | custom-call | flops 17179869184 | bytes 54525952 | tf_op jit(solution)/shard_map/feed_up/pallas_call | solution.py:197
  400.9 14.1 %product_sum.7 = (f32[256,2048]{1,0:T(8,128)}, bf16[512,2048]{1,0:T(8,128)(2,1)}) custom-call(bf16[512,4096]{1,0:T(8,128)(2,1)} %get-tuple-element.111.refs_0_.refs_2_, bf16[2048,4096]{1,0:T(8,128)(2,1)} %all-gather.5.cloned.1.call-done.refs_1_.refs_3_, bf16[512,4096]{1,0:T(8,128)(2,1)} %get-tuple-element.111.refs_0_.refs_2_, ...), custom_call_target="tpu_custom_call" | custom-call | flops 8589934592 | bytes 20971520 | tf_op jit(solution)/shard_map/product_sum/pallas_call | solution.py:197
  415.0 32.0 %feed_up.3 = (f32[512,4096]{1,0:T(8,128)}, f32[512,4096]{1,0:T(8,128)}, bf16[512,4096]{1,0:T(8,128)(2,1)}, bf16[1,256,2048]{2,1,0:T(8,128)(2,1)}) custom-call(bf16[512,2048]{1,0:T(8,128)(2,1)} %bitcast.111, bf16[2048,4096]{1,0:T(8,128)(2,1)} %all-gather.3.cloned.1.call-done.refs_1_.refs_2_.refs_3_, ...), custom_call_target="tpu_custom_call" | custom-call | flops 17179869184 | bytes 54525952 | tf_op jit(solution)/shard_map/feed_up/pallas_call | solution.py:197
  451.6 29.8 %product_sum.8 = (f32[256,2048]{1,0:T(8,128)}, bf16[512,2048]{1,0:T(8,128)(2,1)}, bf16[2,256,2048]{2,1,0:T(8,128)(2,1)}) custom-call(bf16[512,4096]{1,0:T(8,128)(2,1)} %get-tuple-element.117.refs_0_.refs_2_.refs_3_, bf16[2048,4096]{1,0:T(8,128)(2,1)} %all-gather.5.cloned.1.call-done.refs_1_.refs_3_, ...), custom_call_target="tpu_custom_call" | custom-call | flops 8589934592 | bytes 20971520 | tf_op jit(solution)/shard_map/product_sum/pallas_call | solution.py:197
  481.4 28.8 %feed_up_back.2 = (bf16[512,4096]{1,0:T(8,128)(2,1)}, bf16[512,4096]{1,0:T(8,128)(2,1)}, bf16[1,256,2048]{2,1,0:T(8,128)(2,1)S(1)}) custom-call(bf16[512,2048]{1,0:T(8,128)(2,1)} %bitcast.93, bf16[2048,4096]{1,0:T(8,128)(2,1)} %all-gather.5.cloned.1.call-done.refs_1_.refs_3_, f32[512,4096]{1,0:T(8,128)} %get-tuple-element.120.refs_2_, ...), custom_call_target="tpu_custom_call" | custom-call | flops 8589934592 | bytes 41943040 | tf_op jit(solution)/shard_map/feed_up_back/pallas_call | solution.py:197
  515.7 31.9 %product_sum.9 = (f32[256,2048]{1,0:T(8,128)}, bf16[512,2048]{1,0:T(8,128)(2,1)}, bf16[2,256,2048]{2,1,0:T(8,128)(2,1)}) custom-call(bf16[512,4096]{1,0:T(8,128)(2,1)} %get-tuple-element.124.refs_0_.refs_4_.refs_2_, bf16[2048,4096]{1,0:T(8,128)(2,1)} %all-gather.3.cloned.1.call-done.refs_1_.refs_2_.refs_3_, ...), custom_call_target="tpu_custom_call" | custom-call | flops 17179869184 | bytes 37748736 | tf_op jit(solution)/shard_map/product_sum/pallas_call | solution.py:197
  547.6 31.5 %weight_grad.4 = (bf16[1024,4096]{1,0:T(8,128)(2,1)}, bf16[1,256,2048]{2,1,0:T(8,128)(2,1)}) custom-call(bf16[512,2048]{1,0:T(8,128)(2,1)} %bitcast.94, bf16[512,2048]{1,0:T(8,128)(2,1)} %bitcast.91, bf16[512,4096]{1,0:T(8,128)(2,1)} %get-tuple-element.111.refs_0_.refs_2_, bf16[512,4096]{1,0:T(8,128)(2,1)} %get-tuple-element.117.refs_0_.refs_2_.refs_3_, ...), custom_call_target="tpu_custom_call" | custom-call | flops 17179869184 | bytes 29360128 | tf_op jit(solution)/shard_map/weight_grad/pallas_call | solution.py:197
  580.6 3.4 multiply_reduce_fusion.4
  585.4 29.4 %feed_up_back.3 = (bf16[512,4096]{1,0:T(8,128)(2,1)}, bf16[512,4096]{1,0:T(8,128)(2,1)}, bf16[2,256,2048]{2,1,0:T(8,128)(2,1)}) custom-call(bf16[512,2048]{1,0:T(8,128)(2,1)} %bitcast.92, bf16[2048,4096]{1,0:T(8,128)(2,1)} %all-gather.5.cloned.1.call-done.refs_1_.refs_3_, f32[512,4096]{1,0:T(8,128)} %get-tuple-element.130.refs_2_, ...), custom_call_target="tpu_custom_call" | custom-call | flops 8589934592 | bytes 41943040 | tf_op jit(solution)/shard_map/feed_up_back/pallas_call | solution.py:197
  614.8 26.1 %product_sum.10 = (f32[256,2048]{1,0:T(8,128)}, bf16[512,2048]{1,0:T(8,128)(2,1)}) custom-call(bf16[512,4096]{1,0:T(8,128)(2,1)} %get-tuple-element.133.refs_0_.refs_4_.refs_3_, bf16[2048,4096]{1,0:T(8,128)(2,1)} %all-gather.3.cloned.1.call-done.refs_1_.refs_2_.refs_3_, bf16[512,4096]{1,0:T(8,128)(2,1)} %get-tuple-element.134.refs_2_.refs_6_.refs_5_, ...), custom_call_target="tpu_custom_call" | custom-call | flops 17179869184 | bytes 37748736 | tf_op jit(solution)/shard_map/product_sum/pallas_call | solution.py:197
  640.9 31.1 %weight_grad.5 = (bf16[1024,4096]{1,0:T(8,128)(2,1)}, bf16[1,256,2048]{2,1,0:T(8,128)(2,1)}) custom-call(bf16[512,2048]{1,0:T(8,128)(2,1)} %bitcast.109, bf16[512,2048]{1,0:T(8,128)(2,1)} %bitcast.112, bf16[512,4096]{1,0:T(8,128)(2,1)} %get-tuple-element.124.refs_0_.refs_4_.refs_2_, bf16[512,4096]{1,0:T(8,128)(2,1)} %get-tuple-element.133.refs_0_.refs_4_.refs_3_, ...), custom_call_target="tpu_custom_call" | custom-call | flops 17179869184 | bytes 29360128 | tf_op jit(solution)/shard_map/weight_grad/pallas_call | solution.py:197
  673.5 3.4 multiply_reduce_fusion.3
  681.7 43.5 %weight_grad.6 = (bf16[1024,4096]{1,0:T(8,128)(2,1)}, bf16[2,256,2048]{2,1,0:T(8,128)(2,1)}, bf16[256,1024]{1,0:T(8,128)(2,1)}) custom-call(bf16[512,2048]{1,0:T(8,128)(2,1)} %bitcast.110, bf16[512,2048]{1,0:T(8,128)(2,1)} %bitcast.113, bf16[512,4096]{1,0:T(8,128)(2,1)} %get-tuple-element.124.refs_0_.refs_4_.refs_2_, ...), custom_call_target="tpu_custom_call" | custom-call | flops 17179869184 | bytes 29360128 | tf_op jit(solution)/shard_map/weight_grad/pallas_call | solution.py:197
  730.7 8.7 convolution_convert_fusion.refs_3_
  739.5 31.8 %weight_grad.7 = (bf16[1024,1024]{1,0:T(8,128)(2,1)}, bf16[256,1024]{1,0:T(8,128)(2,1)}) custom-call(bf16[1024,2048]{1,0:T(8,128)(2,1)} %pad_maximum_fusion.1.refs_0_, bf16[1024,1024]{1,0:T(8,128)(2,1)} %copy-done.11, bf16[256,4096]{1,0:T(8,128)(2,1)} %reduce-scatter.5.cloned.1.call-done.refs_7_.refs_2_, bf16[1024,1024]{1,0:T(8,128)(2,1)} %convolution_convert_fusion.refs_3_), custom_call_target="tpu_custom_call" | custom-call | flops 4294967296 | bytes 10485760 | tf_op jit(solution)/shard_map/weight_grad/pallas_call | solution.py:197
  774.0 50.5 %attend_back.1 = (f32[1024,1024]{1,0:T(8,128)}, f32[1024,1024]{1,0:T(8,128)}, bf16[1024,1024]{1,0:T(8,128)(2,1)}, f32[1,1024]{1,0:T(1,128)S(1)}, f32[1,1024]{1,0...) custom-call(bf16[1024,1024]{1,0:T(8,128)(2,1)} %copy-done.14, ...), custom_call_target="tpu_custom_call" | custom-call | flops 21474836480 | bytes 33554432 | tf_op jit(solution)/shard_map/attend_back/pallas_call | solution.py:197
  829.1 3.6 add_bitcast_fusion
  837.1 7.3 multiply_convert_fusion.1
  844.4 3.0 pad_maximum_fusion.refs_0_.refs_1_
  847.4 31.9 %product_sum.11 = (f32[512,2048]{1,0:T(8,128)}, bf16[1024,2048]{1,0:T(8,128)(2,1)}, bf16[256,1024]{1,0:T(8,128)(2,1)}) custom-call(bf16[1024,3072]{1,0:T(8,128)(2,1)} %pad_maximum_fusion.refs_0_.refs_1_, bf16[2048,3072]{1,0:T(8,128)(2,1)} %bitcast.103, bf16[256,4096]{1,0:T(8,128)(2,1)} %reduce-scatter.7.cloned.1.call-done.refs_13_.refs_2_.refs_5_), custom_call_target="tpu_custom_call" | custom-call | flops 12884901888 | bytes 20971520 | tf_op jit(solution)/shard_map/product_sum/pallas_call | solution.py:197
  879.3 104.4 %grad_scatter.1 = (f32[256,1536]{1,0:T(8,128)}, f32[4,2048]{1,0:T(4,128)}, bf16[1,512,2048]{2,1,0:T(8,128)(2,1)}, bf16[256,512]{1,0:T(8,128)(2,1)}, bf16[256,1024]{1,0:T(8,128)(2,1)}) custom-call(bf16[1024,2048]{1,0:T(8,128)(2,1)} %bitcast.105, bf16[1024,3072]{1,0:T(8,128)(2,1)} %pad_maximum_fusion.refs_0_.refs_1_, f32[4,2048]{1,0:T(4,128)} %pad_maximum_fusion.6.refs_2_, ...), custom_call_target="tpu_custom_call" | custom-call | flops 12884901888 | bytes 16777216 | tf_op jit(solution)/shard_map/grad_scatter/pallas_call | solution.py:197
  989.1 6.9 maximum_add_fusion
  996.0 4.3 convert_add_fusion.6
  (192 shorter events, 71.2 us)
Async XLA Ops:
  7.2 4.2 copy-start.37
  7.2 209.8 %all-gather.3.cloned.1.call-start = ((), (), s32[]{:S(2)}) async-start(), calls=%async_computation.4 | async-start | bytes 18874368 | tf_op jit(solution)/shard_map/all_gather | solution.py:1348
  12.7 98.2 %copy-start = (bf16[256,4096]{1,0:T(8,128)(2,1)}, bf16[256,4096]{1,0:T(8,128)(2,1)S(1)}, u32[]{:S(2)}) copy-start(bf16[256,4096]{1,0:T(8,128)(2,1)S(1)} %constant_dynamic-update-slice_fusion.refs_9_.refs_1_) | copy-start | bytes 6291460
  111.0 290.0 %all-gather.5.cloned.1.call-start = ((), (), s32[]{:S(2)}) async-start(), calls=%async_computation.5 | async-start | bytes 18874368 | tf_op jit(solution)/shard_map/all_gather | solution.py:1348
  111.0 31.3 %copy-start.50 = (f32[2048]{0:T(1024)S(1)}, f32[2048]{0:T(1024)}, u32[]{:S(2)}) copy-start(f32[2048]{0:T(1024)} %param.21) | copy-start | bytes 24580
  111.0 31.4 %copy-start.51 = (f32[2048]{0:T(1024)S(1)}, f32[2048]{0:T(1024)}, u32[]{:S(2)}) copy-start(f32[2048]{0:T(1024)} %param.22) | copy-start | bytes 24580
  132.2 14.3 %collective-permute-start = (f32[1024,2]{0,1:T(2,128)S(1)}, f32[1024,2]{0,1:T(2,128)S(1)}, u32[]{:S(2)}, u32[]{:S(2)}) collective-permute-start(f32[1024,2]{0,1:T(2,128)S(1)} %pad_maximum_fusion.7), channel_id=1, source_target_pairs={{0,1},{1,0},{2,3},{3,2},{4,5},{5,4},{6,7},{7,6},{8,9},{9,8},{10,11... | collective-permute-start | bytes 24584 | tf_op jit(solution)/shard_map/ppermute | solution.py:1337
  142.5 7.2 copy-start.7
  146.4 3.3 copy-start.1
  146.5 56.5 %copy-start.9 = (f32[1024]{0:T(1024)}, f32[1024]{0:T(1024)S(1)}, u32[]{:S(2)}) copy-start(f32[1024]{0:T(1024)S(1)} %pad_maximum_fusion.10) | copy-start | bytes 12292
  149.8 53.2 %copy-start.3 = (f32[1024,1]{1,0:T(8,128)}, f32[1024,1]{1,0:T(8,128)S(1)}, u32[]{:S(2)}) copy-start(f32[1024,1]{1,0:T(8,128)S(1)} %get-tuple-element.253.refs_4_.refs_8_) | copy-start | bytes 12292
  149.8 53.2 %copy-start.5 = (f32[1024,1]{1,0:T(8,128)}, f32[1024,1]{1,0:T(8,128)S(1)}, u32[]{:S(2)}) copy-start(f32[1024,1]{1,0:T(8,128)S(1)} %get-tuple-element.254.refs_3_.refs_7_) | copy-start | bytes 12292
  217.0 464.7 %reduce-scatter.5.cloned.1.call-start = ((), (), s32[]{:S(2)}) async-start(), calls=%async_computation.6 | async-start | bytes 10485760 | tf_op jit(solution)/shard_map/reduce_scatter | solution.py:1364
  221.1 74.8 %copy-start.42 = (f32[2048]{0:T(1024)S(1)}, f32[2048]{0:T(1024)}, u32[]{:S(2)}) copy-start(f32[2048]{0:T(1024)} %param.23) | copy-start | bytes 24580
  292.2 4.1 copy-start.26
  292.2 4.8 copy-start.30
  415.0 32.0 %copy-start.19 = (f32[256,2048]{1,0:T(8,128)S(1)}, f32[256,2048]{1,0:T(8,128)}, u32[]{:S(2)}) copy-start(f32[256,2048]{1,0:T(8,128)} %get-tuple-element.113) | copy-start | bytes 6291460
  415.0 33.7 %copy-start.16 = (f32[512,2048]{1,0:T(8,128)S(1)}, f32[512,2048]{1,0:T(8,128)}, u32[]{:S(2)}) copy-start(f32[512,2048]{1,0:T(8,128)} %convert_element_type.123) | copy-start | bytes 12582916
  481.4 28.8 %copy-start.25 = (f32[256,2048]{1,0:T(8,128)S(1)}, f32[256,2048]{1,0:T(8,128)}, u32[]{:S(2)}) copy-start(f32[256,2048]{1,0:T(8,128)} %get-tuple-element.118) | copy-start | bytes 6291460
  579.1 192.2 %reduce-scatter.7.cloned.1.call-start = ((), (), s32[]{:S(2)}) async-start(), calls=%async_computation.7 | async-start | bytes 10485760 | tf_op jit(solution)/shard_map/reduce_scatter | solution.py:1364
  580.6 3.8 copy-start.17
  672.0 152.5 %reduce-scatter.9.cloned.1.call-start = ((), (), s32[]{:S(2)}) async-start(), calls=%async_computation.8 | async-start | bytes 2621440 | tf_op jit(solution)/shard_map/reduce_scatter | solution.py:1364
  673.5 3.4 copy-start.35
  727.0 3.7 copy-start.52
  771.3 224.7 %reduce-scatter.11.cloned.1.call-start = ((), (), s32[]{:S(2)}) async-start(), calls=%async_computation.9 | async-start | bytes 10485760 | tf_op jit(solution)/shard_map/reduce_scatter | solution.py:1364
  828.9 7.3 collective-permute-start.1
  837.1 7.3 copy-start.36
  879.3 104.4 %copy-start.44 = (bf16[256,1024]{1,0:T(8,128)(2,1)S(1)}, bf16[256,1024]{1,0:T(8,128)(2,1)}, u32[]{:S(2)}) copy-start(bf16[256,1024]{1,0:T(8,128)(2,1)} %reduce-scatter.9.cloned.1.call-done.refs_4_) | copy-start | bytes 1572868
  984.8 3.7 copy-start.47
  985.8 3.3 copy-start.23
  989.1 6.9 copy-start.40
  989.1 6.9 copy-start.41
  (29 other events, 43.5 us)
Sparse Core Ops, SparseCore 0:
  111.1 97.5 all-gather.2
  217.1 124.8 all-gather.4
  579.2 85.0 reduce-scatter.4
  672.1 85.9 reduce-scatter.6
  771.4 33.9 reduce-scatter.8
  824.7 97.2 reduce-scatter.10

commit v5 on v4

--- a/solution.py
+++ b/solution.py
@@ -607,12 +607,13 @@
     return full, came, *sides.results(results[full_count + len(sends) :])
 
 
-def sum_kernel(pairs, own, sides, steps, *refs):
+def sum_kernel(pairs, own, has_addend, sides, steps, *refs):
     step = pl.program_id(0)
-    count = 2 * pairs + len(sides.operands)
+    first_side = 2 * pairs + has_addend
+    count = first_side + len(sides.operands)
     own_ref, low_ref, outs = refs[count], refs[count + 1], refs[count + 2 :]
     outs, scratch = outs[: len(sides.out_shapes)], outs[len(sides.out_shapes) :]
-    sides_at = (refs[2 * pairs : count], outs, scratch)
+    sides_at = (refs[first_side:count], outs, scratch)
     if sides.jobs:
 
         @pl.when(step == 0)
@@ -624,7 +625,7 @@
     for i in range(pairs):
         term = nt(refs[2 * i][...], refs[2 * i + 1][...])
         total = term if total is None else total + term
-    own_ref[...] = total[:own]
+    own_ref[...] = total[:own] + refs[2 * pairs][...] if has_addend else total[:own]
     low_ref[...] = total.astype(LOW)
     if sides.jobs:
 
@@ -633,7 +634,7 @@
             sides.finish(*sides_at)
 
 
-def product_sum(parts, pairs, earlier=(), number=None, sides=NO_SIDES):
+def product_sum(parts, pairs, earlier=(), number=None, sides=NO_SIDES, addend=None):
     rows, width = pairs[0][0].shape[0], pairs[0][2].shape[0]
     own = rows // parts
     tile = min(512 if rows * sum(depth for *_, depth in pairs) < 5 * MIB else 256, width)
@@ -643,10 +644,13 @@
         specs.append(pl.BlockSpec((tile, depth), lambda j, run=b_run: (j, run)))
         operands += [a, b]
         flops += 2 * rows * depth * width
+    if addend is not None:
+        specs.append(pl.BlockSpec((own, tile), lambda j: (0, j)))
+        operands.append(addend)
     hbm = pl.BlockSpec(memory_space=pl.ANY)
     steps = width // tile
     results = call(
-        functools.partial(sum_kernel, len(pairs), own, sides, steps),
+        functools.partial(sum_kernel, len(pairs), own, addend is not None, sides, steps),
         [*operands, *sides.operands],
         [*specs, *[hbm] * len(sides.operands)],
         earlier,
@@ -1438,18 +1442,17 @@
     halves = [slice(0, half), slice(half, rows_here)]
     middle_low = [middle[h].astype(LOW) for h in halves]
     grad_out = out_cotangent.astype(F32)
-    full_up, _, mixed_first = exchange(
+    full_up, _, *mixed = exchange(
         2,
         fsdp,
         parts,
         spans,
         up_came,
         [(s - 1, s, 0, True) for s in others_spans],
-        sides=Sides(Rows(parts, gather=middle_low[0])),
+        sides=Sides(*[Rows(parts, gather=rows) for rows in middle_low]),
     )
     full_gate_up = [((gate_up_first, 0), (gate_up_first, 1))]
     full_gate_up += [((gate, 0), (up, 0)) for gate, up in zip(full_gate, full_up)]
-    mixed = [mixed_first, None]
     gates, uppers, hiddens = [None] * 2, [None] * 2, [None] * 2
     back, outputs, ffn_gain_parts, grad_middles, attn_gain_parts = [None] * 2, [], [], [], []
 
@@ -1485,9 +1488,7 @@
         attn_gain_parts.append(jnp.sum(grad_middle * hat, axis=0))
         return norm_back(grad_middle * attn_gain, hat, branch_inv[halves[c]], width).astype(LOW)
 
-    gates[0], uppers[0], hiddens[0], mixed[1] = feed_up(
-        mixed[0], full_gate_up, cols, 3, Sides(Rows(parts, gather=middle_low[1]))
-    )
+    gates[0], uppers[0], hiddens[0] = feed_up(mixed[0], full_gate_up, cols)
     second_first, low = product_sum(parts, down_pairs(0))
     gates[1], uppers[1], hiddens[1], came = feed_up(
         mixed[1], full_gate_up, cols, 4, Sides(Rows(parts, deliver=low))
@@ -1513,16 +1514,10 @@
     )
     down_terms = scatter(now)
     grad_branch = back_to_branch(0, mixed_grad_first, came)
-    *back[1], branch_first = feed_up_back(
-        grad_rows_last,
-        full_down,
-        gates[1],
-        uppers[1],
-        [now],
-        9,
-        Sides(Rows(parts, gather=grad_branch)),
-    )
-    mixed_grad_last, low = product_sum(parts, up_pairs(1))
+    back[1] = feed_up_back(grad_rows_last, full_down, gates[1], uppers[1], [now])
+    mixed_grad_last, low, branch_first = product_sum(
+        parts, up_pairs(1), [], 9, Sides(Rows(parts, gather=grad_branch))
+    )
     backs = list(zip(*back))
     gate_up_grad = {}
     for s in reversed(range(spans)):
@@ -1601,7 +1596,12 @@
     )
     sides = Sides(Spans(parts, spans, [(gate_up_grad[s], 2, part_cols, s) for s in others_spans]))
     total, low, up_came_first = product_sum(
-        parts, [(grad_qkv, 0, full_qkv, 0, full_qkv.shape[1])], [], 32, sides
+        parts,
+        [(grad_qkv, 0, full_qkv, 0, full_qkv.shape[1])],
+        [],
+        32,
+        sides,
+        grad_middle,
     )
     gain_parts = [gain_whole(query_gain_part), gain_whole(key_gain_part)]
     sides = Sides(
@@ -1613,7 +1613,7 @@
     qkv_grad, gain_grads, came, out_came, up_came_last = grad_scatter(
         31, fsdp, parts, spans, inputs, grad_qkv, 3, [], sides
     )
-    input_grad = grad_middle + add_pieces(total, came)
+    input_grad = add_pieces(total, came)
     out_grad = add_pieces(out_terms[:, :head_cols].astype(F32), out_came)
     up_came = [jnp.concatenate(pair, axis=1) for pair in zip(up_came_first, up_came_last)]
     gate_grad = add_pieces(gate_up_grad[0][:, :cols].astype(F32), gate_came)

time: 1020 us -> 1010 us (level)
    unnamed x111 -> x119, local copies, waits for them, and re-layouts: 33.6 us -> 33.5 us
where the time goes in v5:
time: 1010 us; the launch traced here: 1000 us
  Pallas kernels  857 us (85%)
  other arithmetic  65.8 us (7%)
  local copies, waits for them, and re-layouts  45.7 us (5%)
  between operations  15.4 us (2%)
  starting transfers between devices  11.2 us (1%)
    pallas_call x20, Pallas kernels, call(): return pl.pallas_call(body, in_specs=specs, **options)(*operands, *earlier)  838 us
    unnamed x119, local copies, waits for them, and re-layouts  33.5 us
  transfers between devices with their start and end apart: 8, of which 0 were waited for; matrix products, arithmetic and copies ran while one was open for 8% of the time, Pallas kernels for 59%

profile of v5, /device:TPU:0, one launch (start us, length us, event | category | flops | bytes accessed | tf_op | source)
XLA Modules:
  0.0 1004.0 jit_solution(14565999743815187715)
XLA Ops:
  12.7 98.2 %exchange.3 = (bf16[8,256,3072]{2,1,0:T(8,128)(2,1)}, bf16[8,256,1024]{2,1,0:T(8,128)(2,1)}, bf16[1,256,2048]{2,1,0:T(8,128)(2,1)}, bf16[2,512,2048]{2,1,0:T(8,128)(2,1)}) custom-call(bf16[512,2048]{1,0:T(8,128)(2,1)} %refs_0_.1, bf16[256,512]{1,0:T(8,128)(2,1)} %refs_5_.1, bf16[256,512]{1,0:T(8,128)(2,1)} %refs_6_.1, bf16[256,512]{1,0:T(8,128)(2,1)} %refs_7_.1, ...), custom_call_target="tpu_custom_call" | custom-call | tf_op jit(solution)/shard_map/exchange/pallas_call | solution.py:197
  111.1 19.4 %project.1 = (f32[1024,2048]{1,0:T(8,128)}, bf16[1024,1024]{1,0:T(8,128)(2,1)S(1)}, f32[1024,1]{1,0:T(8,128)S(1)}, f32[1024,1]{1,0:T(8,128)S(1)}) custom-call(bf16[1024,2048]{1,0:T(8,128)(2,1)} %bitcast.104, bf16[2048,3072]{1,0:T(8,128)(2,1)} %bitcast.102), custom_call_target="tpu_custom_call" | custom-call | flops 12884901888 | bytes 27262976 | tf_op jit(solution)/shard_map/project/pallas_call | solution.py:1200
  132.2 10.1 %collective-permute-start = (f32[1024,2]{0,1:T(2,128)S(1)}, f32[1024,2]{0,1:T(2,128)S(1)}, u32[]{:S(2)}, u32[]{:S(2)}) collective-permute-start(f32[1024,2]{0,1:T(2,128)S(1)} %pad_maximum_fusion.8), channel_id=1, source_target_pairs={{0,1},{1,0},{2,3},{3,2},{4,5},{5,4},{6,7},{7,6},{8,9},{9,8},{10,11... | collective-permute-start | bytes 24584 | tf_op jit(solution)/shard_map/ppermute | solution.py:1341
  151.7 51.2 %attend.1 = (bf16[1024,1024]{1,0:T(8,128)(2,1)S(1)}, bf16[1024,1024]{1,0:T(8,128)(2,1)S(1)}, bf16[1024,1024]{1,0:T(8,128)(2,1)S(1)}, f32[8,1024,1]{2,1,0:T(8,128)}, bf16[256,2048]{1,0:T(8,128)(2,1)S(1)}) custom-call(f32[1024,2048]{1,0:T(8,128)} %get-tuple-element.93.refs_0_.refs_1_.refs_5_.refs_6_, ...), custom_call_target="tpu_custom_call" | custom-call | flops 8589934592 | bytes 16777216 | tf_op jit(solution)/shard_map/attend/pallas_call | solution.py:197
  208.0 8.9 product_sum.6
  221.0 71.1 %exchange.4 = (bf16[8,256,2048]{2,1,0:T(8,128)(2,1)}, bf16[1,512,2048]{2,1,0:T(8,128)(2,1)}, bf16[256,2048]{1,0:T(8,128)(2,1)}) custom-call(bf16[1024,2048]{1,0:T(8,128)(2,1)} %get-tuple-element.103.refs_0_, bf16[256,4096]{1,0:T(8,128)(2,1)} %copy-done, bf16[256,2048]{1,0:T(8,128)(2,1)} %copy-done.2), custom_call_target="tpu_custom_call" | custom-call | tf_op jit(solution)/shard_map/exchange/pallas_call | solution.py:197
  292.2 3.6 multiply_reduce_fusion
  297.0 5.0 multiply_add_fusion
  304.6 64.7 %exchange.5 = (bf16[8,256,2048]{2,1,0:T(8,128)(2,1)}, bf16[2,256,2048]{2,1,0:T(8,128)(2,1)}, bf16[2,256,2048]{2,1,0:T(8,128)(2,1)}) custom-call(bf16[256,2048]{1,0:T(8,128)(2,1)} %get-tuple-element.242.refs_0_, bf16[256,2048]{1,0:T(8,128)(2,1)} %get-tuple-element.241.refs_1_, bf16[256,2048]{1,0:T(8,128)(2,1)} %get-tuple-element.106.refs_2_), custom_call_target="tpu_custom_call" | custom-call | tf_op jit(solution)/shard_map/exchange/pallas_call | solution.py:197
  369.3 27.9 %feed_up.2 = (f32[512,4096]{1,0:T(8,128)}, f32[512,4096]{1,0:T(8,128)}, bf16[512,4096]{1,0:T(8,128)(2,1)}) custom-call(bf16[512,2048]{1,0:T(8,128)(2,1)} %bitcast.108, bf16[2048,4096]{1,0:T(8,128)(2,1)} %all-gather.3.cloned.1.call-done.refs_1_.refs_2_.refs_3_, bf16[2048,4096]{1,0:T(8,128)(2,1)} %all-gather.3.cloned.1.call-done.refs_1_.refs_2_.refs_3_, ...), custom_call_target="tpu_custom_call" | custom-call | flops 17179869184 | bytes 54525952 | tf_op jit(solution)/shard_map/feed_up/pallas_call | solution.py:197
  397.3 14.1 %product_sum.7 = (f32[256,2048]{1,0:T(8,128)}, bf16[512,2048]{1,0:T(8,128)(2,1)}) custom-call(bf16[512,4096]{1,0:T(8,128)(2,1)} %get-tuple-element.111.refs_0_.refs_2_, bf16[2048,4096]{1,0:T(8,128)(2,1)} %all-gather.5.cloned.1.call-done.refs_1_.refs_3_, bf16[512,4096]{1,0:T(8,128)(2,1)} %get-tuple-element.111.refs_0_.refs_2_, ...), custom_call_target="tpu_custom_call" | custom-call | flops 8589934592 | bytes 20971520 | tf_op jit(solution)/shard_map/product_sum/pallas_call | solution.py:197
  411.4 32.7 %feed_up.3 = (f32[512,4096]{1,0:T(8,128)}, f32[512,4096]{1,0:T(8,128)}, bf16[512,4096]{1,0:T(8,128)(2,1)}, bf16[1,256,2048]{2,1,0:T(8,128)(2,1)}) custom-call(bf16[512,2048]{1,0:T(8,128)(2,1)} %bitcast.111, bf16[2048,4096]{1,0:T(8,128)(2,1)} %all-gather.3.cloned.1.call-done.refs_1_.refs_2_.refs_3_, ...), custom_call_target="tpu_custom_call" | custom-call | flops 17179869184 | bytes 54525952 | tf_op jit(solution)/shard_map/feed_up/pallas_call | solution.py:197
  448.7 30.0 %product_sum.8 = (f32[256,2048]{1,0:T(8,128)}, bf16[512,2048]{1,0:T(8,128)(2,1)}, bf16[2,256,2048]{2,1,0:T(8,128)(2,1)}) custom-call(bf16[512,4096]{1,0:T(8,128)(2,1)} %get-tuple-element.117.refs_0_.refs_2_.refs_3_, bf16[2048,4096]{1,0:T(8,128)(2,1)} %all-gather.5.cloned.1.call-done.refs_1_.refs_3_, ...), custom_call_target="tpu_custom_call" | custom-call | flops 8589934592 | bytes 20971520 | tf_op jit(solution)/shard_map/product_sum/pallas_call | solution.py:197
  478.7 29.2 %feed_up_back.2 = (bf16[512,4096]{1,0:T(8,128)(2,1)}, bf16[512,4096]{1,0:T(8,128)(2,1)}, bf16[1,256,2048]{2,1,0:T(8,128)(2,1)S(1)}) custom-call(bf16[512,2048]{1,0:T(8,128)(2,1)} %bitcast.91, bf16[2048,4096]{1,0:T(8,128)(2,1)} %all-gather.5.cloned.1.call-done.refs_1_.refs_3_, f32[512,4096]{1,0:T(8,128)} %get-tuple-element.120.refs_2_, ...), custom_call_target="tpu_custom_call" | custom-call | flops 8589934592 | bytes 41943040 | tf_op jit(solution)/shard_map/feed_up_back/pallas_call | solution.py:197
  513.4 31.9 %product_sum.9 = (f32[256,2048]{1,0:T(8,128)}, bf16[512,2048]{1,0:T(8,128)(2,1)}, bf16[2,256,2048]{2,1,0:T(8,128)(2,1)}) custom-call(bf16[512,4096]{1,0:T(8,128)(2,1)} %get-tuple-element.126.refs_0_.refs_4_.refs_2_, bf16[2048,4096]{1,0:T(8,128)(2,1)} %all-gather.3.cloned.1.call-done.refs_1_.refs_2_.refs_3_, ...), custom_call_target="tpu_custom_call" | custom-call | flops 17179869184 | bytes 37748736 | tf_op jit(solution)/shard_map/product_sum/pallas_call | solution.py:197
  545.3 31.5 %weight_grad.4 = (bf16[1024,4096]{1,0:T(8,128)(2,1)}, bf16[1,256,2048]{2,1,0:T(8,128)(2,1)}) custom-call(bf16[512,2048]{1,0:T(8,128)(2,1)} %bitcast.92, bf16[512,2048]{1,0:T(8,128)(2,1)} %bitcast.93, bf16[512,4096]{1,0:T(8,128)(2,1)} %get-tuple-element.111.refs_0_.refs_2_, bf16[512,4096]{1,0:T(8,128)(2,1)} %get-tuple-element.117.refs_0_.refs_2_.refs_3_, ...), custom_call_target="tpu_custom_call" | custom-call | flops 17179869184 | bytes 29360128 | tf_op jit(solution)/shard_map/weight_grad/pallas_call | solution.py:197
  578.4 3.4 multiply_reduce_fusion.4
  583.8 21.0 %feed_up_back.3 = (bf16[512,4096]{1,0:T(8,128)(2,1)}, bf16[512,4096]{1,0:T(8,128)(2,1)}) custom-call(bf16[512,2048]{1,0:T(8,128)(2,1)} %bitcast.94, bf16[2048,4096]{1,0:T(8,128)(2,1)} %all-gather.5.cloned.1.call-done.refs_1_.refs_3_, f32[512,4096]{1,0:T(8,128)} %get-tuple-element.129.refs_2_, f32[512,4096]{1,0:T(8,128)} %get-tuple-element.130.refs_3_, ...), custom_call_target="tpu_custom_call" | custom-call | flops 8589934592 | bytes 41943040 | tf_op jit(solution)/shard_map/feed_up_back/pallas_call | solution.py:197
  604.7 33.4 %product_sum.10 = (f32[256,2048]{1,0:T(8,128)}, bf16[512,2048]{1,0:T(8,128)(2,1)}, bf16[2,256,2048]{2,1,0:T(8,128)(2,1)}) custom-call(bf16[512,4096]{1,0:T(8,128)(2,1)} %get-tuple-element.133.refs_0_.refs_4_.refs_3_, bf16[2048,4096]{1,0:T(8,128)(2,1)} %all-gather.3.cloned.1.call-done.refs_1_.refs_2_.refs_3_, ...), custom_call_target="tpu_custom_call" | custom-call | flops 17179869184 | bytes 37748736 | tf_op jit(solution)/shard_map/product_sum/pallas_call | solution.py:197
  638.1 31.2 %weight_grad.5 = (bf16[1024,4096]{1,0:T(8,128)(2,1)}, bf16[1,256,2048]{2,1,0:T(8,128)(2,1)}) custom-call(bf16[512,2048]{1,0:T(8,128)(2,1)} %bitcast.109, bf16[512,2048]{1,0:T(8,128)(2,1)} %bitcast.112, bf16[512,4096]{1,0:T(8,128)(2,1)} %get-tuple-element.126.refs_0_.refs_4_.refs_2_, bf16[512,4096]{1,0:T(8,128)(2,1)} %get-tuple-element.133.refs_0_.refs_4_.refs_3_, ...), custom_call_target="tpu_custom_call" | custom-call | flops 17179869184 | bytes 29360128 | tf_op jit(solution)/shard_map/weight_grad/pallas_call | solution.py:197
  670.9 3.4 multiply_reduce_fusion.3
  679.2 43.4 %weight_grad.6 = (bf16[1024,4096]{1,0:T(8,128)(2,1)}, bf16[2,256,2048]{2,1,0:T(8,128)(2,1)}, bf16[256,1024]{1,0:T(8,128)(2,1)}) custom-call(bf16[512,2048]{1,0:T(8,128)(2,1)} %bitcast.110, bf16[512,2048]{1,0:T(8,128)(2,1)} %bitcast.113, bf16[512,4096]{1,0:T(8,128)(2,1)} %get-tuple-element.126.refs_0_.refs_4_.refs_2_, ...), custom_call_target="tpu_custom_call" | custom-call | flops 17179869184 | bytes 29360128 | tf_op jit(solution)/shard_map/weight_grad/pallas_call | solution.py:197
  728.1 8.7 convolution_convert_fusion.refs_3_
  736.8 31.5 %weight_grad.7 = (bf16[1024,1024]{1,0:T(8,128)(2,1)}, bf16[256,1024]{1,0:T(8,128)(2,1)}) custom-call(bf16[1024,2048]{1,0:T(8,128)(2,1)} %pad_maximum_fusion.1.refs_0_, bf16[1024,1024]{1,0:T(8,128)(2,1)} %copy-done.11, bf16[256,4096]{1,0:T(8,128)(2,1)} %reduce-scatter.5.cloned.1.call-done.refs_7_.refs_2_, bf16[1024,1024]{1,0:T(8,128)(2,1)} %convolution_convert_fusion.refs_3_), custom_call_target="tpu_custom_call" | custom-call | flops 4294967296 | bytes 10485760 | tf_op jit(solution)/shard_map/weight_grad/pallas_call | solution.py:197
  771.2 51.0 %attend_back.1 = (f32[1024,1024]{1,0:T(8,128)}, f32[1024,1024]{1,0:T(8,128)}, bf16[1024,1024]{1,0:T(8,128)(2,1)}, f32[1,1024]{1,0:T(1,128)S(1)}, f32[1,1024]{1,0...) custom-call(bf16[1024,1024]{1,0:T(8,128)(2,1)} %copy-done.14, ...), custom_call_target="tpu_custom_call" | custom-call | flops 21474836480 | bytes 33554432 | tf_op jit(solution)/shard_map/attend_back/pallas_call | solution.py:197
  833.0 3.0 copy.57
  836.9 7.3 multiply_convert_fusion.1
  844.2 3.0 pad_maximum_fusion.refs_0_.refs_1_
  847.2 32.0 %product_sum.11 = (f32[512,2048]{1,0:T(8,128)}, bf16[1024,2048]{1,0:T(8,128)(2,1)}, bf16[256,1024]{1,0:T(8,128)(2,1)}) custom-call(bf16[1024,3072]{1,0:T(8,128)(2,1)} %pad_maximum_fusion.refs_0_.refs_1_, bf16[2048,3072]{1,0:T(8,128)(2,1)} %bitcast.103, f32[512,2048]{1,0:T(8,128)} %pad_maximum_fusion.2.refs_2_, ...), custom_call_target="tpu_custom_call" | custom-call | flops 12884901888 | bytes 20971520 | tf_op jit(solution)/shard_map/product_sum/pallas_call | solution.py:197
  879.2 102.6 %grad_scatter.1 = (f32[256,1536]{1,0:T(8,128)}, f32[4,2048]{1,0:T(4,128)}, bf16[1,512,2048]{2,1,0:T(8,128)(2,1)}, bf16[256,512]{1,0:T(8,128)(2,1)}, bf16[256,1024]{1,0:T(8,128)(2,1)}) custom-call(bf16[1024,2048]{1,0:T(8,128)(2,1)} %bitcast.105, bf16[1024,3072]{1,0:T(8,128)(2,1)} %pad_maximum_fusion.refs_0_.refs_1_, f32[4,2048]{1,0:T(4,128)} %pad_maximum_fusion.7.refs_2_, ...), custom_call_target="tpu_custom_call" | custom-call | flops 12884901888 | bytes 16777216 | tf_op jit(solution)/shard_map/grad_scatter/pallas_call | solution.py:197
  987.2 5.2 convert_add_fusion
  992.3 4.3 convert_add_fusion.6
  (201 shorter events, 74.6 us)
Async XLA Ops:
  7.2 4.2 copy-start.39
  7.2 209.8 %all-gather.3.cloned.1.call-start = ((), (), s32[]{:S(2)}) async-start(), calls=%async_computation.4 | async-start | bytes 18874368 | tf_op jit(solution)/shard_map/all_gather | solution.py:1352
  12.7 98.2 %copy-start = (bf16[256,4096]{1,0:T(8,128)(2,1)}, bf16[256,4096]{1,0:T(8,128)(2,1)S(1)}, u32[]{:S(2)}) copy-start(bf16[256,4096]{1,0:T(8,128)(2,1)S(1)} %constant_dynamic-update-slice_fusion.refs_9_.refs_1_) | copy-start | bytes 6291460
  111.0 286.3 %all-gather.5.cloned.1.call-start = ((), (), s32[]{:S(2)}) async-start(), calls=%async_computation.5 | async-start | bytes 18874368 | tf_op jit(solution)/shard_map/all_gather | solution.py:1352
  111.0 31.3 %copy-start.54 = (f32[2048]{0:T(1024)S(1)}, f32[2048]{0:T(1024)}, u32[]{:S(2)}) copy-start(f32[2048]{0:T(1024)} %param.21) | copy-start | bytes 24580
  111.0 31.4 %copy-start.55 = (f32[2048]{0:T(1024)S(1)}, f32[2048]{0:T(1024)}, u32[]{:S(2)}) copy-start(f32[2048]{0:T(1024)} %param.22) | copy-start | bytes 24580
  132.2 14.3 %collective-permute-start = (f32[1024,2]{0,1:T(2,128)S(1)}, f32[1024,2]{0,1:T(2,128)S(1)}, u32[]{:S(2)}, u32[]{:S(2)}) collective-permute-start(f32[1024,2]{0,1:T(2,128)S(1)} %pad_maximum_fusion.8), channel_id=1, source_target_pairs={{0,1},{1,0},{2,3},{3,2},{4,5},{5,4},{6,7},{7,6},{8,9},{9,8},{10,11... | collective-permute-start | bytes 24584 | tf_op jit(solution)/shard_map/ppermute | solution.py:1341
  142.5 7.2 copy-start.7
  146.4 3.3 copy-start.1
  146.4 56.5 %copy-start.9 = (f32[1024]{0:T(1024)}, f32[1024]{0:T(1024)S(1)}, u32[]{:S(2)}) copy-start(f32[1024]{0:T(1024)S(1)} %pad_maximum_fusion.11) | copy-start | bytes 12292
  149.7 53.2 %copy-start.3 = (f32[1024,1]{1,0:T(8,128)}, f32[1024,1]{1,0:T(8,128)S(1)}, u32[]{:S(2)}) copy-start(f32[1024,1]{1,0:T(8,128)S(1)} %get-tuple-element.253.refs_4_.refs_8_) | copy-start | bytes 12292
  149.7 53.2 %copy-start.5 = (f32[1024,1]{1,0:T(8,128)}, f32[1024,1]{1,0:T(8,128)S(1)}, u32[]{:S(2)}) copy-start(f32[1024,1]{1,0:T(8,128)S(1)} %get-tuple-element.254.refs_3_.refs_7_) | copy-start | bytes 12292
  217.0 462.2 %reduce-scatter.5.cloned.1.call-start = ((), (), s32[]{:S(2)}) async-start(), calls=%async_computation.6 | async-start | bytes 10485760 | tf_op jit(solution)/shard_map/reduce_scatter | solution.py:1368
  221.0 74.8 %copy-start.46 = (f32[2048]{0:T(1024)S(1)}, f32[2048]{0:T(1024)}, u32[]{:S(2)}) copy-start(f32[2048]{0:T(1024)} %param.23) | copy-start | bytes 24580
  292.2 4.1 copy-start.27
  292.2 4.8 copy-start.31
  411.4 32.8 %copy-start.19 = (f32[256,2048]{1,0:T(8,128)S(1)}, f32[256,2048]{1,0:T(8,128)}, u32[]{:S(2)}) copy-start(f32[256,2048]{1,0:T(8,128)} %get-tuple-element.113) | copy-start | bytes 6291460
  411.4 34.4 %copy-start.16 = (f32[512,2048]{1,0:T(8,128)S(1)}, f32[512,2048]{1,0:T(8,128)}, u32[]{:S(2)}) copy-start(f32[512,2048]{1,0:T(8,128)} %convert_element_type.123) | copy-start | bytes 12582916
  478.7 29.2 %copy-start.22 = (f32[256,2048]{1,0:T(8,128)S(1)}, f32[256,2048]{1,0:T(8,128)}, u32[]{:S(2)}) copy-start(f32[256,2048]{1,0:T(8,128)} %get-tuple-element.118) | copy-start | bytes 6291460
  576.9 191.6 %reduce-scatter.7.cloned.1.call-start = ((), (), s32[]{:S(2)}) async-start(), calls=%async_computation.7 | async-start | bytes 10485760 | tf_op jit(solution)/shard_map/reduce_scatter | solution.py:1368
  578.4 3.9 copy-start.17
  669.4 152.9 %reduce-scatter.9.cloned.1.call-start = ((), (), s32[]{:S(2)}) async-start(), calls=%async_computation.8 | async-start | bytes 2621440 | tf_op jit(solution)/shard_map/reduce_scatter | solution.py:1368
  670.9 3.4 copy-start.37
  674.3 3.4 copy-start.18
  724.4 3.7 copy-start.56
  768.5 223.9 %reduce-scatter.11.cloned.1.call-start = ((), (), s32[]{:S(2)}) async-start(), calls=%async_computation.9 | async-start | bytes 10485760 | tf_op jit(solution)/shard_map/reduce_scatter | solution.py:1368
  829.3 6.8 collective-permute-start.1
  836.9 7.3 copy-start.38
  879.2 102.6 %copy-start.48 = (bf16[256,1024]{1,0:T(8,128)(2,1)S(1)}, bf16[256,1024]{1,0:T(8,128)(2,1)}, u32[]{:S(2)}) copy-start(bf16[256,1024]{1,0:T(8,128)(2,1)} %reduce-scatter.9.cloned.1.call-done.refs_4_) | copy-start | bytes 1572868
  982.8 3.7 copy-start.51
  987.2 5.2 copy-start.42
  987.2 5.2 copy-start.43
  (33 other events, 56.1 us)
Sparse Core Ops, SparseCore 0:
  111.1 97.5 all-gather.2
  217.1 124.8 all-gather.4
  577.0 84.9 reduce-scatter.4
  669.5 86.0 reduce-scatter.6
  768.6 33.2 reduce-scatter.8
  822.4 92.7 reduce-scatter.10

commit v6 on v5

--- a/solution.py
+++ b/solution.py
@@ -114,7 +114,7 @@
         back = grad * cos_ref[here] - pltpu.roll(grad, half, 1) * sin_ref[here]
         hat = values_ref[here] * inv_ref[here]
         gained = back * gain_ref[...]
-        out_ref[here] = gained
+        out_ref[here] = gained.astype(LOW)
         inner_ref[here] += jnp.sum(gained * hat, axis=1, keepdims=True)
         return jnp.sum(back * hat, axis=0, keepdims=True)
 
@@ -1281,7 +1281,6 @@
     width = value.shape[1]
     heads = width // HEAD_DIM
     head, later, whole, column, gain, lse, hbm = attention_specs(heads)
-    full = jax.ShapeDtypeStruct((SEQ_LEN, width), F32)
     low = jax.ShapeDtypeStruct((SEQ_LEN, width), LOW)
     gain_out = jax.ShapeDtypeStruct((1, width), F32)
     inner = jax.ShapeDtypeStruct((SEQ_LEN, 1), F32)
@@ -1295,7 +1294,7 @@
         earlier,
         grid=(heads,),
         out_specs=[head, head, head, gain, gain, column, column, *[hbm] * len(sides.out_shapes)],
-        out_shape=[full, full, low, gain_out, gain_out, inner, inner, *sides.out_shapes],
+        out_shape=[low, low, low, gain_out, gain_out, inner, inner, *sides.out_shapes],
         scratch_shapes=[
             pltpu.VMEM((SEQ_LEN, HEAD_DIM), LOW),
             pltpu.VMEM((SEQ_LEN, HEAD_DIM), LOW),
@@ -1594,7 +1593,8 @@
     grad_qkv = jnp.concatenate(
         [grad_query.astype(LOW), grad_key.astype(LOW), grad_value], axis=1
     )
-    sides = Sides(Spans(parts, spans, [(gate_up_grad[s], 2, part_cols, s) for s in others_spans]))
+    quarter = cols // 4
+    sides = Sides(Spans(parts, spans, [(gate_up_grad[s], 4, quarter, s) for s in others_spans]))
     total, low, up_came_first = product_sum(
         parts,
         [(grad_qkv, 0, full_qkv, 0, full_qkv.shape[1])],
@@ -1608,14 +1608,21 @@
         SumAll(fsdp, tensor, jnp.stack([*gain_parts, attn_gain_part, ffn_gain_part])),
         Rows(parts, deliver=low),
         Spans(parts, spans, [(out_terms, s, head_cols, s) for s in others_spans]),
-        Spans(parts, spans, [(gate_up_grad[s], 3, part_cols, s) for s in others_spans]),
+        Spans(
+            parts,
+            spans,
+            [(gate_up_grad[s], run, quarter, s) for run in range(5, 8) for s in others_spans],
+        ),
     )
     qkv_grad, gain_grads, came, out_came, up_came_last = grad_scatter(
         31, fsdp, parts, spans, inputs, grad_qkv, 3, [], sides
     )
     input_grad = add_pieces(total, came)
     out_grad = add_pieces(out_terms[:, :head_cols].astype(F32), out_came)
-    up_came = [jnp.concatenate(pair, axis=1) for pair in zip(up_came_first, up_came_last)]
+    up_came = [
+        jnp.concatenate([first, *up_came_last[s :: spans - 1]], axis=1)
+        for s, first in enumerate(up_came_first)
+    ]
     gate_grad = add_pieces(gate_up_grad[0][:, :cols].astype(F32), gate_came)
     up_grad = add_pieces(gate_up_grad[0][:, cols:].astype(F32), up_came)
     query_grad, key_grad, value_grad = jnp.split(qkv_grad, 3, axis=1)

time: 1010 us -> 1010 us (level)
    unnamed x119 -> x123, local copies, waits for them, and re-layouts: 33.5 us -> 33.5 us
where the time goes in v6:
time: 1010 us; the launch traced here: 1000 us
  Pallas kernels  857 us (85%)
  other arithmetic  64.4 us (6%)
  local copies, waits for them, and re-layouts  45.7 us (5%)
  between operations  15.5 us (2%)
  starting transfers between devices  11.2 us (1%)
    pallas_call x20, Pallas kernels, call(): return pl.pallas_call(body, in_specs=specs, **options)(*operands, *earlier)  837 us
    unnamed x123, local copies, waits for them, and re-layouts  33.5 us
  transfers between devices with their start and end apart: 8, of which 0 were waited for; matrix products, arithmetic and copies ran while one was open for 8% of the time, Pallas kernels for 59%

profile of v6, /device:TPU:0, one launch (start us, length us, event | category | flops | bytes accessed | tf_op | source)
XLA Modules:
  0.0 1002.2 jit_solution(11552973330496375668)
XLA Ops:
  12.7 98.2 %exchange.3 = (bf16[8,256,3072]{2,1,0:T(8,128)(2,1)}, bf16[8,256,1024]{2,1,0:T(8,128)(2,1)}, bf16[1,256,2048]{2,1,0:T(8,128)(2,1)}, bf16[2,512,2048]{2,1,0:T(8,128)(2,1)}) custom-call(bf16[512,2048]{1,0:T(8,128)(2,1)} %refs_0_.1, bf16[256,512]{1,0:T(8,128)(2,1)} %refs_5_.1, bf16[256,512]{1,0:T(8,128)(2,1)} %refs_6_.1, bf16[256,512]{1,0:T(8,128)(2,1)} %refs_7_.1, ...), custom_call_target="tpu_custom_call" | custom-call | tf_op jit(solution)/shard_map/exchange/pallas_call | solution.py:197
  111.1 19.4 %project.1 = (f32[1024,2048]{1,0:T(8,128)}, bf16[1024,1024]{1,0:T(8,128)(2,1)S(1)}, f32[1024,1]{1,0:T(8,128)S(1)}, f32[1024,1]{1,0:T(8,128)S(1)}) custom-call(bf16[1024,2048]{1,0:T(8,128)(2,1)} %bitcast.104, bf16[2048,3072]{1,0:T(8,128)(2,1)} %bitcast.102), custom_call_target="tpu_custom_call" | custom-call | flops 12884901888 | bytes 27262976 | tf_op jit(solution)/shard_map/project/pallas_call | solution.py:1200
  132.2 10.1 %collective-permute-start = (f32[1024,2]{0,1:T(2,128)S(1)}, f32[1024,2]{0,1:T(2,128)S(1)}, u32[]{:S(2)}, u32[]{:S(2)}) collective-permute-start(f32[1024,2]{0,1:T(2,128)S(1)} %pad_maximum_fusion.8), channel_id=1, source_target_pairs={{0,1},{1,0},{2,3},{3,2},{4,5},{5,4},{6,7},{7,6},{8,9},{9,8},{10,11... | collective-permute-start | bytes 24584 | tf_op jit(solution)/shard_map/ppermute | solution.py:1340
  151.7 51.2 %attend.1 = (bf16[1024,1024]{1,0:T(8,128)(2,1)S(1)}, bf16[1024,1024]{1,0:T(8,128)(2,1)S(1)}, bf16[1024,1024]{1,0:T(8,128)(2,1)S(1)}, f32[8,1024,1]{2,1,0:T(8,128)}, bf16[256,2048]{1,0:T(8,128)(2,1)S(1)}) custom-call(f32[1024,2048]{1,0:T(8,128)} %get-tuple-element.95.refs_0_.refs_1_.refs_5_.refs_6_, ...), custom_call_target="tpu_custom_call" | custom-call | flops 8589934592 | bytes 16777216 | tf_op jit(solution)/shard_map/attend/pallas_call | solution.py:197
  208.0 8.9 product_sum.6
  221.0 71.1 %exchange.4 = (bf16[8,256,2048]{2,1,0:T(8,128)(2,1)}, bf16[1,512,2048]{2,1,0:T(8,128)(2,1)}, bf16[256,2048]{1,0:T(8,128)(2,1)}) custom-call(bf16[1024,2048]{1,0:T(8,128)(2,1)} %get-tuple-element.105.refs_0_, bf16[256,4096]{1,0:T(8,128)(2,1)} %copy-done, bf16[256,2048]{1,0:T(8,128)(2,1)} %copy-done.2), custom_call_target="tpu_custom_call" | custom-call | tf_op jit(solution)/shard_map/exchange/pallas_call | solution.py:197
  292.2 3.6 multiply_reduce_fusion
  296.9 5.0 multiply_add_fusion
  304.6 64.7 %exchange.5 = (bf16[8,256,2048]{2,1,0:T(8,128)(2,1)}, bf16[2,256,2048]{2,1,0:T(8,128)(2,1)}, bf16[2,256,2048]{2,1,0:T(8,128)(2,1)}) custom-call(bf16[256,2048]{1,0:T(8,128)(2,1)} %get-tuple-element.246.refs_0_, bf16[256,2048]{1,0:T(8,128)(2,1)} %get-tuple-element.245.refs_1_, bf16[256,2048]{1,0:T(8,128)(2,1)} %get-tuple-element.108.refs_2_), custom_call_target="tpu_custom_call" | custom-call | tf_op jit(solution)/shard_map/exchange/pallas_call | solution.py:197
  369.3 28.0 %feed_up.2 = (f32[512,4096]{1,0:T(8,128)}, f32[512,4096]{1,0:T(8,128)}, bf16[512,4096]{1,0:T(8,128)(2,1)}) custom-call(bf16[512,2048]{1,0:T(8,128)(2,1)} %bitcast.108, bf16[2048,4096]{1,0:T(8,128)(2,1)} %all-gather.3.cloned.1.call-done.refs_1_.refs_2_.refs_3_, bf16[2048,4096]{1,0:T(8,128)(2,1)} %all-gather.3.cloned.1.call-done.refs_1_.refs_2_.refs_3_, ...), custom_call_target="tpu_custom_call" | custom-call | flops 17179869184 | bytes 54525952 | tf_op jit(solution)/shard_map/feed_up/pallas_call | solution.py:197
  397.3 14.1 %product_sum.7 = (f32[256,2048]{1,0:T(8,128)}, bf16[512,2048]{1,0:T(8,128)(2,1)}) custom-call(bf16[512,4096]{1,0:T(8,128)(2,1)} %get-tuple-element.113.refs_0_.refs_2_, bf16[2048,4096]{1,0:T(8,128)(2,1)} %all-gather.5.cloned.1.call-done.refs_1_.refs_3_, bf16[512,4096]{1,0:T(8,128)(2,1)} %get-tuple-element.113.refs_0_.refs_2_, ...), custom_call_target="tpu_custom_call" | custom-call | flops 8589934592 | bytes 20971520 | tf_op jit(solution)/shard_map/product_sum/pallas_call | solution.py:197
  411.3 32.8 %feed_up.3 = (f32[512,4096]{1,0:T(8,128)}, f32[512,4096]{1,0:T(8,128)}, bf16[512,4096]{1,0:T(8,128)(2,1)}, bf16[1,256,2048]{2,1,0:T(8,128)(2,1)}) custom-call(bf16[512,2048]{1,0:T(8,128)(2,1)} %bitcast.111, bf16[2048,4096]{1,0:T(8,128)(2,1)} %all-gather.3.cloned.1.call-done.refs_1_.refs_2_.refs_3_, ...), custom_call_target="tpu_custom_call" | custom-call | flops 17179869184 | bytes 54525952 | tf_op jit(solution)/shard_map/feed_up/pallas_call | solution.py:197
  448.8 30.0 %product_sum.8 = (f32[256,2048]{1,0:T(8,128)}, bf16[512,2048]{1,0:T(8,128)(2,1)}, bf16[2,256,2048]{2,1,0:T(8,128)(2,1)}) custom-call(bf16[512,4096]{1,0:T(8,128)(2,1)} %get-tuple-element.119.refs_0_.refs_2_.refs_3_, bf16[2048,4096]{1,0:T(8,128)(2,1)} %all-gather.5.cloned.1.call-done.refs_1_.refs_3_, ...), custom_call_target="tpu_custom_call" | custom-call | flops 8589934592 | bytes 20971520 | tf_op jit(solution)/shard_map/product_sum/pallas_call | solution.py:197
  478.8 29.2 %feed_up_back.2 = (bf16[512,4096]{1,0:T(8,128)(2,1)}, bf16[512,4096]{1,0:T(8,128)(2,1)}, bf16[1,256,2048]{2,1,0:T(8,128)(2,1)S(1)}) custom-call(bf16[512,2048]{1,0:T(8,128)(2,1)} %bitcast.91, bf16[2048,4096]{1,0:T(8,128)(2,1)} %all-gather.5.cloned.1.call-done.refs_1_.refs_3_, f32[512,4096]{1,0:T(8,128)} %get-tuple-element.122.refs_2_, ...), custom_call_target="tpu_custom_call" | custom-call | flops 8589934592 | bytes 41943040 | tf_op jit(solution)/shard_map/feed_up_back/pallas_call | solution.py:197
  513.5 32.0 %product_sum.9 = (f32[256,2048]{1,0:T(8,128)}, bf16[512,2048]{1,0:T(8,128)(2,1)}, bf16[2,256,2048]{2,1,0:T(8,128)(2,1)}) custom-call(bf16[512,4096]{1,0:T(8,128)(2,1)} %get-tuple-element.128.refs_0_.refs_4_.refs_2_, bf16[2048,4096]{1,0:T(8,128)(2,1)} %all-gather.3.cloned.1.call-done.refs_1_.refs_2_.refs_3_, ...), custom_call_target="tpu_custom_call" | custom-call | flops 17179869184 | bytes 37748736 | tf_op jit(solution)/shard_map/product_sum/pallas_call | solution.py:197
  545.5 31.5 %weight_grad.4 = (bf16[1024,4096]{1,0:T(8,128)(2,1)}, bf16[1,256,2048]{2,1,0:T(8,128)(2,1)}) custom-call(bf16[512,2048]{1,0:T(8,128)(2,1)} %bitcast.92, bf16[512,2048]{1,0:T(8,128)(2,1)} %bitcast.93, bf16[512,4096]{1,0:T(8,128)(2,1)} %get-tuple-element.113.refs_0_.refs_2_, bf16[512,4096]{1,0:T(8,128)(2,1)} %get-tuple-element.119.refs_0_.refs_2_.refs_3_, ...), custom_call_target="tpu_custom_call" | custom-call | flops 17179869184 | bytes 29360128 | tf_op jit(solution)/shard_map/weight_grad/pallas_call | solution.py:197
  578.6 3.4 multiply_reduce_fusion.4
  584.0 21.0 %feed_up_back.3 = (bf16[512,4096]{1,0:T(8,128)(2,1)}, bf16[512,4096]{1,0:T(8,128)(2,1)}) custom-call(bf16[512,2048]{1,0:T(8,128)(2,1)} %bitcast.94, bf16[2048,4096]{1,0:T(8,128)(2,1)} %all-gather.5.cloned.1.call-done.refs_1_.refs_3_, f32[512,4096]{1,0:T(8,128)} %get-tuple-element.131.refs_2_, f32[512,4096]{1,0:T(8,128)} %get-tuple-element.132.refs_3_, ...), custom_call_target="tpu_custom_call" | custom-call | flops 8589934592 | bytes 41943040 | tf_op jit(solution)/shard_map/feed_up_back/pallas_call | solution.py:197
  605.0 33.3 %product_sum.10 = (f32[256,2048]{1,0:T(8,128)}, bf16[512,2048]{1,0:T(8,128)(2,1)}, bf16[2,256,2048]{2,1,0:T(8,128)(2,1)}) custom-call(bf16[512,4096]{1,0:T(8,128)(2,1)} %get-tuple-element.135.refs_0_.refs_4_.refs_3_, bf16[2048,4096]{1,0:T(8,128)(2,1)} %all-gather.3.cloned.1.call-done.refs_1_.refs_2_.refs_3_, ...), custom_call_target="tpu_custom_call" | custom-call | flops 17179869184 | bytes 37748736 | tf_op jit(solution)/shard_map/product_sum/pallas_call | solution.py:197
  638.3 31.2 %weight_grad.5 = (bf16[1024,4096]{1,0:T(8,128)(2,1)}, bf16[1,256,2048]{2,1,0:T(8,128)(2,1)}) custom-call(bf16[512,2048]{1,0:T(8,128)(2,1)} %bitcast.109, bf16[512,2048]{1,0:T(8,128)(2,1)} %bitcast.112, bf16[512,4096]{1,0:T(8,128)(2,1)} %get-tuple-element.128.refs_0_.refs_4_.refs_2_, bf16[512,4096]{1,0:T(8,128)(2,1)} %get-tuple-element.135.refs_0_.refs_4_.refs_3_, ...), custom_call_target="tpu_custom_call" | custom-call | flops 17179869184 | bytes 29360128 | tf_op jit(solution)/shard_map/weight_grad/pallas_call | solution.py:197
  671.1 3.4 multiply_reduce_fusion.3
  679.3 43.4 %weight_grad.6 = (bf16[1024,4096]{1,0:T(8,128)(2,1)}, bf16[2,256,2048]{2,1,0:T(8,128)(2,1)}, bf16[256,1024]{1,0:T(8,128)(2,1)}) custom-call(bf16[512,2048]{1,0:T(8,128)(2,1)} %bitcast.110, bf16[512,2048]{1,0:T(8,128)(2,1)} %bitcast.113, bf16[512,4096]{1,0:T(8,128)(2,1)} %get-tuple-element.128.refs_0_.refs_4_.refs_2_, ...), custom_call_target="tpu_custom_call" | custom-call | flops 17179869184 | bytes 29360128 | tf_op jit(solution)/shard_map/weight_grad/pallas_call | solution.py:197
  728.3 8.7 convolution_convert_fusion.refs_3_
  737.0 31.7 %weight_grad.7 = (bf16[1024,1024]{1,0:T(8,128)(2,1)}, bf16[256,1024]{1,0:T(8,128)(2,1)}) custom-call(bf16[1024,2048]{1,0:T(8,128)(2,1)} %pad_maximum_fusion.1.refs_0_, bf16[1024,1024]{1,0:T(8,128)(2,1)} %copy-done.11, bf16[256,4096]{1,0:T(8,128)(2,1)} %reduce-scatter.5.cloned.1.call-done.refs_7_.refs_2_, bf16[1024,1024]{1,0:T(8,128)(2,1)} %convolution_convert_fusion.refs_3_), custom_call_target="tpu_custom_call" | custom-call | flops 4294967296 | bytes 10485760 | tf_op jit(solution)/shard_map/weight_grad/pallas_call | solution.py:197
  771.5 50.6 %attend_back.1 = (bf16[1024,1024]{1,0:T(8,128)(2,1)}, bf16[1024,1024]{1,0:T(8,128)(2,1)}, bf16[1024,1024]{1,0:T(8,128)(2,1)}, f32[1,1024]{1,0:T(1,128)S(1)}, f32...) custom-call(bf16[1024,1024]{1,0:T(8,128)(2,1)} %copy-done.14, ...), custom_call_target="tpu_custom_call" | custom-call | flops 21474836480 | bytes 33554432 | tf_op jit(solution)/shard_map/attend_back/pallas_call | solution.py:197
  832.9 3.1 copy.57
  836.8 5.9 multiply_convert_fusion.1
  842.7 3.0 pad_maximum_fusion.refs_0_.refs_1_
  845.7 22.8 %product_sum.11 = (f32[512,2048]{1,0:T(8,128)}, bf16[1024,2048]{1,0:T(8,128)(2,1)}, bf16[256,512]{1,0:T(8,128)(2,1)}) custom-call(bf16[1024,3072]{1,0:T(8,128)(2,1)} %pad_maximum_fusion.refs_0_.refs_1_, bf16[2048,3072]{1,0:T(8,128)(2,1)} %bitcast.103, f32[512,2048]{1,0:T(8,128)} %pad_maximum_fusion.2.refs_2_, ...), custom_call_target="tpu_custom_call" | custom-call | flops 12884901888 | bytes 20971520 | tf_op jit(solution)/shard_map/product_sum/pallas_call | solution.py:197
  868.5 111.5 %grad_scatter.1 = (f32[256,1536]{1,0:T(8,128)}, f32[4,2048]{1,0:T(4,128)}, bf16[1,512,2048]{2,1,0:T(8,128)(2,1)}, bf16[256,512]{1,0:T(8,128)(2,1)}, bf16[256,512...) custom-call(bf16[1024,2048]{1,0:T(8,128)(2,1)} %bitcast.105, ...), custom_call_target="tpu_custom_call" | custom-call | flops 12884901888 | bytes 16777216 | tf_op jit(solution)/shard_map/grad_scatter/pallas_call | solution.py:197
  985.4 5.2 convert_add_fusion
  990.6 4.3 convert_add_fusion.6
  (205 shorter events, 74.6 us)
Async XLA Ops:
  7.2 4.2 copy-start.39
  7.2 209.7 %all-gather.3.cloned.1.call-start = ((), (), s32[]{:S(2)}) async-start(), calls=%async_computation.4 | async-start | bytes 18874368 | tf_op jit(solution)/shard_map/all_gather | solution.py:1351
  12.7 98.2 %copy-start = (bf16[256,4096]{1,0:T(8,128)(2,1)}, bf16[256,4096]{1,0:T(8,128)(2,1)S(1)}, u32[]{:S(2)}) copy-start(bf16[256,4096]{1,0:T(8,128)(2,1)S(1)} %constant_dynamic-update-slice_fusion.refs_9_.refs_1_) | copy-start | bytes 6291460
  111.0 286.3 %all-gather.5.cloned.1.call-start = ((), (), s32[]{:S(2)}) async-start(), calls=%async_computation.5 | async-start | bytes 18874368 | tf_op jit(solution)/shard_map/all_gather | solution.py:1351
  111.0 31.3 %copy-start.56 = (f32[2048]{0:T(1024)S(1)}, f32[2048]{0:T(1024)}, u32[]{:S(2)}) copy-start(f32[2048]{0:T(1024)} %param.21) | copy-start | bytes 24580
  111.0 31.4 %copy-start.57 = (f32[2048]{0:T(1024)S(1)}, f32[2048]{0:T(1024)}, u32[]{:S(2)}) copy-start(f32[2048]{0:T(1024)} %param.22) | copy-start | bytes 24580
  132.2 14.3 %collective-permute-start = (f32[1024,2]{0,1:T(2,128)S(1)}, f32[1024,2]{0,1:T(2,128)S(1)}, u32[]{:S(2)}, u32[]{:S(2)}) collective-permute-start(f32[1024,2]{0,1:T(2,128)S(1)} %pad_maximum_fusion.8), channel_id=1, source_target_pairs={{0,1},{1,0},{2,3},{3,2},{4,5},{5,4},{6,7},{7,6},{8,9},{9,8},{10,11... | collective-permute-start | bytes 24584 | tf_op jit(solution)/shard_map/ppermute | solution.py:1340
  142.5 7.2 copy-start.7
  146.4 56.5 %copy-start.9 = (f32[1024]{0:T(1024)}, f32[1024]{0:T(1024)S(1)}, u32[]{:S(2)}) copy-start(f32[1024]{0:T(1024)S(1)} %pad_maximum_fusion.11) | copy-start | bytes 12292
  149.7 53.2 %copy-start.3 = (f32[1024,1]{1,0:T(8,128)}, f32[1024,1]{1,0:T(8,128)S(1)}, u32[]{:S(2)}) copy-start(f32[1024,1]{1,0:T(8,128)S(1)} %get-tuple-element.257.refs_4_.refs_8_) | copy-start | bytes 12292
  149.7 53.2 %copy-start.5 = (f32[1024,1]{1,0:T(8,128)}, f32[1024,1]{1,0:T(8,128)S(1)}, u32[]{:S(2)}) copy-start(f32[1024,1]{1,0:T(8,128)S(1)} %get-tuple-element.258.refs_3_.refs_7_) | copy-start | bytes 12292
  217.0 462.4 %reduce-scatter.5.cloned.1.call-start = ((), (), s32[]{:S(2)}) async-start(), calls=%async_computation.6 | async-start | bytes 10485760 | tf_op jit(solution)/shard_map/reduce_scatter | solution.py:1367
  221.0 74.8 %copy-start.48 = (f32[2048]{0:T(1024)S(1)}, f32[2048]{0:T(1024)}, u32[]{:S(2)}) copy-start(f32[2048]{0:T(1024)} %param.23) | copy-start | bytes 24580
  292.1 4.1 copy-start.27
  292.2 4.8 copy-start.31
  411.3 32.8 %copy-start.19 = (f32[256,2048]{1,0:T(8,128)S(1)}, f32[256,2048]{1,0:T(8,128)}, u32[]{:S(2)}) copy-start(f32[256,2048]{1,0:T(8,128)} %get-tuple-element.115) | copy-start | bytes 6291460
  411.3 34.5 %copy-start.16 = (f32[512,2048]{1,0:T(8,128)S(1)}, f32[512,2048]{1,0:T(8,128)}, u32[]{:S(2)}) copy-start(f32[512,2048]{1,0:T(8,128)} %convert_element_type.129) | copy-start | bytes 12582916
  478.8 29.2 %copy-start.22 = (f32[256,2048]{1,0:T(8,128)S(1)}, f32[256,2048]{1,0:T(8,128)}, u32[]{:S(2)}) copy-start(f32[256,2048]{1,0:T(8,128)} %get-tuple-element.120) | copy-start | bytes 6291460
  577.0 191.7 %reduce-scatter.7.cloned.1.call-start = ((), (), s32[]{:S(2)}) async-start(), calls=%async_computation.7 | async-start | bytes 10485760 | tf_op jit(solution)/shard_map/reduce_scatter | solution.py:1367
  578.6 4.0 copy-start.17
  669.5 152.5 %reduce-scatter.9.cloned.1.call-start = ((), (), s32[]{:S(2)}) async-start(), calls=%async_computation.8 | async-start | bytes 2621440 | tf_op jit(solution)/shard_map/reduce_scatter | solution.py:1367
  671.1 3.4 copy-start.37
  724.5 3.7 copy-start.58
  768.7 221.8 %reduce-scatter.11.cloned.1.call-start = ((), (), s32[]{:S(2)}) async-start(), calls=%async_computation.9 | async-start | bytes 10485760 | tf_op jit(solution)/shard_map/reduce_scatter | solution.py:1367
  829.1 6.8 collective-permute-start.1
  836.8 5.9 copy-start.38
  868.5 111.5 %copy-start.50 = (bf16[256,1024]{1,0:T(8,128)(2,1)S(1)}, bf16[256,1024]{1,0:T(8,128)(2,1)}, u32[]{:S(2)}) copy-start(bf16[256,1024]{1,0:T(8,128)(2,1)} %reduce-scatter.9.cloned.1.call-done.refs_4_) | copy-start | bytes 1572868
  981.0 3.7 copy-start.53
  985.3 5.2 copy-start.44
  985.3 5.2 copy-start.45
  985.3 5.2 copy-start.46
  985.4 5.2 copy-start.47
  (35 other events, 62.8 us)
Sparse Core Ops, SparseCore 0:
  111.1 97.5 all-gather.2
  217.1 124.8 all-gather.4
  577.1 84.8 reduce-scatter.4
  669.7 85.9 reduce-scatter.6
  768.9 33.2 reduce-scatter.8
  822.2 103.0 reduce-scatter.10
